TPU v7x, 32 devices: a whole 2x2x4 slice. The times are simulated.
32 devices in a mesh: lon: 8 (over y, x, core), lat: 4 (over z).
Axes of the slice: x: 2, y: 2, z: 4, core: 2. Of those that a mesh axis runs over, the one named last changes fastest.
Arguments:
- members: bfloat16 [3, 128, 1440, 128], P(None, 'lat', 'lon'), may hold values from -6 to 6
- background: bfloat16 [3, 128, 1440], P(None, 'lat', 'lon'), may hold values from -6 to 6
Outputs:
- modes: float32 [3, 128, 1440, 128], P(None, 'lat', 'lon')
- r_factor: float32 [128, 128], replicated
All inputs are finite; a program needn't handle non-finite values.
Results may differ from a plain program's by a relative error of at most 0.0076.
The roundings to bfloat16 on the way count: a program that leaves them out, or rounds other values in their place, can miss the bound.
Values may be sent and summed in bfloat16 or wider, within the bound.
No kernel may reach another device: no remote copies, remote signals or barrier semaphores. Data moves between devices by JAX's collectives and lax.ppermute only.
A program may use at most 64 MiB of HBM per device.

v0:
```python
import math

import jax
import jax.numpy as jnp
from jax import lax
from jax.sharding import PartitionSpec as P


def extended(shard, sides, width, wrap):
    for axis, dim in sides:
        peers, length = (lax.axis_size(axis), shard.shape[dim])
        up = [(i, (i + 1) % peers) for i in range(peers if wrap else peers - 1)]
        down = [(j, i) for i, j in up]
        last = lax.slice_in_dim(shard, length - width, length, axis=dim)
        leading = lax.slice_in_dim(shard, 0, width, axis=dim)
        before = lax.ppermute(last, axis, up)
        after = lax.ppermute(leading, axis, down)
        shard = jnp.concatenate([before, shard, after], axis=dim)
    return shard


def row_coefs(glob, nlat):
    phi = (0.125 * (glob.astype(jnp.float32) + 0.5) - 0.0625 * nlat) * (math.pi / 180.0)
    kx = 0.05 + 0.2 * (1.0 - jnp.cos(phi))
    weight = jnp.sqrt(jnp.cos(phi))
    return (kx, weight)


def smooth_pass(padded, kx):
    centre = padded[:, 1:-1, 1:-1]
    east_west = padded[:, 1:-1, 2:] + padded[:, 1:-1, :-2] - 2.0 * centre
    north_south = padded[:, 2:, 1:-1] + padded[:, :-2, 1:-1] - 2.0 * centre
    return centre + kx[None, :, None, None] * east_west + 0.2 * north_south


def chol_upper(gram):
    order = gram.shape[0]
    index = jnp.arange(order)

    def column(j, lower):
        row_j = lax.dynamic_slice_in_dim(lower, j, 1, 0)[0]
        col_g = lax.dynamic_slice_in_dim(gram, j, 1, 1)[:, 0]
        resid = col_g - jnp.dot(lower, row_j, precision=lax.Precision.HIGHEST)
        pivot = jnp.sqrt(jnp.sum(jnp.where(index == j, resid, 0.0)))
        col_new = jnp.where(index >= j, resid / pivot, 0.0)
        return lower + col_new[:, None] * (index[None, :] == j).astype(jnp.float32)

    lower = lax.fori_loop(0, order, column, jnp.zeros((order, order), jnp.float32))
    return lower.T


def upper_inverse(upper):
    order = upper.shape[0]
    index = jnp.arange(order)
    ident = jnp.eye(order, dtype=jnp.float32)

    def row_step(step, solved):
        i = order - 1 - step
        row_u = lax.dynamic_slice_in_dim(upper, i, 1, 0)[0]
        diag = jnp.sum(jnp.where(index == i, row_u, 0.0))
        above = jnp.where(index > i, row_u, 0.0)
        unit = lax.dynamic_slice_in_dim(ident, i, 1, 0)[0]
        new_row = (unit - jnp.dot(above, solved, precision=lax.Precision.HIGHEST)) / diag
        return solved + (index == i).astype(jnp.float32)[:, None] * new_row[None, :]

    return lax.fori_loop(0, order, row_step, jnp.zeros((order, order), jnp.float32))


def local(members, background):
    fields, rows, cols, width = members.shape
    nlat = rows * lax.axis_size("lat")
    first = lax.axis_index("lat") * rows
    kx_rows, unused_weight = row_coefs(first + jnp.arange(rows), nlat)
    padded = extended(members, (("lat", 1),), 1, False)
    padded = extended(padded, (("lon", 2),), 1, True)
    inner = smooth_pass(padded.astype(jnp.float32), kx_rows)
    padded = extended(inner, (("lat", 1),), 1, False)
    padded = extended(padded, (("lon", 2),), 1, True)
    final = smooth_pass(padded, kx_rows)
    unused_kx, weight = row_coefs(first + jnp.arange(rows), nlat)
    anomaly = (
        (final - background.astype(jnp.float32)[:, :, :, None]) * weight[None, :, None, None]
    ).astype(jnp.bfloat16)
    matrix = anomaly.reshape(-1, width)
    partial_gram = lax.dot_general(
        matrix, matrix, (((0,), (0,)), ((), ())), preferred_element_type=jnp.float32
    )
    gram = lax.psum(partial_gram, "lat")
    gram = lax.psum(gram, "lon")
    total_rows = fields * nlat * cols * lax.axis_size("lon")
    gram = gram / total_rows
    r_factor = chol_upper(gram)
    inverse = upper_inverse(r_factor)
    modes = jnp.dot(
        matrix, inverse, precision=lax.Precision.HIGHEST, preferred_element_type=jnp.float32
    )
    return (modes.reshape(fields, rows, cols, width), r_factor)


def solution(mesh):
    return jax.shard_map(
        local,
        mesh=mesh,
        in_specs=(P(None, "lat", "lon", None), P(None, "lat", "lon")),
        out_specs=(P(None, "lat", "lon", None), P()),
        check_vma=False,
    )
```

profile of v0, /device:TPU:0, one launch (start us, length us, event | category | flops | bytes accessed | tf_op | source)
XLA Modules:
  0.0 595.3 jit_solution(14647362568405315845)
XLA Ops:
  7.2 2.0 fusion.45
  9.3 4.9 collective-permute-start
  14.2 1.3 collective-permute-start.1
  15.5 1.6 collective-permute-done
  17.2 4.3 constant_dynamic-update-slice_fusion.1
  21.6 2.6 collective-permute-start.3
  24.3 1.8 collective-permute-done.2
  26.1 2.0 maximum_convert_fusion
  28.0 5.8 fusion.34
  33.9 4.4 collective-permute-start.4
  38.4 1.3 collective-permute-start.5
  39.7 5.5 collective-permute-done.4
  45.2 4.1 collective-permute-done.5
  49.4 1.6 collective-permute-start.6
  51.1 1.7 collective-permute-done.6
  52.8 2.7 collective-permute-done.7
  55.5 14.0 %fusion.27 = bf16[3,32,180,128]{3,2,1,0:T(8,128)(2,1)S(1)} fusion(f32[3,32,180,128]{3,2,1,0:T(8,128)S(1)} %fusion.34, f32[3,1,180,128]{3,2,1,0:T(8,128)S(1)} %collective-permute-done.4, f32[3,1,180,128]{3,2,1,0:T(8,128)S(1)} %collective-permute-done.5, f32[3,34,1,128]{3,2,1,0:T(1,128)S(1)} %collective-permute-done.7, ...), kind=kLoop, calls=%fused_computation.37 | loop fusion | flops 44236800 | bytes 13997824 | tf_op jit(solution)/shard_map/convert_element_type | solution.py:83
  69.5 2.1 copy-done
  71.6 2.0 convolution_bitcast_fusion.2
  73.9 32.2 %all-reduce.3.cloned.1.call-done = f32[128,128]{1,0:T(8,128)} async-done(((f32[128,128]{1,0:T(8,128)}), f32[128,128]{1,0:T(8,128)}) %all-reduce.3.cloned.1.call-update) | async-done | bytes 65552 | tf_op jit(solution)/shard_map/psum | solution.py:88
  106.2 55.5 %all-reduce.5.cloned.1.call-done = f32[128,128]{1,0:T(8,128)} async-done(((f32[128,128]{1,0:T(8,128)}), f32[128,128]{1,0:T(8,128)}) %all-reduce.5.cloned.1.call-update) | async-done | bytes 65552 | tf_op jit(solution)/shard_map/psum | solution.py:89
  162.6 220.1 %while.32 = (s32[]{:T(128)}, f32[128,128]{1,0:T(8,128)S(1)}, f32[128,128]{0,1:T(8,128)S(1)}, s32[]{:T(128)}, s32[]{:T(128)}) while((s32[]{:T(128)}, f32[128,128]{1,0:T(8,128)S(1)}, f32[128,128]{0,1:T(8,128)S(1)}, s32[]{:T(128)}, s32[]{:T(128)}) %tuple.88), condition=%wide.region_4.5_spmd.clone.clone, body=%wide.region_2.4_spmd.clone.clone.sunk | while | flops 263298 | bytes 333408 | solution.py:48
  162.6 0.9 fusion.56
  164.3 0.9 fusion.56
  166.0 0.9 fusion.56
  167.8 0.9 fusion.56
  169.5 0.9 fusion.56
  171.2 0.9 fusion.56
  172.9 0.9 fusion.56
  174.6 0.9 fusion.56
  176.4 0.9 fusion.56
  178.1 0.9 fusion.56
  179.8 0.9 fusion.56
  181.5 0.9 fusion.56
  183.2 0.9 fusion.56
  184.9 0.9 fusion.56
  186.7 0.9 fusion.56
  188.4 0.9 fusion.56
  190.1 0.9 fusion.56
  191.8 0.9 fusion.56
  202.1 0.9 fusion.56
  234.8 0.9 fusion.56
  267.5 0.9 fusion.56
  300.2 0.9 fusion.56
  332.8 0.9 fusion.56
  365.5 0.9 fusion.56
  382.8 197.9 %while.33 = (s32[]{:T(128)}, f32[128,128]{1,0:T(8,128)S(1)}, f32[128,128]{1,0:T(8,128)S(1)}, f32[128,128]{1,0:T(8,128)S(1)}, s32[]{:T(128)}, /*index=5*/s32[]{:T(128)}, s32[]{:T(128)}, s32[]{:T(128)}) while((s32[]{:T(128)}, f32[128,128]{1,0:T(8,128)S(1)}, f32[128,128]{1,0:T(8,128)S(1)}, f32[128,128]{1,0:T(8,128)S(1)}, ...), condition=%wide.region_7.8_spmd.clone.clone, body=%wide.region_5.7_spmd.clone.clone.sunk | while | flops 263302 | bytes 202401 | solution.py:66
  580.7 7.7 %fusion.38 = f32[3,32,180,128]{3,1,2,0:T(8,128)} fusion(bf16[3,32,180,128]{3,2,1,0:T(8,128)(2,1)} %copy-done, f32[128,128]{1,0:T(8,128)S(1)} %get-tuple-element.220), kind=kOutput, calls=%fused_computation.58 | convolution fusion | flops 3397386240 | bytes 13336576 | tf_op jit(solution)/shard_map/dot_general | solution.py:94
  (1157 shorter events, 300.7 us)
Async XLA Ops:
  7.2 98.9 %all-reduce.3.cloned.1.call-start = ((), (), s32[]{:S(2)}) async-start(), calls=%async_computation | async-start | bytes 131072 | tf_op jit(solution)/shard_map/psum | solution.py:88
  9.3 7.9 %collective-permute-start = (bf16[3,1,180,128]{3,2,1,0:T(8,128)(2,1)S(1)}, bf16[3,1,180,128]{3,2,1,0:T(8,128)(2,1)S(1)}, u32[]{:S(2)}, u32[]{:S(2)}) collective-permute-start(bf16[3,1,180,128]{3,2,1,0:T(8,128)(2,1)S(1)} %copy.24), channel_id=1, source_target_pairs={{0,1},{1,2},{2,3},{4,5},{5,6},{6,7},{8,9},{9,10},{10,11},{12,13},{... | collective-permute-start | bytes 414728 | tf_op jit(solution)/shard_map/ppermute | solution.py:16
  14.2 7.2 %collective-permute-start.1 = (bf16[3,1,180,128]{3,2,1,0:T(8,128)(2,1)S(1)}, bf16[3,1,180,128]{3,2,1,0:T(8,128)(2,1)S(1)}, u32[]{:S(2)}, u32[]{:S(2)}) collective-permute-start(bf16[3,1,180,128]{3,2,1,0:T(8,128)(2,1)S(1)} %copy.25), channel_id=1, source_target_pairs={{1,0},{2,1},{3,2},{5,4},{6,5},{7,6},{9,8},{10,9},{11,10},{13,12},{... | collective-permute-start | bytes 414728 | tf_op jit(solution)/shard_map/ppermute | solution.py:17
  21.6 4.5 collective-permute-start.2
  21.6 4.4 collective-permute-start.3
  33.9 17.2 %copy-start.2 = (bf16[3,32,180]{2,1,0:T(8,128)(2,1)S(1)}, bf16[3,32,180]{2,1,0:T(8,128)(2,1)}, u32[]{:S(2)}) copy-start(bf16[3,32,180]{2,1,0:T(8,128)(2,1)} %param.7) | copy-start | bytes 103684
  33.9 11.2 %collective-permute-start.4 = (f32[3,1,180,128]{3,2,1,0:T(8,128)S(1)}, f32[3,1,180,128]{3,2,1,0:T(8,128)S(1)}, u32[]{:S(2)}, u32[]{:S(2)}) collective-permute-start(f32[3,1,180,128]{3,2,1,0:T(8,128)S(1)} %get-tuple-element.307), channel_id=1, source_target_pairs={{0,1},{1,2},{2,3},{4,5},{5,6},{6,7},{8,9},{9,10},{10,11},{12,13},{... | collective-permute-start | bytes 829448 | tf_op jit(solution)/shard_map/ppermute | solution.py:16
  38.4 11.0 %collective-permute-start.5 = (f32[3,1,180,128]{3,2,1,0:T(8,128)S(1)}, f32[3,1,180,128]{3,2,1,0:T(8,128)S(1)}, u32[]{:S(2)}, u32[]{:S(2)}) collective-permute-start(f32[3,1,180,128]{3,2,1,0:T(8,128)S(1)} %get-tuple-element.306), channel_id=1, source_target_pairs={{1,0},{2,1},{3,2},{5,4},{6,5},{7,6},{9,8},{10,9},{11,10},{13,12},{... | collective-permute-start | bytes 829448 | tf_op jit(solution)/shard_map/ppermute | solution.py:17
  49.4 3.4 collective-permute-start.6
  51.0 4.4 collective-permute-start.7
  69.5 2.1 copy-start
  73.6 88.0 %all-reduce.5.cloned.1.call-start = ((), (), s32[]{:S(2)}) async-start(), calls=%async_computation.1 | async-start | bytes 131072 | tf_op jit(solution)/shard_map/psum | solution.py:89
  580.7 7.8 %copy-start.1 = (f32[128,128]{1,0:T(8,128)}, f32[128,128]{1,0:T(8,128)S(1)}, u32[]{:S(2)}) copy-start(f32[128,128]{1,0:T(8,128)S(1)} %get-tuple-element.411) | copy-start | bytes 196612
Sparse Core Ops, SparseCore 0:
  73.8 32.2 all-reduce.2
  109.4 52.1 all-reduce.4
where the time goes:
time: 598 us; the launch traced here: 595 us
  matrix products  226 us (38%)
  other arithmetic  127 us (21%)
  waiting for transfers between devices  105 us (18%)
  loops' own time  97.8 us (16%)
  starting transfers between devices  16.5 us (3%)
  between operations  14.3 us (2%)
  local copies, waits for them, and re-layouts  8.73 us (1%)
    dot_general x128, matrix products, column(): resid = col_g - jnp.dot(lower, row_j, precision=lax.Precision.HIGHEST)  114 us
    dot_general x128, matrix products, row_step(): jnp.dot(above, solved, precision=lax.Precision.HIGHEST)  102 us
    another operation x1, loops' own time, chol_upper(): lax.fori_loop(0, order, column, jnp.zeros((order, order), jnp.float32))  93.2 us
    reduce_sum x128, other arithmetic, row_step(): diag = jnp.sum(jnp.where(index == i, row_u, 0.0))  77.7 us
    psum x1, waiting for transfers between devices, local(): gram = lax.psum(gram, 'lon')  55.5 us
    psum x1, waiting for transfers between devices, local(): gram = lax.psum(partial_gram, 'lat')  32.2 us
    convert_element_type x1, other arithmetic, local(): anomaly = ((final - background.astype(jnp.float32)[:, :, :, None]) * weig...  14 us
    add x128, other arithmetic, row_step(): return solved + (index == i).astype(jnp.float32)[:, None] * new_row[None, :]  12.9 us
  transfers between devices with their start and end apart: 10, of which 8 were waited for; matrix products, arithmetic and copies ran while one was open for 1% of the time, Pallas kernels for 0%

commit v1 on v0

v1 whole, which is shorter than its diff:
```python
import functools
import math

import jax
import jax.numpy as jnp
from jax import lax
from jax.experimental import pallas as pl
from jax.experimental.pallas import tpu as pltpu
from jax.sharding import PartitionSpec as P

VMEM_LIMIT = 48 * 1024 * 1024
F32 = jnp.float32
BF16 = jnp.bfloat16


def row_coefs(glob, nlat):
    row = jnp.full((8, 128), glob, jnp.int32).astype(F32)
    phi = (0.125 * (row + 0.5) - 0.0625 * nlat) * (math.pi / 180.0)
    cosine = jnp.cos(phi)
    return 0.05 + 0.2 * (1.0 - cosine), jnp.sqrt(cosine)


def rows_of(tile, count):
    return jnp.concatenate([tile] * (count // 8), axis=0)


def stencil_kernel(first_ref, m_ref, north_ref, south_ref, side_ref, bg_ref, a_ref, g_ref,
                   u_ref, v_ref, b_ref, *, nlat):
    rows, cols = m_ref.shape[1], m_ref.shape[2]
    ring = u_ref.shape[1] - 16
    first = first_ref[0]

    def fill(r, value):
        u_ref[r, 8:8 + cols] = value.astype(F32)
        u_ref[r, 8 + cols:12 + cols] = side_ref[0, r]
        u_ref[r, 7:8] = side_ref[0, r, 3:4]
        u_ref[r, 8 + ring:9 + ring] = value[0:1].astype(F32)

    for r in range(2):
        fill(r, north_ref[0, r])
        fill(rows + 2 + r, south_ref[0, r])

    @pl.loop(0, rows)
    def _(j):
        fill(j + 2, m_ref[0, j])

    @pl.loop(1, rows + 3)
    def _(r):
        glob = first + r - 2
        kx, _ = row_coefs(glob, nlat)
        inside = jnp.full((8, 128), (glob >= 0) & (glob < nlat), jnp.bool_)
        c = rows_of(jnp.where(inside, 3.0 - 10.0 * kx, 0.0), ring)
        k = rows_of(jnp.where(inside, 5.0 * kx, 0.0), ring)
        one = rows_of(jnp.where(inside, 1.0, 0.0), ring)
        v = (one * (u_ref[r - 1, 8:8 + ring] + u_ref[r + 1, 8:8 + ring]) + c * u_ref[r, 8:8 + ring]
             + k * (u_ref[r, 7:7 + ring] + u_ref[r, 9:9 + ring]))
        v_ref[r, 8:8 + ring] = v
        v_ref[r, 7:8] = v[ring - 1:ring]
        v_ref[r, 8 + ring:9 + ring] = v[0:1]

    live = lax.broadcasted_iota(jnp.int32, (ring, 128), 0) < cols
    pick = lax.broadcasted_iota(jnp.int32, (rows, 128), 0)

    @pl.loop(0, rows)
    def _(j):
        r = j + 2
        kx, weight = row_coefs(first + j, nlat)
        c = rows_of(3.0 - 10.0 * kx, ring)
        k = rows_of(5.0 * kx, ring)
        w = rows_of(weight, ring)
        ground = lax.dot_general(bg_ref[0], (pick == j).astype(BF16), (((0,), (0,)), ((), ())),
                                 preferred_element_type=F32)
        y = (v_ref[r - 1, 8:8 + ring] + v_ref[r + 1, 8:8 + ring] + c * v_ref[r, 8:8 + ring]
             + k * (v_ref[r, 7:7 + ring] + v_ref[r, 9:9 + ring]))
        a = jnp.where(live, (y * 0.04 - ground) * w, 0.0)
        b_ref[j, 0:ring] = a
        b_ref[j, ring:] = jnp.zeros((b_ref.shape[1] - ring, 128), F32)
        a_ref[j] = b_ref[j].astype(BF16)

    flat = a_ref[...].reshape(-1, 128)
    gram = lax.dot_general(flat, flat, (((0,), (0,)), ((), ())), preferred_element_type=F32)

    @pl.when(pl.program_id(0) == 0)
    def _():
        g_ref[...] = gram

    @pl.when(pl.program_id(0) > 0)
    def _():
        g_ref[...] += gram


def factor(g):
    n = 128
    lane = lax.broadcasted_iota(jnp.int32, (8, n), 1)
    sub = lax.broadcasted_iota(jnp.int32, (8, n), 0)
    w = list(g)
    tiles = len(w)
    for b0 in range(tiles):
        cols = [[jnp.broadcast_to(w[b][:, 8 * b0 + j:8 * b0 + j + 1], (8, n)) for b in range(b0, tiles)]
                for j in range(8)]
        for s in range(8):
            k = 8 * b0 + s
            inverse = 1.0 / jnp.broadcast_to(cols[s][0][s:s + 1], (8, n))
            pivot_row = jnp.where(lane == k, 1.0, jnp.broadcast_to(w[b0][s:s + 1], (8, n)))
            rows = [jnp.broadcast_to(cols[j][0][s:s + 1], (8, n)) for j in range(s + 1, 8)]
            for b in range(b0, tiles):
                i = b - b0
                f = cols[s][i] * inverse
                if i == 0:
                    if s == 7:
                        continue
                    f = jnp.where(sub > s, f, 0.0)
                    kept = jnp.where((lane == k) & (sub > s), 0.0, w[b])
                else:
                    kept = jnp.where(lane == k, 0.0, w[b])
                w[b] = kept - f * pivot_row
                for j in range(s + 1, 8):
                    cols[j][i] = cols[j][i] - f * rows[j - s - 1]
    r, x = [], []
    for b in range(tiles):
        diag = lane == sub + 8 * b
        scale = lax.rsqrt(jnp.sum(jnp.where(diag, w[b], 0.0), axis=1, keepdims=True))
        r.append(jnp.where(lane >= sub + 8 * b, w[b] * scale, 0.0))
        x.append(jnp.where(diag, scale, jnp.where(lane < sub + 8 * b, w[b] * scale, 0.0)))
    return jnp.concatenate(r, axis=0), jnp.concatenate(x, axis=0)


def modes_kernel(core_ref, own_ref, other_ref, a_hbm, out_ref, r_ref, a_ref, x_ref, sem, *, total):
    step = pl.program_id(0)
    lats, cols = out_ref.shape[1], out_ref.shape[2]
    copy = pltpu.make_async_copy(a_hbm, a_ref, sem)

    @pl.when(step == 0)
    def _():
        copy.start()
        own = jnp.full((8, 128), core_ref[0], jnp.int32) == 1
        g = [jnp.where(own, own_ref[8 * b:8 * b + 8], other_ref[8 * b:8 * b + 8]) * (1.0 / total)
             for b in range(16)]
        r, x = factor(g)
        r_ref[...] = r
        inv = x.T
        high = inv.astype(BF16)
        x_ref[0] = high
        x_ref[1] = (inv - high.astype(F32)).astype(BF16)
        copy.wait()

    a = a_ref[pl.ds(step * lats, lats)].reshape(-1, 128)
    m = jnp.dot(a, x_ref[0], preferred_element_type=F32) + jnp.dot(a, x_ref[1], preferred_element_type=F32)
    out_ref[0] = m.reshape(lats, -1, 128)[:, :cols]


def halos(members):
    lat, lon = lax.axis_size("lat"), lax.axis_size("lon")
    north = [(i, i + 1) for i in range(lat - 1)]
    south = [(i + 1, i) for i in range(lat - 1)]
    east = [((i + 1) % lon, i) for i in range(lon)]
    west = [(i, (i + 1) % lon) for i in range(lon)]
    from_north = lax.ppermute(members[:, -2:], "lat", north)
    from_south = lax.ppermute(members[:, :2], "lat", south)
    from_east = lax.ppermute(members[:, :, :2], "lon", east)
    from_west = lax.ppermute(members[:, :, -2:], "lon", west)
    ends = jnp.concatenate([from_north, from_south], axis=1)
    ends_east = lax.ppermute(ends[:, :, :2], "lon", east)
    ends_west = lax.ppermute(ends[:, :, -2:], "lon", west)
    side = jnp.concatenate([from_east, from_west], axis=2)
    corner = jnp.concatenate([ends_east, ends_west], axis=2)
    side = jnp.concatenate([corner[:, :2], side, corner[:, 2:]], axis=1)
    return from_north, from_south, side.astype(F32)


def total_gram(gram):
    lat, lon = lax.axis_size("lat"), lax.axis_size("lon")
    gram = gram + lax.ppermute(gram, "lon", [(i, i + 1) for i in range(0, lon, 2)])
    step = 2
    while step < lon:
        gram = gram + lax.ppermute(gram, "lon", [(i, i ^ step) for i in range(1, lon, 2)])
        step *= 2
    step = 1
    while step < lat:
        pairs = [(k * lat + i, k * lat + (i ^ step)) for k in range(1, lon, 2) for i in range(lat)]
        gram = gram + lax.ppermute(gram, ("lon", "lat"), pairs)
        step *= 2
    other = lax.ppermute(gram, "lon", [(i + 1, i) for i in range(0, lon, 2)])
    return gram, other


def local(members, background):
    fields, rows, cols, width = members.shape
    lat, lon = lax.axis_size("lat"), lax.axis_size("lon")
    nlat = rows * lat
    ring = -(-(cols + 4) // 8) * 8
    held = -(-ring // 16) * 16
    first = (lax.axis_index("lat") * rows).astype(jnp.int32).reshape(1)
    north, south, side = halos(members)
    ground = jnp.pad(background, ((0, 0), (0, 0), (0, ring - cols)))
    vmem = functools.partial(pltpu.VMEM)
    a, gram = pl.pallas_call(
        functools.partial(stencil_kernel, nlat=nlat),
        grid=(fields,),
        out_shape=(jax.ShapeDtypeStruct((fields * rows, held, width), BF16),
                   jax.ShapeDtypeStruct((width, width), F32)),
        in_specs=[
            pl.BlockSpec(memory_space=pltpu.SMEM),
            pl.BlockSpec((1, rows, cols, width), lambda f: (f, 0, 0, 0)),
            pl.BlockSpec((1, 2, cols, width), lambda f: (f, 0, 0, 0)),
            pl.BlockSpec((1, 2, cols, width), lambda f: (f, 0, 0, 0)),
            pl.BlockSpec((1, rows + 4, 4, width), lambda f: (f, 0, 0, 0)),
            pl.BlockSpec((1, rows, ring), lambda f: (f, 0, 0)),
        ],
        out_specs=(pl.BlockSpec((rows, held, width), lambda f: (f, 0, 0)),
                   pl.BlockSpec((width, width), lambda f: (0, 0))),
        scratch_shapes=[vmem((rows + 4, ring + 16, width), F32), vmem((rows + 4, ring + 16, width), F32),
                        vmem((rows, held, width), F32)],
        compiler_params=pltpu.CompilerParams(vmem_limit_bytes=VMEM_LIMIT),
    )(first, members, north, south, side, ground)
    own, other = total_gram(gram)
    core = (lax.axis_index("lon") % 2).astype(jnp.int32).reshape(1)
    lats = 8
    per = rows // lats
    modes, r_factor = pl.pallas_call(
        functools.partial(modes_kernel, total=float(fields * nlat * cols * lon)),
        grid=(fields * per,),
        out_shape=(jax.ShapeDtypeStruct(members.shape, F32), jax.ShapeDtypeStruct((width, width), F32)),
        in_specs=[
            pl.BlockSpec(memory_space=pltpu.SMEM),
            pl.BlockSpec((width, width), lambda s: (0, 0)),
            pl.BlockSpec((width, width), lambda s: (0, 0)),
            pl.BlockSpec(memory_space=pl.ANY),
        ],
        out_specs=(pl.BlockSpec((1, lats, cols, width), lambda s: (s // per, s % per, 0, 0)),
                   pl.BlockSpec((width, width), lambda s: (0, 0))),
        scratch_shapes=[vmem((fields * rows, held, width), BF16), vmem((2, width, width), BF16),
                        pltpu.SemaphoreType.DMA],
        compiler_params=pltpu.CompilerParams(vmem_limit_bytes=VMEM_LIMIT),
    )(core, own, other, a)
    return modes, r_factor


def solution(mesh):
    return jax.shard_map(
        local,
        mesh=mesh,
        in_specs=(P(None, "lat", "lon", None), P(None, "lat", "lon")),
        out_specs=(P(None, "lat", "lon", None), P()),
        check_vma=False,
    )
```

time: 598 us -> 112 us (0.19)
  matrix products: 226 us -> 0 us
  other arithmetic: 127 us -> 0.17 us
  loops' own time: 97.8 us -> 0 us
  waiting for transfers between devices: 105 us -> 33.3 us
  Pallas kernels: 0 us -> 42.6 us
  between operations: 14.3 us -> 0.87 us
  local copies, waits for them, and re-layouts: 8.73 us -> 19.6 us
    dot_general x258 -> x0, matrix products: 226 us -> none  [the longest x128 114 us: column(): resid = col_g - jnp.dot(lower, row_j, precision=lax.Precision.HIGHEST)]
    another operation x2 -> x0, loops' own time: 97.8 us -> none  [the longest x1 93.2 us: chol_upper(): lax.fori_loop(0, order, column, jnp.zeros((order, order), jnp.float32))]
    psum x2 -> x0, waiting for transfers between devices: 87.7 us -> none  [the longest x1 55.5 us: local(): gram = lax.psum(gram, 'lon')]
    reduce_sum x128 -> x0, other arithmetic: 77.7 us -> none  [row_step(): diag = jnp.sum(jnp.where(index == i, row_u, 0.0))]
    pallas_call x0 -> x2, Pallas kernels: none -> 42.6 us  [the longest x1 30.3 us: local(): pl.pallas_call(functools.partial(stencil_kernel, nlat=nlat), grid=(fields...]
    add x258 -> x5, other arithmetic: 29.7 us -> 0.05 us  [the longest x2 0.02 us: total_gram(): gram + lax.ppermute(gram, 'lon', [(i, i ^ step) for i in range(1, lon, 2)])]
    convert_element_type x260 -> x1, other arithmetic: 16.9 us -> 0.1 us  [halos(): return (from_north, from_south, side.astype(F32))]
    ppermute x8 -> x12, waiting for transfers between devices: 17.4 us -> 33.3 us  [the longest x1 19.3 us: total_gram(): other = lax.ppermute(gram, 'lon', [(i + 1, i) for i in range(0, lon, 2)])]
  transfers between devices with their start and end apart: 10 -> 12, of which waited for: 8 -> 6; matrix products, arithmetic and copies ran while one was open for 1% -> 0% of each run, Pallas kernels for 0% -> 0%
where the time goes in v1:
time: 112 us; the launch traced here: 111 us
  Pallas kernels  42.6 us (38%)
  waiting for transfers between devices  33.3 us (30%)
  local copies, waits for them, and re-layouts  19.6 us (18%)
  starting transfers between devices  14.9 us (13%)
    pallas_call x1, Pallas kernels, local(): pl.pallas_call(functools.partial(stencil_kernel, nlat=nlat), grid=(fields...  30.3 us
    ppermute x1, waiting for transfers between devices, total_gram(): other = lax.ppermute(gram, 'lon', [(i + 1, i) for i in range(0, lon, 2)])  19.3 us
    pallas_call x1, Pallas kernels, local(): pl.pallas_call(functools.partial(modes_kernel, total=float(fields * nlat...  12.3 us
    unnamed x10, local copies, waits for them, and re-layouts  10.7 us
    pallas_call x1, local copies, waits for them, and re-layouts, local(): pl.pallas_call(functools.partial(modes_kernel, total=float(fields * nlat...  8.63 us
    ppermute x1, starting transfers between devices, halos(): from_north = lax.ppermute(members[:, -2:], 'lat', north)  4.95 us
    ppermute x1, waiting for transfers between devices, halos(): from_north = lax.ppermute(members[:, -2:], 'lat', north)  4.67 us
    ppermute x1, waiting for transfers between devices, halos(): from_south = lax.ppermute(members[:, :2], 'lat', south)  4.11 us
  transfers between devices with their start and end apart: 12, of which 6 were waited for; matrix products, arithmetic and copies ran while one was open for 0% of the time, Pallas kernels for 0%

profile of v1, /device:TPU:0, one launch (start us, length us, event | category | flops | bytes accessed | tf_op | source)
XLA Modules:
  0.0 111.3 jit_solution(5887967729795295198)
XLA Ops:
  0.6 0.0 copy-start.3
  0.6 4.0 %copy.8.m_ref = bf16[3,32,180,128]{3,2,1,0:T(8,128)(2,1)S(1)} copy(bf16[3,32,180,128]{3,1,2,0:T(8,128)(2,1)} %param.2) | data formatting | bytes 8847360 | tf_op args[0]
  4.7 4.9 %collective-permute-start = (bf16[3,2,180,128]{3,2,1,0:T(8,128)(2,1)S(1)}, bf16[3,2,180,128]{3,2,1,0:T(8,128)(2,1)S(1)}, u32[]{:S(2)}, u32[]{:S(2)}) collective-permute-start(bf16[3,2,180,128]{3,2,1,0:T(8,128)(2,1)S(1)} %get-tuple-element.11), channel_id=1, source_target_pairs={{0,1},{1,2},{2,3},{4,5},{5,6},{6,7},{8,9},{9,10},{10,11},{12,13},{... | collective-permute-start | bytes 829448 | tf_op jit(solution)/shard_map/ppermute | solution.py:158
  9.6 1.3 %collective-permute-start.1 = (bf16[3,2,180,128]{3,2,1,0:T(8,128)(2,1)S(1)}, bf16[3,2,180,128]{3,2,1,0:T(8,128)(2,1)S(1)}, u32[]{:S(2)}, u32[]{:S(2)}) collective-permute-start(bf16[3,2,180,128]{3,2,1,0:T(8,128)(2,1)S(1)} %get-tuple-element.10), channel_id=1, source_target_pairs={{1,0},{2,1},{3,2},{5,4},{6,5},{7,6},{9,8},{10,9},{11,10},{13,12},{... | collective-permute-start | bytes 829448 | tf_op jit(solution)/shard_map/ppermute | solution.py:159
  10.9 4.7 %collective-permute-done.north_ref = bf16[3,2,180,128]{3,2,1,0:T(8,128)(2,1)S(1)} collective-permute-done((bf16[3,2,180,128]{3,2,1,0:T(8,128)(2,1)S(1)}, bf16[3,2,180,128]{3,2,1,0:T(8,128)(2,1)S(1)}, u32[]{:S(2)}, u32[]{:S(2)}) %collective-permute-start) | collective-permute-done | bytes 276512 | tf_op jit(solution)/shard_map/ppermute | solution.py:158
  15.6 4.1 %collective-permute-done.1.south_ref = bf16[3,2,180,128]{3,2,1,0:T(8,128)(2,1)S(1)} collective-permute-done((bf16[3,2,180,128]{3,2,1,0:T(8,128)(2,1)S(1)}, bf16[3,2,180,128]{3,2,1,0:T(8,128)(2,1)S(1)}, u32[]{:S(2)}, u32[]{:S(2)}) %collective-permute-start.1) | collective-permute-done | bytes 276512 | tf_op jit(solution)/shard_map/ppermute | solution.py:159
  19.8 0.7 collective-permute-start.2
  20.5 0.0 collective-permute-start.3
  20.5 0.1 fusion.6
  20.6 0.0 copy-start
  20.6 2.1 %copy-done = bf16[3,32,180,128]{3,2,1,0:T(8,128)(2,1)} copy-done((bf16[3,32,180,128]{3,2,1,0:T(8,128)(2,1)}, bf16[3,32,180,128]{3,2,1,0:T(8,128)(2,1)S(1)}, u32[]{:S(2)}) %copy-start) | copy-done | bytes 4423704
  22.8 2.6 %collective-permute-start.4 = (bf16[3,32,2,128]{3,2,1,0:T(2,128)(2,1)S(1)}, bf16[3,32,2,128]{3,2,1,0:T(2,128)(2,1)S(1)}, u32[]{:S(2)}, u32[]{:S(2)}) collective-permute-start(bf16[3,32,2,128]{3,2,1,0:T(2,128)(2,1)S(1)} %get-tuple-element.8), channel_id=1, source_target_pairs={{4,0},{8,4},{12,8},{16,12},{20,16},{24,20},{28,24},{0,28},{5,1},{9... | collective-permute-start | bytes 147464 | tf_op jit(solution)/shard_map/ppermute | solution.py:160
  25.4 0.0 collective-permute-start.5
  25.4 0.0 copy-done.3
  25.4 0.0 collective-permute-done.2
  25.4 0.0 collective-permute-done.3
  25.5 1.7 %collective-permute-done.4 = bf16[3,32,2,128]{3,2,1,0:T(2,128)(2,1)S(1)} collective-permute-done((bf16[3,32,2,128]{3,2,1,0:T(2,128)(2,1)S(1)}, bf16[3,32,2,128]{3,2,1,0:T(2,128)(2,1)S(1)}, u32[]{:S(2)}, u32[]{:S(2)}) %collective-permute-start.4) | collective-permute-done | bytes 49184 | tf_op jit(solution)/shard_map/ppermute | solution.py:160
  27.1 2.7 %collective-permute-done.5 = bf16[3,32,2,128]{3,2,1,0:T(2,128)(2,1)S(1)} collective-permute-done((bf16[3,32,2,128]{3,2,1,0:T(2,128)(2,1)S(1)}, bf16[3,32,2,128]{3,2,1,0:T(2,128)(2,1)S(1)}, u32[]{:S(2)}, u32[]{:S(2)}) %collective-permute-start.5) | collective-permute-done | bytes 49184 | tf_op jit(solution)/shard_map/ppermute | solution.py:161
  29.8 0.1 fusion.4.side_ref
  29.9 0.0 copy-start.1
  29.9 2.3 %copy-done.1 = bf16[3,32,180,128]{3,2,1,0:T(8,128)(2,1)S(1)} copy-done((bf16[3,32,180,128]{3,2,1,0:T(8,128)(2,1)S(1)}, bf16[3,32,180,128]{3,2,1,0:T(8,128)(2,1)}, u32[]{:S(2)}) %copy-start.1) | copy-done | bytes 4423704
  32.2 30.3 %shard_map.41 = (bf16[96,192,128]{2,1,0:T(8,128)(2,1)}, f32[128,128]{1,0:T(8,128)S(1)}) custom-call(s32[1]{0:T(128)} %bitcast.1.first_ref, bf16[3,32,180,128]{3,2,1,0:T(8,128)(2,1)S(1)} %copy-done.1, bf16[3,2,180,128]{3,2,1,0:T(8,128)(2,1)S(1)} %collective-permute-done.north_ref, bf16[3,2,180,128]{3,2,1,0:T(8,128)(2,1)S(1)} %collective-permute-done.1.south_ref, ...), custom_call_target="tpu_custom_call" | custom-call | tf_op jit(solution)/shard_map/pallas_call | solution.py:197
  62.5 1.3 %collective-permute-start.6 = (f32[128,128]{1,0:T(8,128)S(1)}, f32[128,128]{1,0:T(8,128)S(1)}, u32[]{:S(2)}, u32[]{:S(2)}) collective-permute-start(f32[128,128]{1,0:T(8,128)S(1)} %get-tuple-element.4), channel_id=1, source_target_pairs={{0,4},{8,12},{16,20},{24,28},{1,5},{9,13},{17,21},{25,29},{2,6},{1... | collective-permute-start | bytes 196616 | tf_op jit(solution)/shard_map/ppermute | solution.py:173
  63.8 0.9 collective-permute-done.6
  64.7 0.7 collective-permute-start.7
  65.4 0.0 collective-permute-done.7
  65.4 0.7 collective-permute-start.8
  66.1 0.0 collective-permute-done.8
  66.1 0.7 collective-permute-start.9
  66.8 0.0 collective-permute-done.9
  66.8 0.7 collective-permute-start.10
  67.5 0.0 collective-permute-done.10
  67.5 1.3 %collective-permute-start.11 = (f32[128,128]{1,0:T(8,128)S(1)}, f32[128,128]{1,0:T(8,128)S(1)}, u32[]{:S(2)}, u32[]{:S(2)}) collective-permute-start(f32[128,128]{1,0:T(8,128)S(1)} %add.26.own_ref), channel_id=1, source_target_pairs={{4,0},{12,8},{20,16},{28,24},{5,1},{13,9},{21,17},{29,25},{6,2},{1... | collective-permute-start | bytes 196616 | tf_op jit(solution)/shard_map/ppermute | solution.py:183
  68.8 19.3 %collective-permute-done.11.other_ref = f32[128,128]{1,0:T(8,128)S(1)} collective-permute-done((f32[128,128]{1,0:T(8,128)S(1)}, f32[128,128]{1,0:T(8,128)S(1)}, u32[]{:S(2)}, u32[]{:S(2)}) %collective-permute-start.11) | collective-permute-done | bytes 65568 | tf_op jit(solution)/shard_map/ppermute | solution.py:183
  88.1 0.0 copy-start.2
  88.1 2.3 %copy-done.2 = bf16[96,192,128]{2,1,0:T(8,128)(2,1)S(1)} copy-done((bf16[96,192,128]{2,1,0:T(8,128)(2,1)S(1)}, bf16[96,192,128]{2,1,0:T(8,128)(2,1)}, u32[]{:S(2)}) %copy-start.2) | copy-done | bytes 4718616
  90.4 12.3 %shard_map.42 = (f32[3,32,180,128]{3,2,1,0:T(8,128)}, f32[128,128]{1,0:T(8,128)}) custom-call(s32[1]{0:T(128)} %bitcast.core_ref, f32[128,128]{1,0:T(8,128)S(1)} %add.26.own_ref, f32[128,128]{1,0:T(8,128)S(1)} %collective-permute-done.11.other_ref, bf16[96,192,128]{2,1,0:T(8,128)(2,1)S(1)} %copy-done.2), custom_call_target="tpu_custom_call" | custom-call | tf_op jit(solution)/shard_map/pallas_call | solution.py:220
  102.7 8.6 %copy.9 = f32[3,32,180,128]{3,1,2,0:T(8,128)} copy(f32[3,32,180,128]{3,2,1,0:T(8,128)} %get-tuple-element.6) | data formatting | bytes 17694720 | tf_op jit(solution)/shard_map/pallas_call | solution.py:220
  (11 shorter events, 0.2 us)
Async XLA Ops:
  0.6 24.8 %copy-start.3 = (bf16[3,32,180]{2,1,0:T(8,128)(2,1)S(1)}, bf16[3,32,180]{2,1,0:T(8,128)(2,1)}, u32[]{:S(2)}) copy-start(bf16[3,32,180]{2,1,0:T(8,128)(2,1)} %param.3) | copy-start | bytes 103684
  4.7 10.9 %collective-permute-start = (bf16[3,2,180,128]{3,2,1,0:T(8,128)(2,1)S(1)}, bf16[3,2,180,128]{3,2,1,0:T(8,128)(2,1)S(1)}, u32[]{:S(2)}, u32[]{:S(2)}) collective-permute-start(bf16[3,2,180,128]{3,2,1,0:T(8,128)(2,1)S(1)} %get-tuple-element.11), channel_id=1, source_target_pairs={{0,1},{1,2},{2,3},{4,5},{5,6},{6,7},{8,9},{9,10},{10,11},{12,13},{... | collective-permute-start | bytes 829448 | tf_op jit(solution)/shard_map/ppermute | solution.py:158
  9.6 10.1 %collective-permute-start.1 = (bf16[3,2,180,128]{3,2,1,0:T(8,128)(2,1)S(1)}, bf16[3,2,180,128]{3,2,1,0:T(8,128)(2,1)S(1)}, u32[]{:S(2)}, u32[]{:S(2)}) collective-permute-start(bf16[3,2,180,128]{3,2,1,0:T(8,128)(2,1)S(1)} %get-tuple-element.10), channel_id=1, source_target_pairs={{1,0},{2,1},{3,2},{5,4},{6,5},{7,6},{9,8},{10,9},{11,10},{13,12},{... | collective-permute-start | bytes 829448 | tf_op jit(solution)/shard_map/ppermute | solution.py:159
  19.8 5.6 %collective-permute-start.2 = (bf16[3,4,2,128]{3,2,1,0:T(2,128)(2,1)S(1)}, bf16[3,4,2,128]{3,2,1,0:T(2,128)(2,1)S(1)}, u32[]{:S(2)}, u32[]{:S(2)}) collective-permute-start(bf16[3,4,2,128]{3,2,1,0:T(2,128)(2,1)S(1)} %get-tuple-element.12), channel_id=1, source_target_pairs={{4,0},{8,4},{12,8},{16,12},{20,16},{24,20},{28,24},{0,28},{5,1},{9... | collective-permute-start | bytes 18440 | tf_op jit(solution)/shard_map/ppermute | solution.py:163
  20.5 4.9 %collective-permute-start.3 = (bf16[3,4,2,128]{3,2,1,0:T(2,128)(2,1)S(1)}, bf16[3,4,2,128]{3,2,1,0:T(2,128)(2,1)S(1)}, u32[]{:S(2)}, u32[]{:S(2)}) collective-permute-start(bf16[3,4,2,128]{3,2,1,0:T(2,128)(2,1)S(1)} %get-tuple-element.13), channel_id=1, source_target_pairs={{0,4},{4,8},{8,12},{12,16},{16,20},{20,24},{24,28},{28,0},{1,5},{5... | collective-permute-start | bytes 18440 | tf_op jit(solution)/shard_map/ppermute | solution.py:164
  20.6 2.1 %copy-start = (bf16[3,32,180,128]{3,2,1,0:T(8,128)(2,1)}, bf16[3,32,180,128]{3,2,1,0:T(8,128)(2,1)S(1)}, u32[]{:S(2)}) copy-start(bf16[3,32,180,128]{3,2,1,0:T(8,128)(2,1)S(1)} %copy.8.m_ref) | copy-start | bytes 13271044
  22.8 4.4 %collective-permute-start.4 = (bf16[3,32,2,128]{3,2,1,0:T(2,128)(2,1)S(1)}, bf16[3,32,2,128]{3,2,1,0:T(2,128)(2,1)S(1)}, u32[]{:S(2)}, u32[]{:S(2)}) collective-permute-start(bf16[3,32,2,128]{3,2,1,0:T(2,128)(2,1)S(1)} %get-tuple-element.8), channel_id=1, source_target_pairs={{4,0},{8,4},{12,8},{16,12},{20,16},{24,20},{28,24},{0,28},{5,1},{9... | collective-permute-start | bytes 147464 | tf_op jit(solution)/shard_map/ppermute | solution.py:160
  25.4 4.4 %collective-permute-start.5 = (bf16[3,32,2,128]{3,2,1,0:T(2,128)(2,1)S(1)}, bf16[3,32,2,128]{3,2,1,0:T(2,128)(2,1)S(1)}, u32[]{:S(2)}, u32[]{:S(2)}) collective-permute-start(bf16[3,32,2,128]{3,2,1,0:T(2,128)(2,1)S(1)} %get-tuple-element.9), channel_id=1, source_target_pairs={{0,4},{4,8},{8,12},{12,16},{16,20},{20,24},{24,28},{28,0},{1,5},{5... | collective-permute-start | bytes 147464 | tf_op jit(solution)/shard_map/ppermute | solution.py:161
  29.9 2.3 %copy-start.1 = (bf16[3,32,180,128]{3,2,1,0:T(8,128)(2,1)S(1)}, bf16[3,32,180,128]{3,2,1,0:T(8,128)(2,1)}, u32[]{:S(2)}) copy-start(bf16[3,32,180,128]{3,2,1,0:T(8,128)(2,1)} %copy-done) | copy-start | bytes 13271044
  62.5 2.2 %collective-permute-start.6 = (f32[128,128]{1,0:T(8,128)S(1)}, f32[128,128]{1,0:T(8,128)S(1)}, u32[]{:S(2)}, u32[]{:S(2)}) collective-permute-start(f32[128,128]{1,0:T(8,128)S(1)} %get-tuple-element.4), channel_id=1, source_target_pairs={{0,4},{8,12},{16,20},{24,28},{1,5},{9,13},{17,21},{25,29},{2,6},{1... | collective-permute-start | bytes 196616 | tf_op jit(solution)/shard_map/ppermute | solution.py:173
  64.7 0.7 collective-permute-start.7
  65.4 0.7 collective-permute-start.8
  66.1 0.7 collective-permute-start.9
  66.8 0.7 collective-permute-start.10
  67.5 20.6 %collective-permute-start.11 = (f32[128,128]{1,0:T(8,128)S(1)}, f32[128,128]{1,0:T(8,128)S(1)}, u32[]{:S(2)}, u32[]{:S(2)}) collective-permute-start(f32[128,128]{1,0:T(8,128)S(1)} %add.26.own_ref), channel_id=1, source_target_pairs={{4,0},{12,8},{20,16},{28,24},{5,1},{13,9},{21,17},{29,25},{6,2},{1... | collective-permute-start | bytes 196616 | tf_op jit(solution)/shard_map/ppermute | solution.py:183
  88.1 2.3 %copy-start.2 = (bf16[96,192,128]{2,1,0:T(8,128)(2,1)S(1)}, bf16[96,192,128]{2,1,0:T(8,128)(2,1)}, u32[]{:S(2)}) copy-start(bf16[96,192,128]{2,1,0:T(8,128)(2,1)} %get-tuple-element.5.a_hbm) | copy-start | bytes 14155780

commit v2 on v1

v2 whole, which is shorter than its diff:
```python
import functools
import math

import jax
import jax.numpy as jnp
from jax import lax
from jax.experimental import pallas as pl
from jax.experimental.pallas import tpu as pltpu
from jax.sharding import PartitionSpec as P

VMEM_LIMIT = 40 * 1024 * 1024
F32 = jnp.float32
BF16 = jnp.bfloat16
TILE = (8, 128)


def row_coefs(glob, nlat):
    phi = (0.125 * (glob.astype(F32) + 0.5) - 0.0625 * nlat) * (math.pi / 180.0)
    cosine = jnp.cos(phi)
    return 0.05 + 0.2 * (1.0 - cosine), jnp.sqrt(cosine)


def scaled_coefs(glob, nlat):
    kx, weight = row_coefs(glob, nlat)
    return 3.0 - 10.0 * kx, 5.0 * kx, weight


def sublane():
    return lax.broadcasted_iota(jnp.int32, TILE, 0)


def tiles_of(x):
    return [x[8 * t:8 * t + 8] for t in range(x.shape[0] // 8)]


def neighbours(x, above, below):
    sub = sublane()
    down = [pltpu.roll(t, 1, 0) for t in x]
    up = [pltpu.roll(t, 7, 0) for t in x]
    out = []
    for i in range(len(x)):
        north = jnp.where(sub == 0, down[i - 1] if i else above, down[i])
        south = jnp.where(sub == 7, up[i + 1] if i + 1 < len(x) else below, up[i])
        out.append(north + south)
    return out


def gram_of(a):
    return lax.dot_general(a, a, (((0,), (0,)), ((), ())), preferred_element_type=F32)


def inner_kernel(first_ref, m_ref, bg_ref, a_ref, en_ref, es_ref, g_ref, coef_ref, bgf_ref, *, nlat, group):
    cols, rows = m_ref.shape[1], m_ref.shape[2]
    nt = rows // 8
    first = first_ref[0]
    sub = sublane()
    for t in range(nt):
        c, k, w = scaled_coefs(first + 8 * t + sub, nlat)
        live = (8 * t + sub >= 2) & (8 * t + sub < rows - 2)
        coef_ref[0, t], coef_ref[1, t] = c, k
        coef_ref[2, t], coef_ref[3, t] = 0.04 * w, w
        coef_ref[4, t], coef_ref[5, t] = jnp.where(live, 0.04 * w, 0.0), jnp.where(live, w, 0.0)
    bgf_ref[:, 0:cols] = bg_ref[0].astype(F32)
    north_in = jnp.where(jnp.full(TILE, first, jnp.int32) > 0, 1.0, 0.0)
    south_in = jnp.where(jnp.full(TILE, first, jnp.int32) + rows < nlat, 1.0, 0.0)
    zero = jnp.zeros(TILE, F32)
    width = bgf_ref.shape[1]

    def load(l):
        return tiles_of(m_ref[0, l].astype(F32))

    def body(g, carry):
        u0, u1, v0, v1, gram = carry
        base = g * group
        ground = pltpu.roll(bgf_ref[...], lax.rem(width + 1 - base, width), 1)
        made = []
        for i in range(group):
            u2 = load(jnp.minimum(base + i + 1, cols - 1))
            ns = neighbours(u1, zero, zero)
            v2 = [ns[t] + coef_ref[0, t] * u1[t] + coef_ref[1, t] * (u0[t] + u2[t]) for t in range(nt)]
            ns = neighbours(v1, north_in * pltpu.roll(u0[0], 0, 0), south_in * u0[nt - 1])
            y = [ns[t] + coef_ref[0, t] * v1[t] + coef_ref[1, t] * (v0[t] + v2[t]) for t in range(nt)]
            b = [jnp.broadcast_to(ground[8 * t:8 * t + 8, i:i + 1], TILE) for t in range(nt)]
            a = jnp.concatenate([y[t] * coef_ref[4, t] - b[t] * coef_ref[5, t] for t in range(nt)],
                                axis=0).astype(BF16)
            a_ref[0, jnp.maximum(base + i - 1, 0)] = a
            e = y[0] * coef_ref[2, 0] - b[0] * coef_ref[3, 0]
            en_ref.at[0, pl.ds(pl.multiple_of(g * 2 * group, 8), 2 * group)][2 * i:2 * i + 2] = e[0:2]
            e = y[nt - 1] * coef_ref[2, nt - 1] - b[nt - 1] * coef_ref[3, nt - 1]
            es_ref.at[0, pl.ds(pl.multiple_of(g * 2 * group, 8), 2 * group)][2 * i:2 * i + 2] = e[6:8]
            made.append(a)
            u0, u1, v0, v1 = u1, u2, v1, v2
        if True:
            for i in (0, 1, 2):
                made[i] = jnp.where(jnp.full((rows, 128), base + i - 1, jnp.int32) >= 2, made[i], jnp.zeros_like(made[i]))
            i = group - 1
            made[i] = jnp.where(jnp.full((rows, 128), base + i - 1, jnp.int32) < cols - 2, made[i],
                                jnp.zeros_like(made[i]))
        gram = gram + gram_of(jnp.concatenate(made, axis=0))
        return u0, u1, v0, v1, gram

    u = load(0)
    start = ([zero] * nt, u, [zero] * nt, [zero] * nt, jnp.zeros((128, 128), F32))
    gram = lax.fori_loop(0, cols // group, body, start)[4]
    for l in (0, 1, cols - 2, cols - 1):
        a_ref[0, l] = jnp.zeros((rows, 128), BF16)

    @pl.when(pl.program_id(0) == 0)
    def _():
        g_ref[...] = gram

    @pl.when(pl.program_id(0) > 0)
    def _():
        g_ref[...] += gram


def pack(g):
    lane = lax.broadcasted_iota(jnp.int32, (32, 128), 1)
    middle = jnp.where(lane < 32, pltpu.roll(g[96:128], 32, 1), g[32:64])
    last = jnp.where(lane[:16] < 64, pltpu.roll(g[80:96], 64, 1), g[64:80])
    return jnp.concatenate([g[0:32], middle, last], axis=0)


def unpack(p):
    upper = jnp.concatenate([p[0:80], pltpu.roll(p[64:80], 64, 1), pltpu.roll(p[32:64], 96, 1)], axis=0)
    row = lax.broadcasted_iota(jnp.int32, (128, 128), 0)
    col = lax.broadcasted_iota(jnp.int32, (128, 128), 1)
    return jnp.where(col >= row, upper, upper.T)


def outer_kernel(first_ref, en_ref, es_ref, n_ref, s_ref, x_ref, bg_ref, gin_ref, an_ref, as_ref, ac_ref, g_ref,
                 pad_ref, *, nlat):
    fields, pairs = n_ref.shape[0], n_ref.shape[1]
    rows, cols = bg_ref.shape[1], bg_ref.shape[2]
    first = first_ref[0]
    nt = rows // 8
    sub = sublane()
    gram = gin_ref[...]
    where = lax.broadcasted_iota(jnp.int32, (pairs, 128), 0)
    inside = (where >= 4) & (where < pairs - 4)

    def splat(row):
        return jnp.full((8, 128), row, jnp.int32)

    for e_ref, h_ref, out_ref, near, halo, par, sign in ((en_ref, n_ref, an_ref, 0, -1, 0, 1),
                                                         (es_ref, s_ref, as_ref, rows - 1, rows, 1, -1)):
        c0, k0, _ = scaled_coefs(splat(first + near), nlat)
        c1, k1, _ = scaled_coefs(splat(first + halo), nlat)
        _, _, wa = scaled_coefs(splat(first + near) + (sub % 2 - par), nlat)
        many = pairs // 8
        c = jnp.concatenate([c0 + c1] * many, axis=0)
        k = jnp.concatenate([k0 + k1] * many, axis=0)
        w = jnp.concatenate([0.04 * wa] * many, axis=0)
        outermost = where % 2 == par
        for f in range(fields):
            h = h_ref[f].astype(F32)
            pad_ref[8:8 + pairs] = h
            nearer = pad_ref[8 + sign:8 + sign + pairs]
            wide = pad_ref[8 + sign - 2:8 + sign - 2 + pairs] + pad_ref[8 + sign + 2:8 + sign + 2 + pairs]
            more = h + jnp.where(outermost, c * nearer + k * wide, 0.0)
            made = jnp.where(inside, e_ref[f, 2:2 + pairs] + w * more, 0.0).astype(BF16)
            out_ref[f] = made
            gram = gram + gram_of(made)

    coefs = [scaled_coefs(first + 8 * t + sub, nlat) for t in range(nt)]
    beyond = first + rows + jnp.where(sub < 4, sub, sub - 8 - rows)
    c, k, _ = scaled_coefs(beyond, nlat)
    real = (beyond >= 0) & (beyond < nlat)
    vc = [x[0] for x in coefs] + [jnp.where(real, c, 0.0)]
    vk = [x[1] for x in coefs] + [jnp.where(real, k, 0.0)]
    one = jnp.where(real, 1.0, 0.0)
    for f in range(fields):
        bg = bg_ref[f].astype(F32)
        for side in range(2):
            u = [tiles_of(x_ref[f, 6 * side + l]) for l in range(6)]
            v = []
            for l in range(1, 5):
                ns = neighbours(u[l], pltpu.roll(u[l][nt], 1, 0), pltpu.roll(u[l][0], 7, 0))
                ns[nt] = one * ns[nt]
                v.append([ns[t] + vc[t] * u[l][t] + vk[t] * (u[l - 1][t] + u[l + 1][t]) for t in range(nt + 1)])
            for l in range(2):
                ns = neighbours(v[l + 1], pltpu.roll(v[l + 1][nt], 1, 0), pltpu.roll(v[l + 1][0], 7, 0))
                at = l + side * (cols - 2)
                parts = []
                for t in range(nt):
                    y = ns[t] + vc[t] * v[l + 1][t] + vk[t] * (v[l][t] + v[l + 2][t])
                    b = jnp.broadcast_to(bg[8 * t:8 * t + 8, at:at + 1], TILE)
                    parts.append((0.04 * y - b) * coefs[t][2])
                ac_ref[f, 2 * side + l] = jnp.concatenate(parts, axis=0).astype(BF16)
    gram = gram + gram_of(ac_ref[...].reshape(-1, 128))
    g_ref[...] = pack(gram)


def factor(g):
    n = 128
    lane = lax.broadcasted_iota(jnp.int32, (8, n), 1)
    sub = lax.broadcasted_iota(jnp.int32, (8, n), 0)
    w = list(g)
    tiles = len(w)
    for b0 in range(tiles):
        cols = [[jnp.broadcast_to(w[b][:, 8 * b0 + j:8 * b0 + j + 1], (8, n)) for b in range(b0, tiles)]
                for j in range(8)]
        for s in range(8):
            k = 8 * b0 + s
            inverse = 1.0 / jnp.broadcast_to(cols[s][0][s:s + 1], (8, n))
            pivot_row = jnp.where(lane == k, 1.0, jnp.broadcast_to(w[b0][s:s + 1], (8, n)))
            rows = [jnp.broadcast_to(cols[j][0][s:s + 1], (8, n)) for j in range(s + 1, 8)]
            for b in range(b0, tiles):
                i = b - b0
                f = cols[s][i] * inverse
                if i == 0:
                    if s == 7:
                        continue
                    f = jnp.where(sub > s, f, 0.0)
                    kept = jnp.where((lane == k) & (sub > s), 0.0, w[b])
                else:
                    kept = jnp.where(lane == k, 0.0, w[b])
                w[b] = kept - f * pivot_row
                for j in range(s + 1, 8):
                    cols[j][i] = cols[j][i] - f * rows[j - s - 1]
    r, x = [], []
    for b in range(tiles):
        diag = lane == sub + 8 * b
        scale = lax.rsqrt(jnp.sum(jnp.where(diag, w[b], 0.0), axis=1, keepdims=True))
        r.append(jnp.where(lane >= sub + 8 * b, w[b] * scale, 0.0))
        x.append(jnp.where(diag, scale, jnp.where(lane < sub + 8 * b, w[b] * scale, 0.0)))
    return jnp.concatenate(r, axis=0), jnp.concatenate(x, axis=0)


def modes_kernel(p_ref, an_ref, as_ref, ac_hbm, a_hbm, out_ref, r_ref, a_ref, x_ref, sems, *, total):
    step = pl.program_id(0)
    lons, rows = out_ref.shape[1], out_ref.shape[2]
    fields, cols = a_ref.shape[0], a_ref.shape[1]
    per = cols // lons

    @pl.when(step == 0)
    def _():
        copy = pltpu.make_async_copy(a_hbm, a_ref, sems.at[0])
        copy.start()
        g = unpack(p_ref[...]) * (1.0 / total)
        r, x = factor(tiles_of(g))
        r_ref[...] = r
        inv = x.T
        high = inv.astype(BF16)
        x_ref[0] = high
        x_ref[1] = (inv - high.astype(F32)).astype(BF16)
        copy.wait()
        sides = [pltpu.make_async_copy(ac_hbm.at[:, pl.ds(2 * s, 2)], a_ref.at[:, pl.ds(s * (cols - 2), 2)],
                                       sems.at[1 + s]) for s in range(2)]
        for side in sides:
            side.start()
        for side in sides:
            side.wait()

    def times(a):
        return jnp.dot(a, x_ref[0], preferred_element_type=F32) + jnp.dot(a, x_ref[1], preferred_element_type=F32)

    f, part = lax.div(step, per), lax.rem(step, per)
    a = a_ref[f, pl.ds(part * lons, lons)].reshape(-1, 128)
    out_ref[0] = times(a).reshape(lons, rows, 128)
    north, south = times(an_ref[0]), times(as_ref[0])
    for l in range(lons):
        def put(l=l):
            out_ref[0, l, 0:2] = north[2 * l:2 * l + 2]
            out_ref[0, l, rows - 2:rows] = south[2 * l:2 * l + 2]
        if l < 2:
            pl.when(part > 0)(put)
        elif l >= lons - 2:
            pl.when(part < per - 1)(put)
        else:
            put()


def shifts(count, wrap):
    ahead = [(i, (i + 1) % count) for i in range(count if wrap else count - 1)]
    return ahead, [(j, i) for i, j in ahead]


def halos(m):
    fields, cols, rows, width = m.shape
    down, up = shifts(lax.axis_size("lat"), False)
    east, west = shifts(lax.axis_size("lon"), True)
    north = lax.ppermute(m[:, :, rows - 2:].reshape(fields, 2 * cols, width), "lat", down)
    south = lax.ppermute(m[:, :, :2].reshape(fields, 2 * cols, width), "lat", up)
    from_west = lax.ppermute(m[:, cols - 2:], "lon", east)
    from_east = lax.ppermute(m[:, :2], "lon", west)
    both = jnp.concatenate([from_west, from_east], axis=1)
    corner_north = lax.ppermute(both[:, :, rows - 2:], "lat", down)
    corner_south = lax.ppermute(both[:, :, :2], "lat", up)
    n4 = north.reshape(fields, cols, 2, width)
    s4 = south.reshape(fields, cols, 2, width)
    zero = jnp.zeros((fields, 12, 4, width), BF16)

    def around(sides, whole):
        return jnp.concatenate([sides[:, :2], whole[:, :4], whole[:, cols - 4:], sides[:, 2:]], axis=1)

    ring = jnp.concatenate([around(both, m), around(corner_south, s4), zero, around(corner_north, n4)], axis=2)
    return north, south, ring.astype(F32)


def total_gram(gram):
    for axis in ("lon", "lat"):
        size, step = lax.axis_size(axis), 1
        while step < size:
            gram = gram + lax.ppermute(gram, axis, [(i, i ^ step) for i in range(size)])
            step *= 2
    return gram


def whole(*shape):
    return pl.BlockSpec(shape, lambda *_: (0,) * len(shape))


def local(members, background):
    fields, rows, cols, width = members.shape
    lat, lon = lax.axis_size("lat"), lax.axis_size("lon")
    nlat = rows * lat
    group = 12
    per = 4
    lons = cols // per
    first = (lax.axis_index("lat") * rows).astype(jnp.int32).reshape(1)
    m = jnp.transpose(members, (0, 2, 1, 3))
    north, south, ring = halos(m)
    smem = pl.BlockSpec(memory_space=pltpu.SMEM)
    params = pltpu.CompilerParams(vmem_limit_bytes=VMEM_LIMIT)
    pairs = 2 * cols
    a, en, es, gram = pl.pallas_call(
        functools.partial(inner_kernel, nlat=nlat, group=group),
        grid=(fields,),
        out_shape=(jax.ShapeDtypeStruct((fields, cols, rows, width), BF16),
                   jax.ShapeDtypeStruct((fields, pairs + 8, width), F32),
                   jax.ShapeDtypeStruct((fields, pairs + 8, width), F32),
                   jax.ShapeDtypeStruct((width, width), F32)),
        in_specs=[smem,
                  pl.BlockSpec((1, cols, rows, width), lambda f: (f, 0, 0, 0)),
                  pl.BlockSpec((1, rows, cols), lambda f: (f, 0, 0))],
        out_specs=(pl.BlockSpec((1, cols, rows, width), lambda f: (f, 0, 0, 0)),
                   pl.BlockSpec((1, pairs + 8, width), lambda f: (f, 0, 0)),
                   pl.BlockSpec((1, pairs + 8, width), lambda f: (f, 0, 0)),
                   whole(width, width)),
        scratch_shapes=[pltpu.VMEM((6, rows // 8, 8, 128), F32), pltpu.VMEM((rows, -(-cols // 128) * 128), F32)],
        compiler_params=params,
        cost_estimate=pl.CostEstimate(flops=2 * fields * cols * rows * width * width,
                                      bytes_accessed=5 * fields * cols * rows * width, transcendentals=0),
    )(first, m, background)
    an, as_, ac, packed = pl.pallas_call(
        functools.partial(outer_kernel, nlat=nlat),
        grid=(1,),
        out_shape=(jax.ShapeDtypeStruct((fields, pairs, width), BF16),
                   jax.ShapeDtypeStruct((fields, pairs, width), BF16),
                   jax.ShapeDtypeStruct((fields, 4, rows, width), BF16),
                   jax.ShapeDtypeStruct((80, width), F32)),
        in_specs=[smem, whole(fields, pairs + 8, width), whole(fields, pairs + 8, width),
                  whole(fields, pairs, width), whole(fields, pairs, width),
                  whole(fields, 12, rows + 8, width), whole(fields, rows, cols), whole(width, width)],
        out_specs=(whole(fields, pairs, width), whole(fields, pairs, width),
                   whole(fields, 4, rows, width), whole(80, width)),
        scratch_shapes=[pltpu.VMEM((pairs + 16, width), F32)],
        compiler_params=params,
    )(first, en, es, north, south, ring, background, gram)
    packed = total_gram(packed)
    any_place = pl.BlockSpec(memory_space=pl.ANY)
    split = fields * per
    edge = pl.BlockSpec((1, 2 * lons, width), lambda s: (s, 0, 0))
    modes, r_factor = pl.pallas_call(
        functools.partial(modes_kernel, total=float(fields * nlat * cols * lon)),
        grid=(split,),
        out_shape=(jax.ShapeDtypeStruct((fields, cols, rows, width), F32),
                   jax.ShapeDtypeStruct((width, width), F32)),
        in_specs=[whole(80, width), edge, edge, any_place, any_place],
        out_specs=(pl.BlockSpec((1, lons, rows, width), lambda s: (s // per, s % per, 0, 0)),
                   whole(width, width)),
        scratch_shapes=[pltpu.VMEM((fields, cols, rows, width), BF16), pltpu.VMEM((2, width, width), BF16),
                        pltpu.SemaphoreType.DMA((3,))],
        compiler_params=params,
    )(packed, an.reshape(split, 2 * lons, width), as_.reshape(split, 2 * lons, width), ac, a)
    return jnp.transpose(modes, (0, 2, 1, 3)), r_factor


def solution(mesh):
    return jax.shard_map(
        local,
        mesh=mesh,
        in_specs=(P(None, "lat", "lon", None), P(None, "lat", "lon")),
        out_specs=(P(None, "lat", "lon", None), P()),
        check_vma=False,
    )
```

time: 112 us -> 81.9 us (0.73)
  waiting for transfers between devices: 33.3 us -> 13.5 us
  Pallas kernels: 42.6 us -> 34.2 us
  local copies, waits for them, and re-layouts: 19.6 us -> 11.5 us
  starting transfers between devices: 14.9 us -> 21.3 us
    ppermute x12 -> x11, waiting for transfers between devices: 33.3 us -> 13.5 us  [the longest x5 12.2 us: total_gram(): gram = gram + lax.ppermute(gram, axis, [(i, i ^ step) for i in range(size)])]
    pallas_call x1 -> x2, Pallas kernels: 30.3 us -> 21.3 us  [the longest x1 20 us: local(): pl.pallas_call(functools.partial(inner_kernel, nlat=nlat, group=group), g...]
    pallas_call x1 -> x0, local copies, waits for them, and re-layouts: 8.63 us -> none  [local(): pl.pallas_call(functools.partial(modes_kernel, total=float(fields * nlat...]
    ppermute x12 -> x11, starting transfers between devices: 14.9 us -> 21.3 us  [the longest x5 6.67 us: total_gram(): gram = gram + lax.ppermute(gram, axis, [(i, i ^ step) for i in range(size)])]
    slice x3 -> x8, local copies, waits for them, and re-layouts: 0.14 us -> 3.87 us  [the longest x1 2.02 us: halos(): m[:, :, :2].reshape(fields, 2 * cols, width)]
    unnamed x10 -> x9, local copies, waits for them, and re-layouts: 10.7 us -> 7.38 us
  transfers between devices with their start and end apart: 12 -> 11, of which waited for: 6 -> 6; matrix products, arithmetic and copies ran while one was open for 0% -> 4% of each run, Pallas kernels for 0% -> 25%
where the time goes in v2:
time: 81.9 us; the launch traced here: 81.4 us
  Pallas kernels  34.2 us (42%)
  starting transfers between devices  21.3 us (26%)
  waiting for transfers between devices  13.5 us (16%)
  local copies, waits for them, and re-layouts  11.5 us (14%)
  between operations  0.82 us (1%)
    pallas_call x1, Pallas kernels, local(): pl.pallas_call(functools.partial(inner_kernel, nlat=nlat, group=group), g...  20 us
    pallas_call x1, Pallas kernels, local(): pl.pallas_call(functools.partial(modes_kernel, total=float(fields * nlat...  12.8 us
    ppermute x5, waiting for transfers between devices, total_gram(): gram = gram + lax.ppermute(gram, axis, [(i, i ^ step) for i in range(size)])  12.2 us
    unnamed x9, local copies, waits for them, and re-layouts  7.38 us
    ppermute x5, starting transfers between devices, total_gram(): gram = gram + lax.ppermute(gram, axis, [(i, i ^ step) for i in range(size)])  6.67 us
    ppermute x1, starting transfers between devices, halos(): corner_north = lax.ppermute(both[:, :, rows - 2:], 'lat', down)  5.16 us
    ppermute x1, starting transfers between devices, halos(): lax.ppermute(m[:, :, rows - 2:].reshape(fields, 2 * cols, width), 'lat',...  3.5 us
    ppermute x1, starting transfers between devices, halos(): from_east = lax.ppermute(m[:, :2], 'lon', west)  3.37 us
  transfers between devices with their start and end apart: 11, of which 6 were waited for; matrix products, arithmetic and copies ran while one was open for 4% of the time, Pallas kernels for 25%

profile of v2, /device:TPU:0, one launch (start us, length us, event | category | flops | bytes accessed | tf_op | source)
XLA Modules:
  0.0 81.4 jit_solution(3272941921345080356)
XLA Ops:
  0.6 0.8 %fusion.1 = (bf16[3,2,32,128]{3,2,1,0:T(8,128)(2,1)S(1)}, bf16[3,2,32,128]{3,2,1,0:T(8,128)(2,1)S(1)}) fusion(bf16[3,180,32,128]{3,2,1,0:T(8,128)(2,1)} %bitcast.7), kind=kLoop, calls=%fused_computation.4 | loop fusion | bytes 196608 | tf_op jit(solution)/shard_map/slice | solution.py:286
  1.5 3.4 %collective-permute-start.3 = (bf16[3,2,32,128]{3,2,1,0:T(8,128)(2,1)S(1)}, bf16[3,2,32,128]{3,2,1,0:T(8,128)(2,1)S(1)}, u32[]{:S(2)}, u32[]{:S(2)}) collective-permute-start(bf16[3,2,32,128]{3,2,1,0:T(8,128)(2,1)S(1)} %get-tuple-element.24), channel_id=1, source_target_pairs={{4,0},{8,4},{12,8},{16,12},{20,16},{24,20},{28,24},{0,28},{5,1},{9... | collective-permute-start | bytes 147464 | tf_op jit(solution)/shard_map/ppermute | solution.py:286
  4.8 0.0 collective-permute-start.2
  4.8 2.0 %fusion.2 = (bf16[3,180,2,128]{3,2,1,0:T(2,128)(2,1)S(1)}, bf16[3,180,2,128]{3,2,1,0:T(2,128)(2,1)S(1)}) fusion(bf16[3,180,32,128]{3,2,1,0:T(8,128)(2,1)} %bitcast.8), kind=kLoop, calls=%fused_computation.5 | loop fusion | bytes 1105920 | tf_op jit(solution)/shard_map/slice | solution.py:284
  6.9 3.5 %collective-permute-start = (bf16[3,360,128]{2,1,0:T(8,128)(2,1)S(1)}, bf16[3,360,128]{2,1,0:T(8,128)(2,1)S(1)}, u32[]{:S(2)}, u32[]{:S(2)}) collective-permute-start(bf16[3,360,128]{2,1,0:T(8,128)(2,1)S(1)} %bitcast.14), channel_id=1, source_target_pairs={{0,1},{1,2},{2,3},{4,5},{5,6},{6,7},{8,9},{9,10},{10,11},{12,13},{... | collective-permute-start | bytes 829448 | tf_op jit(solution)/shard_map/ppermute | solution.py:283
  10.4 1.3 %collective-permute-start.1 = (bf16[3,360,128]{2,1,0:T(8,128)(2,1)S(1)}, bf16[3,360,128]{2,1,0:T(8,128)(2,1)S(1)}, u32[]{:S(2)}, u32[]{:S(2)}) collective-permute-start(bf16[3,360,128]{2,1,0:T(8,128)(2,1)S(1)} %bitcast.13), channel_id=1, source_target_pairs={{1,0},{2,1},{3,2},{5,4},{6,5},{7,6},{9,8},{10,9},{11,10},{13,12},{... | collective-permute-start | bytes 829448 | tf_op jit(solution)/shard_map/ppermute | solution.py:284
  11.7 1.0 %fusion = (bf16[3,4,32,128]{3,2,1,0:T(8,128)(2,1)S(1)}, bf16[3,4,32,128]{3,2,1,0:T(8,128)(2,1)S(1)}) fusion(bf16[3,180,32,128]{3,2,1,0:T(8,128)(2,1)} %bitcast.9), kind=kLoop, calls=%fused_computation.3 | loop fusion | bytes 393216 | tf_op jit(solution)/shard_map/slice | solution.py:295
  12.6 0.0 collective-permute-done.2
  12.7 0.0 collective-permute-done.3
  12.7 1.3 %collective-permute-start.4 = (bf16[3,4,2,128]{3,2,1,0:T(2,128)(2,1)S(1)}, bf16[3,4,2,128]{3,2,1,0:T(2,128)(2,1)S(1)}, u32[]{:S(2)}, u32[]{:S(2)}) collective-permute-start(bf16[3,4,2,128]{3,2,1,0:T(2,128)(2,1)S(1)} %get-tuple-element.32), channel_id=1, source_target_pairs={{1,0},{2,1},{3,2},{5,4},{6,5},{7,6},{9,8},{10,9},{11,10},{13,12},{... | collective-permute-start | bytes 18440 | tf_op jit(solution)/shard_map/ppermute | solution.py:289
  14.0 0.0 copy-start
  14.0 2.2 %copy-done = bf16[3,32,180,128]{3,1,2,0:T(8,128)(2,1)S(1)} copy-done((bf16[3,32,180,128]{3,1,2,0:T(8,128)(2,1)S(1)}, bf16[3,32,180,128]{3,1,2,0:T(8,128)(2,1)}, u32[]{:S(2)}) %copy-start) | copy-done | bytes 4423704
  16.3 0.0 copy-start.3
  16.3 0.8 copy-done.3
  17.1 20.0 %shard_map.41 = (bf16[3,180,32,128]{3,2,1,0:T(8,128)(2,1)S(1)}, f32[3,368,128]{2,1,0:T(8,128)S(1)}, f32[3,368,128]{2,1,0:T(8,128)S(1)}, f32[128,128]{1,0:T(8,128)S(1)}) custom-call(s32[1]{0:T(128)} %bitcast.first_ref, bf16[3,180,32,128]{3,2,1,0:T(8,128)(2,1)S(1)} %bitcast.10, bf16[3,32,180]{2,1,0:T(8,128)(2,1)S(1)} %copy-done.3), custom_call_target="tpu_custom_call" | custom-call | flops 566231040 | bytes 11059200 | tf_op jit(solution)/shard_map/pallas_call | solution.py:327
  37.1 0.0 copy-start.1
  37.1 2.1 %copy-done.1 = bf16[3,180,32,128]{3,2,1,0:T(8,128)(2,1)} copy-done((bf16[3,180,32,128]{3,2,1,0:T(8,128)(2,1)}, bf16[3,180,32,128]{3,2,1,0:T(8,128)(2,1)S(1)}, u32[]{:S(2)}) %copy-start.1) | copy-done | bytes 4423704
  39.2 0.1 pad.8.clone
  39.3 5.2 %collective-permute-start.5 = (bf16[3,4,2,128]{3,2,1,0:T(2,128)(2,1)S(1)}, bf16[3,4,2,128]{3,2,1,0:T(2,128)(2,1)S(1)}, u32[]{:S(2)}, u32[]{:S(2)}) collective-permute-start(bf16[3,4,2,128]{3,2,1,0:T(2,128)(2,1)S(1)} %get-tuple-element.33), channel_id=1, source_target_pairs={{0,1},{1,2},{2,3},{4,5},{5,6},{6,7},{8,9},{9,10},{10,11},{12,13},{... | collective-permute-start | bytes 18440 | tf_op jit(solution)/shard_map/ppermute | solution.py:288
  44.5 0.0 collective-permute-done.4
  44.5 1.3 %collective-permute-done.5 = bf16[3,4,2,128]{3,2,1,0:T(2,128)(2,1)S(1)} collective-permute-done((bf16[3,4,2,128]{3,2,1,0:T(2,128)(2,1)S(1)}, bf16[3,4,2,128]{3,2,1,0:T(2,128)(2,1)S(1)}, u32[]{:S(2)}, u32[]{:S(2)}) %collective-permute-start.5) | collective-permute-done | bytes 6176 | tf_op jit(solution)/shard_map/ppermute | solution.py:288
  45.8 0.0 collective-permute-done.n_ref
  45.8 0.0 collective-permute-done.1.s_ref
  45.9 0.1 maximum_convert_fusion.x_ref
  46.0 1.3 %shard_map.42 = (bf16[3,360,128]{2,1,0:T(8,128)(2,1)S(1)}, bf16[3,360,128]{2,1,0:T(8,128)(2,1)S(1)}, bf16[3,4,32,128]{3,2,1,0:T(8,128)(2,1)S(1)}, f32[80,128]{1,0:T(8,128)S(1)}) custom-call(s32[1]{0:T(128)} %bitcast.first_ref, f32[3,368,128]{2,1,0:T(8,128)S(1)} %get-tuple-element.12.en_ref, f32[3,368,128]{2,1,0:T(8,128)S(1)} %get-tuple-element.13.es_ref, ...), custom_call_target="tpu_custom_call" | custom-call | tf_op jit(solution)/shard_map/pallas_call | solution.py:346
  47.3 0.1 collective-permute-start.6
  47.4 1.2 %collective-permute-done.6 = f32[80,128]{1,0:T(8,128)S(1)} collective-permute-done((f32[80,128]{1,0:T(8,128)S(1)}, f32[80,128]{1,0:T(8,128)S(1)}, u32[]{:S(2)}, u32[]{:S(2)}) %collective-permute-start.6) | collective-permute-done | bytes 40992 | tf_op jit(solution)/shard_map/ppermute | solution.py:305
  48.6 0.3 collective-permute-start.7
  48.9 3.7 %collective-permute-done.7 = f32[80,128]{1,0:T(8,128)S(1)} collective-permute-done((f32[80,128]{1,0:T(8,128)S(1)}, f32[80,128]{1,0:T(8,128)S(1)}, u32[]{:S(2)}, u32[]{:S(2)}) %collective-permute-start.7) | collective-permute-done | bytes 40992 | tf_op jit(solution)/shard_map/ppermute | solution.py:305
  52.6 0.5 collective-permute-start.8
  53.1 3.5 %collective-permute-done.8 = f32[80,128]{1,0:T(8,128)S(1)} collective-permute-done((f32[80,128]{1,0:T(8,128)S(1)}, f32[80,128]{1,0:T(8,128)S(1)}, u32[]{:S(2)}, u32[]{:S(2)}) %collective-permute-start.8) | collective-permute-done | bytes 40992 | tf_op jit(solution)/shard_map/ppermute | solution.py:305
  56.6 2.3 %collective-permute-start.9 = (f32[80,128]{1,0:T(8,128)S(1)}, f32[80,128]{1,0:T(8,128)S(1)}, u32[]{:S(2)}, u32[]{:S(2)}) collective-permute-start(f32[80,128]{1,0:T(8,128)S(1)} %add.17), channel_id=1, source_target_pairs={{0,1},{1,0},{2,3},{3,2},{4,5},{5,4},{6,7},{7,6},{8,9},{9,8},{10,11... | collective-permute-start | bytes 122888 | tf_op jit(solution)/shard_map/ppermute | solution.py:305
  58.9 2.0 %collective-permute-done.9 = f32[80,128]{1,0:T(8,128)S(1)} collective-permute-done((f32[80,128]{1,0:T(8,128)S(1)}, f32[80,128]{1,0:T(8,128)S(1)}, u32[]{:S(2)}, u32[]{:S(2)}) %collective-permute-start.9) | collective-permute-done | bytes 40992 | tf_op jit(solution)/shard_map/ppermute | solution.py:305
  60.9 3.5 %collective-permute-start.10 = (f32[80,128]{1,0:T(8,128)S(1)}, f32[80,128]{1,0:T(8,128)S(1)}, u32[]{:S(2)}, u32[]{:S(2)}) collective-permute-start(f32[80,128]{1,0:T(8,128)S(1)} %add.18), channel_id=1, source_target_pairs={{0,2},{1,3},{2,0},{3,1},{4,6},{5,7},{6,4},{7,5},{8,10},{9,11},{10,... | collective-permute-start | bytes 122888 | tf_op jit(solution)/shard_map/ppermute | solution.py:305
  64.4 0.1 reshape.30.an_ref
  64.4 0.1 reshape.31.as_ref
  64.5 1.8 %collective-permute-done.10 = f32[80,128]{1,0:T(8,128)S(1)} collective-permute-done((f32[80,128]{1,0:T(8,128)S(1)}, f32[80,128]{1,0:T(8,128)S(1)}, u32[]{:S(2)}, u32[]{:S(2)}) %collective-permute-start.10) | collective-permute-done | bytes 40992 | tf_op jit(solution)/shard_map/ppermute | solution.py:305
  66.3 0.0 copy-start.2
  66.3 2.2 %copy-done.2 = bf16[3,180,32,128]{3,2,1,0:T(8,128)(2,1)S(1)} copy-done((bf16[3,180,32,128]{3,2,1,0:T(8,128)(2,1)S(1)}, bf16[3,180,32,128]{3,2,1,0:T(8,128)(2,1)}, u32[]{:S(2)}) %copy-start.2) | copy-done | bytes 4423704
  68.6 12.8 %shard_map.43 = (f32[3,180,32,128]{3,2,1,0:T(8,128)}, f32[128,128]{1,0:T(8,128)}) custom-call(f32[80,128]{1,0:T(8,128)S(1)} %add.19.p_ref, bf16[12,90,128]{2,1,0:T(8,128)(2,1)S(1)} %reshape.30.an_ref, bf16[12,90,128]{2,1,0:T(8,128)(2,1)S(1)} %reshape.31.as_ref, bf16[3,4,32,128]{3,2,1,0:T(8,128)(2,1)S(1)} %get-tuple-element.18.ac_hbm, ...), custom_call_target="tpu_custom_call" | custom-call | tf_op jit(solution)/shard_map/pallas_call | solution.py:365
  (13 shorter events, 0.1 us)
Async XLA Ops:
  1.5 11.2 %collective-permute-start.3 = (bf16[3,2,32,128]{3,2,1,0:T(8,128)(2,1)S(1)}, bf16[3,2,32,128]{3,2,1,0:T(8,128)(2,1)S(1)}, u32[]{:S(2)}, u32[]{:S(2)}) collective-permute-start(bf16[3,2,32,128]{3,2,1,0:T(8,128)(2,1)S(1)} %get-tuple-element.24), channel_id=1, source_target_pairs={{4,0},{8,4},{12,8},{16,12},{20,16},{24,20},{28,24},{0,28},{5,1},{9... | collective-permute-start | bytes 147464 | tf_op jit(solution)/shard_map/ppermute | solution.py:286
  4.8 7.8 %collective-permute-start.2 = (bf16[3,2,32,128]{3,2,1,0:T(8,128)(2,1)S(1)}, bf16[3,2,32,128]{3,2,1,0:T(8,128)(2,1)S(1)}, u32[]{:S(2)}, u32[]{:S(2)}) collective-permute-start(bf16[3,2,32,128]{3,2,1,0:T(8,128)(2,1)S(1)} %get-tuple-element.25), channel_id=1, source_target_pairs={{0,4},{4,8},{8,12},{12,16},{16,20},{20,24},{24,28},{28,0},{1,5},{5... | collective-permute-start | bytes 147464 | tf_op jit(solution)/shard_map/ppermute | solution.py:285
  6.9 38.9 %collective-permute-start = (bf16[3,360,128]{2,1,0:T(8,128)(2,1)S(1)}, bf16[3,360,128]{2,1,0:T(8,128)(2,1)S(1)}, u32[]{:S(2)}, u32[]{:S(2)}) collective-permute-start(bf16[3,360,128]{2,1,0:T(8,128)(2,1)S(1)} %bitcast.14), channel_id=1, source_target_pairs={{0,1},{1,2},{2,3},{4,5},{5,6},{6,7},{8,9},{9,10},{10,11},{12,13},{... | collective-permute-start | bytes 829448 | tf_op jit(solution)/shard_map/ppermute | solution.py:283
  10.4 35.5 %collective-permute-start.1 = (bf16[3,360,128]{2,1,0:T(8,128)(2,1)S(1)}, bf16[3,360,128]{2,1,0:T(8,128)(2,1)S(1)}, u32[]{:S(2)}, u32[]{:S(2)}) collective-permute-start(bf16[3,360,128]{2,1,0:T(8,128)(2,1)S(1)} %bitcast.13), channel_id=1, source_target_pairs={{1,0},{2,1},{3,2},{5,4},{6,5},{7,6},{9,8},{10,9},{11,10},{13,12},{... | collective-permute-start | bytes 829448 | tf_op jit(solution)/shard_map/ppermute | solution.py:284
  12.7 31.8 %collective-permute-start.4 = (bf16[3,4,2,128]{3,2,1,0:T(2,128)(2,1)S(1)}, bf16[3,4,2,128]{3,2,1,0:T(2,128)(2,1)S(1)}, u32[]{:S(2)}, u32[]{:S(2)}) collective-permute-start(bf16[3,4,2,128]{3,2,1,0:T(2,128)(2,1)S(1)} %get-tuple-element.32), channel_id=1, source_target_pairs={{1,0},{2,1},{3,2},{5,4},{6,5},{7,6},{9,8},{10,9},{11,10},{13,12},{... | collective-permute-start | bytes 18440 | tf_op jit(solution)/shard_map/ppermute | solution.py:289
  14.0 2.3 %copy-start = (bf16[3,32,180,128]{3,1,2,0:T(8,128)(2,1)S(1)}, bf16[3,32,180,128]{3,1,2,0:T(8,128)(2,1)}, u32[]{:S(2)}) copy-start(bf16[3,32,180,128]{3,1,2,0:T(8,128)(2,1)} %param.2) | copy-start | bytes 13271044
  16.3 0.8 copy-start.3
  37.1 2.1 %copy-start.1 = (bf16[3,180,32,128]{3,2,1,0:T(8,128)(2,1)}, bf16[3,180,32,128]{3,2,1,0:T(8,128)(2,1)S(1)}, u32[]{:S(2)}) copy-start(bf16[3,180,32,128]{3,2,1,0:T(8,128)(2,1)S(1)} %get-tuple-element.19.a_hbm) | copy-start | bytes 13271044
  39.3 6.5 %collective-permute-start.5 = (bf16[3,4,2,128]{3,2,1,0:T(2,128)(2,1)S(1)}, bf16[3,4,2,128]{3,2,1,0:T(2,128)(2,1)S(1)}, u32[]{:S(2)}, u32[]{:S(2)}) collective-permute-start(bf16[3,4,2,128]{3,2,1,0:T(2,128)(2,1)S(1)} %get-tuple-element.33), channel_id=1, source_target_pairs={{0,1},{1,2},{2,3},{4,5},{5,6},{6,7},{8,9},{9,10},{10,11},{12,13},{... | collective-permute-start | bytes 18440 | tf_op jit(solution)/shard_map/ppermute | solution.py:288
  47.3 1.3 %collective-permute-start.6 = (f32[80,128]{1,0:T(8,128)S(1)}, f32[80,128]{1,0:T(8,128)S(1)}, u32[]{:S(2)}, u32[]{:S(2)}) collective-permute-start(f32[80,128]{1,0:T(8,128)S(1)} %get-tuple-element.15), channel_id=1, source_target_pairs={{0,4},{4,0},{8,12},{12,8},{16,20},{20,16},{24,28},{28,24},{1,5},{5... | collective-permute-start | bytes 122888 | tf_op jit(solution)/shard_map/ppermute | solution.py:305
  48.6 4.0 %collective-permute-start.7 = (f32[80,128]{1,0:T(8,128)S(1)}, f32[80,128]{1,0:T(8,128)S(1)}, u32[]{:S(2)}, u32[]{:S(2)}) collective-permute-start(f32[80,128]{1,0:T(8,128)S(1)} %add.15), channel_id=1, source_target_pairs={{0,8},{4,12},{8,0},{12,4},{16,24},{20,28},{24,16},{28,20},{1,9},{5... | collective-permute-start | bytes 122888 | tf_op jit(solution)/shard_map/ppermute | solution.py:305
  52.6 4.0 %collective-permute-start.8 = (f32[80,128]{1,0:T(8,128)S(1)}, f32[80,128]{1,0:T(8,128)S(1)}, u32[]{:S(2)}, u32[]{:S(2)}) collective-permute-start(f32[80,128]{1,0:T(8,128)S(1)} %add.16), channel_id=1, source_target_pairs={{0,16},{4,20},{8,24},{12,28},{16,0},{20,4},{24,8},{28,12},{1,17},{... | collective-permute-start | bytes 122888 | tf_op jit(solution)/shard_map/ppermute | solution.py:305
  56.6 4.3 %collective-permute-start.9 = (f32[80,128]{1,0:T(8,128)S(1)}, f32[80,128]{1,0:T(8,128)S(1)}, u32[]{:S(2)}, u32[]{:S(2)}) collective-permute-start(f32[80,128]{1,0:T(8,128)S(1)} %add.17), channel_id=1, source_target_pairs={{0,1},{1,0},{2,3},{3,2},{4,5},{5,4},{6,7},{7,6},{8,9},{9,8},{10,11... | collective-permute-start | bytes 122888 | tf_op jit(solution)/shard_map/ppermute | solution.py:305
  60.9 5.5 %collective-permute-start.10 = (f32[80,128]{1,0:T(8,128)S(1)}, f32[80,128]{1,0:T(8,128)S(1)}, u32[]{:S(2)}, u32[]{:S(2)}) collective-permute-start(f32[80,128]{1,0:T(8,128)S(1)} %add.18), channel_id=1, source_target_pairs={{0,2},{1,3},{2,0},{3,1},{4,6},{5,7},{6,4},{7,5},{8,10},{9,11},{10,... | collective-permute-start | bytes 122888 | tf_op jit(solution)/shard_map/ppermute | solution.py:305
  66.3 2.3 %copy-start.2 = (bf16[3,180,32,128]{3,2,1,0:T(8,128)(2,1)S(1)}, bf16[3,180,32,128]{3,2,1,0:T(8,128)(2,1)}, u32[]{:S(2)}) copy-start(bf16[3,180,32,128]{3,2,1,0:T(8,128)(2,1)} %copy-done.1) | copy-start | bytes 13271044

commit v3 on v2

v3 whole, which is shorter than its diff:
```python
import functools
import math

import jax
import jax.numpy as jnp
from jax import lax
from jax.experimental import pallas as pl
from jax.experimental.pallas import tpu as pltpu
from jax.sharding import PartitionSpec as P

VMEM_LIMIT = 32 * 1024 * 1024
F32 = jnp.float32
BF16 = jnp.bfloat16
TILE = (8, 128)


def row_coefs(glob, nlat):
    phi = (0.125 * (glob.astype(F32) + 0.5) - 0.0625 * nlat) * (math.pi / 180.0)
    cosine = jnp.cos(phi)
    return 0.05 + 0.2 * (1.0 - cosine), jnp.sqrt(cosine)


def scaled_coefs(glob, nlat):
    kx, weight = row_coefs(glob, nlat)
    return 3.0 - 10.0 * kx, 5.0 * kx, weight


def sublane():
    return lax.broadcasted_iota(jnp.int32, TILE, 0)


def tiles_of(x):
    return [x[8 * t:8 * t + 8] for t in range(x.shape[0] // 8)]


def neighbours(x, above, below):
    sub = sublane()
    down = [pltpu.roll(t, 1, 0) for t in x]
    up = [pltpu.roll(t, 7, 0) for t in x]
    out = []
    for i in range(len(x)):
        north = jnp.where(sub == 0, down[i - 1] if i else above, down[i])
        south = jnp.where(sub == 7, up[i + 1] if i + 1 < len(x) else below, up[i])
        out.append(north + south)
    return out


def gram_of(a):
    return lax.dot_general(a, a, (((0,), (0,)), ((), ())), preferred_element_type=F32)


def fetch_kernel(place_ref, m_hbm, m_ref, lon_a_ref, lon_b_ref, lat_a_ref, lat_b_ref, low_ref, high_ref, sems):
    fields, cols, rows, width = m_ref.shape
    lon_even = lax.rem(place_ref[0], 2) == 0
    lat_even = lax.rem(place_ref[1], 2) == 0
    copies = [pltpu.make_async_copy(m_hbm.at[f], m_ref.at[f], sems.at[f]) for f in range(fields)]
    for copy in copies:
        copy.start()
    for f in range(fields):
        copies[f].wait()
        first, last = m_ref[f, 0:2], m_ref[f, cols - 2:cols]
        lon_a_ref[f] = jnp.where(lon_even, last, first)
        lon_b_ref[f] = jnp.where(lon_even, first, last)
        for l in range(cols):
            low_ref[2 * l:2 * l + 2] = m_ref[f, l, 0:16].astype(F32)[0:2]
            high_ref[2 * l:2 * l + 2] = m_ref[f, l, rows - 16:rows].astype(F32)[14:16]
        low, high = low_ref[...], high_ref[...]
        lat_a_ref[f] = jnp.where(lat_even, high, low).astype(BF16)
        lat_b_ref[f] = jnp.where(lat_even, low, high).astype(BF16)


def inner_kernel(place_ref, m_ref, bg_ref, a_ref, en_ref, es_ref, g_ref, mat_ref, coef_ref, entries_ref, *, nlat):
    cols, rows = m_ref.shape[1], m_ref.shape[2]
    wide = 2
    nt = rows // 8
    first = place_ref[1] * rows

    sub = sublane()
    lane = lax.broadcasted_iota(jnp.int32, TILE, 1)
    for t in range(nt):
        row = 8 * t + sub
        glob = first + row
        c, k, w = scaled_coefs(glob, nlat)
        cn, kn, _ = scaled_coefs(glob - 1, nlat)
        cs, ks, _ = scaled_coefs(glob + 1, nlat)
        live = (row >= 2) & (row < rows - 2)
        coef_ref[0, t], coef_ref[1, t] = 0.04 * w, w
        coef_ref[2, t], coef_ref[3, t] = jnp.where(live, 0.04 * w, 0.0), jnp.where(live, w, 0.0)
        both = jnp.where((glob == 0) | (glob == nlat - 1), 1.0, 2.0)
        dj = lax.rem(lane, rows) - row
        for i in range(4):
            for half in range(2):
                dl = jnp.abs(4 * half + lax.div(lane, rows) - i - 2)
                by_lon = lambda zero, one, two: jnp.where(
                    dl == 0, zero, jnp.where(dl == 1, one, jnp.where(dl == 2, two, 0.0)))
                entry = jnp.where(
                    dj == 0, by_lon(both + c * c + 2.0 * k * k, 2.0 * c * k, k * k), jnp.where(
                        dj == -1, by_lon(c + cn, k + kn, 0.0), jnp.where(
                            dj == 1, by_lon(c + cs, k + ks, 0.0), jnp.where(
                                (jnp.abs(dj) == 2) & (dl == 0), 1.0, 0.0))))
                high = entry.astype(BF16).astype(F32)
                at = pl.ds(rows * i + 8 * t, 8), pl.ds(128 * half, 128)
                entries_ref[at[0], at[1]] = high
                entries_ref[pl.ds(128 + rows * i + 8 * t, 8), at[1]] = entry - high
    mat_ref[...] = entries_ref[...].astype(BF16)

    def field(f, gram):
        ground = bg_ref[f].astype(F32)
        for l in (0, 1, cols - 2, cols - 1):
            a_ref[f, l] = jnp.zeros((rows, 128), BF16)
        for l0 in range(2, cols - 2, 4 * wide):
            chunk = [m_ref[f, l - 2:l + 6].reshape(256, 128) for l in range(l0, min(l0 + 4 * wide, cols - 2), 4)]
            y = jnp.dot(mat_ref[...], jnp.concatenate(chunk, axis=1), preferred_element_type=F32)
            y = y[:128] + y[128:]
            for q in range(len(chunk)):
                made = []
                for i in range(4):
                    l = l0 + 4 * q + i
                    for t in range(nt):
                        yt = y[rows * i + 8 * t:rows * i + 8 * t + 8, 128 * q:128 * q + 128]
                        b = jnp.broadcast_to(ground[8 * t:8 * t + 8, l:l + 1], TILE)
                        made.append(yt * coef_ref[2, t] - b * coef_ref[3, t])
                        if t == 0:
                            en_ref[f, 2 * l:2 * l + 2] = (yt * coef_ref[0, t] - b * coef_ref[1, t])[0:2]
                        if t == nt - 1:
                            es_ref[f, 2 * l:2 * l + 2] = (yt * coef_ref[0, t] - b * coef_ref[1, t])[6:8]
                made = jnp.concatenate(made, axis=0).astype(BF16)
                l = l0 + 4 * q
                a_ref[f, l:l + 4] = made.reshape(4, rows, 128)
        return gram + gram_of(a_ref[f].reshape(-1, 128))

    g_ref[...] = lax.fori_loop(0, m_ref.shape[0], field, jnp.zeros((128, 128), F32))


def pack(g):
    lane = lax.broadcasted_iota(jnp.int32, (32, 128), 1)
    middle = jnp.where(lane < 32, pltpu.roll(g[96:128], 32, 1), g[32:64])
    last = jnp.where(lane[:16] < 64, pltpu.roll(g[80:96], 64, 1), g[64:80])
    return jnp.concatenate([g[0:32], middle, last], axis=0)


def unpack(p):
    upper = jnp.concatenate([p[0:80], pltpu.roll(p[64:80], 64, 1), pltpu.roll(p[32:64], 96, 1)], axis=0)
    row = lax.broadcasted_iota(jnp.int32, (128, 128), 0)
    col = lax.broadcasted_iota(jnp.int32, (128, 128), 1)
    return jnp.where(col >= row, upper, upper.T)


def outer_kernel(place_ref, en_ref, es_ref, m_ref, lon_a_ref, lon_b_ref, lat_a_ref, lat_b_ref, corner_a_ref,
                 corner_b_ref, bg_ref, gin_ref, an_ref, as_ref, ac_ref, g_ref, pad_ref, x_ref, *, nlat):
    fields, pairs = lat_a_ref.shape[0], lat_a_ref.shape[1]
    rows, cols = bg_ref.shape[1], bg_ref.shape[2]
    first = place_ref[1] * rows
    lon_even = lax.rem(place_ref[0], 2) == 0
    lat_even = lax.rem(place_ref[1], 2) == 0
    has_north, has_south = first > 0, first + rows < nlat
    nt = rows // 8
    sub = sublane()
    gram = gin_ref[...]
    where = lax.broadcasted_iota(jnp.int32, (pairs, 128), 0)
    inside = (where >= 4) & (where < pairs - 4)

    def splat(row):
        return jnp.full((8, 128), row, jnp.int32)

    for e_ref, a_h_ref, b_h_ref, a_c_ref, b_c_ref, use_b, exists, out_ref, near, halo, par, sign, at in (
            (en_ref, lat_a_ref, lat_b_ref, corner_a_ref, corner_b_ref, lat_even, has_north, an_ref, 0, -1, 0, 1, rows + 6),
            (es_ref, lat_b_ref, lat_a_ref, corner_b_ref, corner_a_ref, lat_even, has_south, as_ref, rows - 1, rows, 1, -1,
             rows)):
        c0, k0, _ = scaled_coefs(splat(first + near), nlat)
        c1, k1, _ = scaled_coefs(splat(first + halo), nlat)
        _, _, wa = scaled_coefs(splat(first + near) + (sub % 2 - par), nlat)
        many = pairs // 8
        c = jnp.concatenate([c0 + c1] * many, axis=0)
        k = jnp.concatenate([k0 + k1] * many, axis=0)
        w = jnp.concatenate([0.04 * wa] * many, axis=0)
        outermost = where % 2 == par
        for f in range(fields):
            h = jnp.where(use_b, b_h_ref[f].astype(F32), a_h_ref[f].astype(F32))
            h = jnp.where(exists, h, 0.0)
            pad_ref[8:8 + pairs] = h
            nearer = pad_ref[8 + sign:8 + sign + pairs]
            wide = pad_ref[8 + sign - 2:8 + sign - 2 + pairs] + pad_ref[8 + sign + 2:8 + sign + 2 + pairs]
            more = h + jnp.where(outermost, c * nearer + k * wide, 0.0)
            made = jnp.where(inside, e_ref[f] + w * more, 0.0).astype(BF16)
            out_ref[f] = made
            gram = gram + gram_of(made)
            for l in range(4):
                x_ref[f, 2 + l, at:at + 2] = h[2 * l:2 * l + 2]
                x_ref[f, 6 + l, at:at + 2] = h[pairs - 8 + 2 * l:pairs - 6 + 2 * l]
            corner = jnp.where(use_b, b_c_ref[f].astype(F32), a_c_ref[f].astype(F32))
            corner = jnp.where(exists, corner, 0.0)
            west = jnp.where(lon_even, corner[4:8], corner[0:4])
            east = jnp.where(lon_even, corner[0:4], corner[4:8])
            for l in range(2):
                x_ref[f, l, at:at + 2] = west[2 * l:2 * l + 2]
                x_ref[f, 10 + l, at:at + 2] = east[2 * l:2 * l + 2]
    for f in range(fields):
        for l in range(12):
            x_ref[f, l, rows + 2:rows + 6] = jnp.zeros((4, 128), F32)
        for l in range(4):
            x_ref[f, 2 + l, 0:rows] = m_ref[f, l].astype(F32)
            x_ref[f, 6 + l, 0:rows] = m_ref[f, cols - 4 + l].astype(F32)
        for l in range(2):
            a, b = lon_a_ref[f, l].astype(F32), lon_b_ref[f, l].astype(F32)
            x_ref[f, l, 0:rows] = jnp.where(lon_even, b, a)
            x_ref[f, 10 + l, 0:rows] = jnp.where(lon_even, a, b)

    coefs = [scaled_coefs(first + 8 * t + sub, nlat) for t in range(nt)]
    beyond = first + rows + jnp.where(sub < 4, sub, sub - 8 - rows)
    c, k, _ = scaled_coefs(beyond, nlat)
    real = (beyond >= 0) & (beyond < nlat)
    vc = [x[0] for x in coefs] + [jnp.where(real, c, 0.0)]
    vk = [x[1] for x in coefs] + [jnp.where(real, k, 0.0)]
    one = jnp.where(real, 1.0, 0.0)
    for f in range(fields):
        bg = bg_ref[f].astype(F32)
        for side in range(2):
            u = [tiles_of(x_ref[f, 6 * side + l]) for l in range(6)]
            v = []
            for l in range(1, 5):
                ns = neighbours(u[l], pltpu.roll(u[l][nt], 1, 0), pltpu.roll(u[l][0], 7, 0))
                ns[nt] = one * ns[nt]
                v.append([ns[t] + vc[t] * u[l][t] + vk[t] * (u[l - 1][t] + u[l + 1][t]) for t in range(nt + 1)])
            for l in range(2):
                ns = neighbours(v[l + 1], pltpu.roll(v[l + 1][nt], 1, 0), pltpu.roll(v[l + 1][0], 7, 0))
                at = l + side * (cols - 2)
                parts = []
                for t in range(nt):
                    y = ns[t] + vc[t] * v[l + 1][t] + vk[t] * (v[l][t] + v[l + 2][t])
                    b = jnp.broadcast_to(bg[8 * t:8 * t + 8, at:at + 1], TILE)
                    parts.append((0.04 * y - b) * coefs[t][2])
                ac_ref[f, 2 * side + l] = jnp.concatenate(parts, axis=0).astype(BF16)
    gram = gram + gram_of(ac_ref[...].reshape(-1, 128))
    g_ref[...] = pack(gram)


def factor(g):
    n = 128
    lane = lax.broadcasted_iota(jnp.int32, (8, n), 1)
    sub = lax.broadcasted_iota(jnp.int32, (8, n), 0)
    w = list(g)
    tiles = len(w)
    for b0 in range(tiles):
        cols = [[jnp.broadcast_to(w[b][:, 8 * b0 + j:8 * b0 + j + 1], (8, n)) for b in range(b0, tiles)]
                for j in range(8)]
        for s in range(8):
            k = 8 * b0 + s
            inverse = 1.0 / jnp.broadcast_to(cols[s][0][s:s + 1], (8, n))
            pivot_row = jnp.where(lane == k, 1.0, jnp.broadcast_to(w[b0][s:s + 1], (8, n)))
            rows = [jnp.broadcast_to(cols[j][0][s:s + 1], (8, n)) for j in range(s + 1, 8)]
            for b in range(b0, tiles):
                i = b - b0
                f = cols[s][i] * inverse
                if i == 0:
                    if s == 7:
                        continue
                    f = jnp.where(sub > s, f, 0.0)
                    kept = jnp.where((lane == k) & (sub > s), 0.0, w[b])
                else:
                    kept = jnp.where(lane == k, 0.0, w[b])
                w[b] = kept - f * pivot_row
                for j in range(s + 1, 8):
                    cols[j][i] = cols[j][i] - f * rows[j - s - 1]
    r, x = [], []
    for b in range(tiles):
        diag = lane == sub + 8 * b
        scale = lax.rsqrt(jnp.sum(jnp.where(diag, w[b], 0.0), axis=1, keepdims=True))
        r.append(jnp.where(lane >= sub + 8 * b, w[b] * scale, 0.0))
        x.append(jnp.where(diag, scale, jnp.where(lane < sub + 8 * b, w[b] * scale, 0.0)))
    return jnp.concatenate(r, axis=0), jnp.concatenate(x, axis=0)


def modes_kernel(p_ref, an_ref, as_ref, ac_ref, a_ref, out_hbm, r_ref, x_ref, o_ref, sems, *, total, lons):
    fields, cols, rows, width = out_hbm.shape
    per = cols // lons
    g = unpack(p_ref[...]) * (1.0 / total)
    r, x = factor(tiles_of(g))
    r_ref[...] = r
    inv = x.T
    high = inv.astype(BF16)
    x_ref[0:width] = high
    x_ref[width:] = (inv - high.astype(F32)).astype(BF16)

    def times(a):
        return jnp.dot(jnp.concatenate([a, a], axis=1), x_ref[...], preferred_element_type=F32)

    def part_copy(f, q):
        part = pl.ds(q * lons, lons)
        return pltpu.make_async_copy(o_ref.at[f, part], out_hbm.at[f, part], sems.at[f * per + q])

    for f in range(fields):
        for q in range(per):
            at = slice(q * lons, q * lons + lons)
            o_ref[f, at] = times(a_ref[f, at].reshape(-1, width)).reshape(lons, rows, width)
            north = times(an_ref[f, 2 * q * lons:2 * (q + 1) * lons])
            south = times(as_ref[f, 2 * q * lons:2 * (q + 1) * lons])
            for l in range(lons):
                at = q * lons + l
                if at < 2 or at >= cols - 2:
                    o_ref[f, at] = times(ac_ref[f, at if at < 2 else at - cols + 4])
                else:
                    o_ref[f, at, 0:2] = north[2 * l:2 * l + 2]
                    o_ref[f, at, rows - 2:rows] = south[2 * l:2 * l + 2]
            part_copy(f, q).start()
    for f in range(fields):
        for q in range(per):
            part_copy(f, q).wait()


def exchanges(lon, lat):
    def device(k, z):
        return k * lat + z

    lon_a = [(k, k ^ 1) for k in range(lon)]
    lon_b = [(k, (k - 1 if k % 2 == 0 else k + 1) % lon) for k in range(lon)]
    lat_a = [(device(k, z), device(k, z ^ 1)) for k in range(lon) for z in range(lat)]
    lat_b = []
    for k in range(lon):
        for z in range(lat):
            to = z - 1 if z % 2 == 0 else z + 1
            lat_b.append((device(k, z), device(k, to) if 0 <= to < lat else device(k ^ 1, z)))
    return lon_a, lon_b, lat_a, lat_b


def halos(lon_a, lon_b, lat_a, lat_b):
    lon, lat = lax.axis_size("lon"), lax.axis_size("lat")
    by_lon_a, by_lon_b, by_lat_a, by_lat_b = exchanges(lon, lat)
    both = ("lon", "lat")
    fields, _, rows, width = lon_a.shape
    lat_b = lax.ppermute(lat_b, both, by_lat_b)
    lat_a = lax.ppermute(lat_a, both, by_lat_a)
    lon_b = lax.ppermute(lon_b, "lon", by_lon_b)
    lon_a = lax.ppermute(lon_a, "lon", by_lon_a)
    sides = jnp.concatenate([lon_a, lon_b], axis=1)
    low = sides[:, :, :2].reshape(fields, 8, width)
    high = sides[:, :, rows - 2:].reshape(fields, 8, width)
    even = lax.axis_index("lat") % 2 == 0
    corner_b = lax.ppermute(jnp.where(even, low, high), both, by_lat_b)
    corner_a = lax.ppermute(jnp.where(even, high, low), both, by_lat_a)
    return lon_a, lon_b, lat_a, lat_b, corner_a, corner_b


def total_gram(gram):
    lon, lat = lax.axis_size("lon"), lax.axis_size("lat")

    def partner(dk, dz):
        pairs = [(k * lat + z, (k ^ dk) * lat + (z ^ dz)) for k in range(lon) for z in range(lat)]
        return lax.ppermute(gram, ("lon", "lat"), pairs)

    gram = gram + partner(1, 0)
    by_lon = [1 << i for i in range(1, lon.bit_length() - 1)]
    by_lat = [1 << i for i in range(lat.bit_length() - 1)]
    while by_lon or by_lat:
        if by_lon and by_lat:
            dk, dz = by_lon.pop(0), by_lat.pop(0)
            x, z, xz = partner(dk ^ 1, 0), partner(1, dz), partner(dk ^ 1, dz)
            gram = (gram + x) + (z + xz)
        elif by_lon:
            gram = gram + partner(by_lon.pop(0) ^ 1, 0)
        else:
            gram = gram + partner(1, by_lat.pop(0))
    return gram


def local(members, background):
    fields, rows, cols, width = members.shape
    lat, lon = lax.axis_size("lat"), lax.axis_size("lon")
    nlat = rows * lat
    lons = cols // 4
    pairs = 2 * cols
    place = jnp.stack([lax.axis_index("lon"), lax.axis_index("lat")]).astype(jnp.int32)
    smem = pl.BlockSpec(memory_space=pltpu.SMEM)
    vmem = pl.BlockSpec(memory_space=pltpu.VMEM)
    hbm = pl.BlockSpec(memory_space=pl.ANY)
    params = pltpu.CompilerParams(vmem_limit_bytes=VMEM_LIMIT)

    def kept(*xs):
        return [pltpu.with_memory_space_constraint(x, pltpu.VMEM) for x in xs]

    m, *sent = pl.pallas_call(
        fetch_kernel,
        out_shape=(pltpu.VMEM((fields, cols, rows, width), BF16),) + (pltpu.VMEM((fields, 2, rows, width), BF16),) * 2
        + (pltpu.VMEM((fields, pairs, width), BF16),) * 2,
        in_specs=[smem, hbm],
        out_specs=(vmem,) * 5,
        scratch_shapes=[pltpu.VMEM((pairs, width), F32), pltpu.VMEM((pairs, width), F32),
                        pltpu.SemaphoreType.DMA((fields,))],
        compiler_params=params,
    )(place, pltpu.with_memory_space_constraint(jnp.transpose(members, (0, 2, 1, 3)), pltpu.HBM))
    beside = halos(*sent)
    a, en, es, gram = pl.pallas_call(
        functools.partial(inner_kernel, nlat=nlat),
        out_shape=(pltpu.VMEM((fields, cols, rows, width), BF16), pltpu.VMEM((fields, pairs, width), F32),
                   pltpu.VMEM((fields, pairs, width), F32), pltpu.VMEM((width, width), F32)),
        in_specs=[smem, vmem, vmem],
        out_specs=(vmem,) * 4,
        scratch_shapes=[pltpu.VMEM((256, 256), BF16), pltpu.VMEM((4, rows // 8, 8, 128), F32),
                        pltpu.VMEM((256, 256), F32)],
        compiler_params=params,
        cost_estimate=pl.CostEstimate(flops=16 * fields * cols * rows * width * width,
                                      bytes_accessed=8 * fields * cols * rows * width, transcendentals=0),
    )(place, *kept(m), background)
    an, as_, ac, packed = pl.pallas_call(
        functools.partial(outer_kernel, nlat=nlat),
        out_shape=(pltpu.VMEM((fields, pairs, width), BF16), pltpu.VMEM((fields, pairs, width), BF16),
                   pltpu.VMEM((fields, 4, rows, width), BF16), pltpu.VMEM((80, width), F32)),
        in_specs=[smem] + [vmem] * 11,
        out_specs=(vmem,) * 4,
        scratch_shapes=[pltpu.VMEM((pairs + 16, width), F32), pltpu.VMEM((fields, 12, rows + 8, width), F32)],
        compiler_params=params,
    )(place, *kept(en, es, m, *beside, background, gram))
    packed = total_gram(packed)
    modes, r_factor = pl.pallas_call(
        functools.partial(modes_kernel, total=float(fields * nlat * cols * lon), lons=lons),
        out_shape=(jax.ShapeDtypeStruct((fields, cols, rows, width), F32),
                   jax.ShapeDtypeStruct((width, width), F32)),
        in_specs=[vmem] * 5,
        out_specs=(hbm, vmem),
        scratch_shapes=[pltpu.VMEM((2 * width, width), BF16), pltpu.VMEM((fields, cols, rows, width), F32),
                        pltpu.SemaphoreType.DMA((fields * 4,))],
        compiler_params=params,
    )(*kept(packed, an, as_, ac, a))
    return jnp.transpose(modes, (0, 2, 1, 3)), r_factor


def solution(mesh):
    return jax.shard_map(
        local,
        mesh=mesh,
        in_specs=(P(None, "lat", "lon", None), P(None, "lat", "lon")),
        out_specs=(P(None, "lat", "lon", None), P()),
        check_vma=False,
    )
```

time: 81.9 us -> 50 us (0.61)
  Pallas kernels: 34.2 us -> 20 us
  local copies, waits for them, and re-layouts: 11.5 us -> 4.36 us
  waiting for transfers between devices: 13.5 us -> 8.33 us
  starting transfers between devices: 21.3 us -> 16.3 us
    pallas_call x2 -> x3, Pallas kernels: 21.3 us -> 10.6 us  [the longest x1 5.63 us: local(): pl.pallas_call(functools.partial(inner_kernel, nlat=nlat), out_shape=(plt...]
    ppermute x11 -> x13, waiting for transfers between devices: 13.5 us -> 8.33 us  [the longest x7 8.13 us: partner(): return lax.ppermute(gram, ('lon', 'lat'), pairs)]
    ppermute x11 -> x13, starting transfers between devices: 21.3 us -> 16.3 us  [the longest x7 7.69 us: partner(): return lax.ppermute(gram, ('lon', 'lat'), pairs)]
    slice x8 -> x0, local copies, waits for them, and re-layouts: 3.87 us -> none  [the longest x1 2.02 us: halos(): m[:, :, :2].reshape(fields, 2 * cols, width)]
    pallas_call x1, Pallas kernels: 12.8 us -> 9.33 us  [local(): pl.pallas_call(functools.partial(modes_kernel, total=float(fields * nlat...]
    unnamed x9 -> x7, local copies, waits for them, and re-layouts: 7.38 us -> 4.35 us
  transfers between devices with their start and end apart: 11 -> 13, of which waited for: 6 -> 6; matrix products, arithmetic and copies ran while one was open for 4% -> 0% of each run, Pallas kernels for 25% -> 11%
where the time goes in v3:
time: 50 us; the launch traced here: 49.8 us
  Pallas kernels  20 us (40%)
  starting transfers between devices  16.3 us (33%)
  waiting for transfers between devices  8.33 us (17%)
  local copies, waits for them, and re-layouts  4.36 us (9%)
  between operations  0.74 us (1%)
    pallas_call x1, Pallas kernels, local(): pl.pallas_call(functools.partial(modes_kernel, total=float(fields * nlat...  9.33 us
    ppermute x7, waiting for transfers between devices, partner(): return lax.ppermute(gram, ('lon', 'lat'), pairs)  8.13 us
    ppermute x7, starting transfers between devices, partner(): return lax.ppermute(gram, ('lon', 'lat'), pairs)  7.69 us
    pallas_call x1, Pallas kernels, local(): pl.pallas_call(functools.partial(inner_kernel, nlat=nlat), out_shape=(plt...  5.63 us
    unnamed x7, local copies, waits for them, and re-layouts  4.35 us
    ppermute x1, starting transfers between devices, halos(): lon_b = lax.ppermute(lon_b, 'lon', by_lon_b)  3.56 us
    ppermute x1, starting transfers between devices, halos(): corner_a = lax.ppermute(jnp.where(even, high, low), both, by_lat_a)  3.04 us
    pallas_call x1, Pallas kernels, local(): pl.pallas_call(fetch_kernel, out_shape=(pltpu.VMEM((fields, cols, rows, w...  2.97 us
  transfers between devices with their start and end apart: 13, of which 6 were waited for; matrix products, arithmetic and copies ran while one was open for 0% of the time, Pallas kernels for 11%

profile of v3, /device:TPU:0, one launch (start us, length us, event | category | flops | bytes accessed | tf_op | source)
XLA Modules:
  0.0 49.8 jit_solution(4417516609768373638)
XLA Ops:
  0.6 0.0 copy-start.2
  0.6 0.1 pad_add_fusion.place_ref
  0.7 3.0 %shard_map.41 = (bf16[3,180,32,128]{3,2,1,0:T(8,128)(2,1)S(1)}, bf16[3,2,32,128]{3,2,1,0:T(8,128)(2,1)S(1)}, bf16[3,2,32,128]{3,2,1,0:T(8,128)(2,1)S(1)}, bf16[3...) custom-call(s32[2]{0:T(128)S(1)} %pad_add_fusion.place_ref, bf16[3,180,32,128]{3,2,1,0:T(8,128)(2,1)} %bitcast.6), custom_call_target="tpu_custom_call" | custom-call | tf_op jit(solution)/shard_map/pallas_call | solution.py:381
  3.7 0.0 copy-start
  3.7 2.1 %copy-done = bf16[3,180,32,128]{3,2,1,0:T(8,128)(2,1)} copy-done((bf16[3,180,32,128]{3,2,1,0:T(8,128)(2,1)}, bf16[3,180,32,128]{3,2,1,0:T(8,128)(2,1)S(1)}, u32[]{:S(2)}) %copy-start) | copy-done | bytes 4423704
  5.8 0.5 collective-permute-start
  6.2 3.6 %collective-permute-start.1 = (bf16[3,2,32,128]{3,2,1,0:T(8,128)(2,1)S(1)}, bf16[3,2,32,128]{3,2,1,0:T(8,128)(2,1)S(1)}, u32[]{:S(2)}, u32[]{:S(2)}) collective-permute-start(bf16[3,2,32,128]{3,2,1,0:T(8,128)(2,1)S(1)} %get-tuple-element.21), channel_id=1, source_target_pairs={{0,28},{4,8},{8,4},{12,16},{16,12},{20,24},{24,20},{28,0},{1,29},{... | collective-permute-start | bytes 147464 | tf_op jit(solution)/shard_map/ppermute | solution.py:333
  9.8 1.6 %collective-permute-start.2 = (bf16[3,360,128]{2,1,0:T(8,128)(2,1)S(1)}, bf16[3,360,128]{2,1,0:T(8,128)(2,1)S(1)}, u32[]{:S(2)}, u32[]{:S(2)}) collective-permute-start(bf16[3,360,128]{2,1,0:T(8,128)(2,1)S(1)} %get-tuple-element.22), channel_id=1, source_target_pairs={{0,1},{1,0},{2,3},{3,2},{4,5},{5,4},{6,7},{7,6},{8,9},{9,8},{10,11... | collective-permute-start | bytes 829448 | tf_op jit(solution)/shard_map/ppermute | solution.py:332
  11.4 0.0 collective-permute-start.3
  11.4 0.0 collective-permute-done.lon_a_ref
  11.4 0.2 collective-permute-done.1.lon_b_ref
  11.6 3.0 %collective-permute-start.4 = (bf16[3,8,128]{2,1,0:T(8,128)(2,1)S(1)}, bf16[3,8,128]{2,1,0:T(8,128)(2,1)S(1)}, u32[]{:S(2)}, u32[]{:S(2)}) collective-permute-start(bf16[3,8,128]{2,1,0:T(8,128)(2,1)S(1)} %bitcast.8), channel_id=1, source_target_pairs={{0,1},{1,0},{2,3},{3,2},{4,5},{5,4},{6,7},{7,6},{8,9},{9,8},{10,11... | collective-permute-start | bytes 18440 | tf_op jit(solution)/shard_map/ppermute | solution.py:340
  14.7 0.0 collective-permute-start.5
  14.7 0.0 copy-done.2
  14.7 0.0 copy-start.1
  14.7 2.3 %copy-done.1 = bf16[3,180,32,128]{3,2,1,0:T(8,128)(2,1)S(1)} copy-done((bf16[3,180,32,128]{3,2,1,0:T(8,128)(2,1)S(1)}, bf16[3,180,32,128]{3,2,1,0:T(8,128)(2,1)}, u32[]{:S(2)}) %copy-start.1) | copy-done | bytes 4423704
  16.9 5.6 %shard_map.42 = (bf16[3,180,32,128]{3,2,1,0:T(8,128)(2,1)S(1)}, f32[3,360,128]{2,1,0:T(8,128)S(1)}, f32[3,360,128]{2,1,0:T(8,128)S(1)}, f32[128,128]{1,0:T(8,128)S(1)}) custom-call(s32[2]{0:T(128)S(1)} %pad_add_fusion.place_ref, bf16[3,180,32,128]{3,2,1,0:T(8,128)(2,1)S(1)} %copy-done.1, bf16[3,32,180]{2,1,0:T(8,128)(2,1)S(1)} %copy-done.2), custom_call_target="tpu_custom_call" | custom-call | flops 4529848320 | bytes 17694720 | tf_op jit(solution)/shard_map/pallas_call | solution.py:392
  22.6 0.0 collective-permute-done.4.corner_a_ref
  22.6 0.0 collective-permute-done.5.corner_b_ref
  22.6 0.0 collective-permute-done.2.lat_a_ref
  22.6 0.0 collective-permute-done.3.lat_b_ref
  22.6 2.0 %shard_map.43 = (bf16[3,360,128]{2,1,0:T(8,128)(2,1)S(1)}, bf16[3,360,128]{2,1,0:T(8,128)(2,1)S(1)}, bf16[3,4,32,128]{3,2,1,0:T(8,128)(2,1)S(1)}, f32[80,128]{1,0:T(8,128)S(1)}) custom-call(s32[2]{0:T(128)S(1)} %pad_add_fusion.place_ref, f32[3,360,128]{2,1,0:T(8,128)S(1)} %get-tuple-element.18.en_ref, f32[3,360,128]{2,1,0:T(8,128)S(1)} %get-tuple-element.19.es_ref, ...), custom_call_target="tpu_custom_call" | custom-call | tf_op jit(solution)/shard_map/pallas_call | solution.py:404
  24.6 0.6 %collective-permute-start.6 = (f32[80,128]{1,0:T(8,128)S(1)}, f32[80,128]{1,0:T(8,128)S(1)}, u32[]{:S(2)}, u32[]{:S(2)}) collective-permute-start(f32[80,128]{1,0:T(8,128)S(1)} %get-tuple-element.25), channel_id=1, source_target_pairs={{0,4},{1,5},{2,6},{3,7},{4,0},{5,1},{6,2},{7,3},{8,12},{9,13},{10,... | collective-permute-start | bytes 122888 | tf_op jit(solution)/shard_map/ppermute | solution.py:349
  25.2 0.9 %collective-permute-done.6 = f32[80,128]{1,0:T(8,128)S(1)} collective-permute-done((f32[80,128]{1,0:T(8,128)S(1)}, f32[80,128]{1,0:T(8,128)S(1)}, u32[]{:S(2)}, u32[]{:S(2)}) %collective-permute-start.6) | collective-permute-done | bytes 40992 | tf_op jit(solution)/shard_map/ppermute | solution.py:349
  26.1 2.1 %collective-permute-start.9 = (f32[80,128]{1,0:T(8,128)S(1)}, f32[80,128]{1,0:T(8,128)S(1)}, u32[]{:S(2)}, u32[]{:S(2)}) collective-permute-start(f32[80,128]{1,0:T(8,128)S(1)} %add.26), channel_id=1, source_target_pairs={{0,13},{1,12},{2,15},{3,14},{4,9},{5,8},{6,11},{7,10},{8,5},{9,4},... | collective-permute-start | bytes 122888 | tf_op jit(solution)/shard_map/ppermute | solution.py:349
  28.2 0.0 collective-permute-start.8
  28.2 1.0 %collective-permute-start.7 = (f32[80,128]{1,0:T(8,128)S(1)}, f32[80,128]{1,0:T(8,128)S(1)}, u32[]{:S(2)}, u32[]{:S(2)}) collective-permute-start(f32[80,128]{1,0:T(8,128)S(1)} %add.26), channel_id=1, source_target_pairs={{0,12},{1,13},{2,14},{3,15},{4,8},{5,9},{6,10},{7,11},{8,4},{9,5},... | collective-permute-start | bytes 122888 | tf_op jit(solution)/shard_map/ppermute | solution.py:349
  29.3 1.2 %collective-permute-done.9 = f32[80,128]{1,0:T(8,128)S(1)} collective-permute-done((f32[80,128]{1,0:T(8,128)S(1)}, f32[80,128]{1,0:T(8,128)S(1)}, u32[]{:S(2)}, u32[]{:S(2)}) %collective-permute-start.9) | collective-permute-done | bytes 40992 | tf_op jit(solution)/shard_map/ppermute | solution.py:349
  30.4 1.3 %collective-permute-done.8 = f32[80,128]{1,0:T(8,128)S(1)} collective-permute-done((f32[80,128]{1,0:T(8,128)S(1)}, f32[80,128]{1,0:T(8,128)S(1)}, u32[]{:S(2)}, u32[]{:S(2)}) %collective-permute-start.8) | collective-permute-done | bytes 40992 | tf_op jit(solution)/shard_map/ppermute | solution.py:349
  31.8 0.0 collective-permute-done.7
  31.8 2.4 %collective-permute-start.12 = (f32[80,128]{1,0:T(8,128)S(1)}, f32[80,128]{1,0:T(8,128)S(1)}, u32[]{:S(2)}, u32[]{:S(2)}) collective-permute-start(f32[80,128]{1,0:T(8,128)S(1)} %add_add_fusion.1), channel_id=1, source_target_pairs={{0,22},{1,23},{2,20},{3,21},{4,18},{5,19},{6,16},{7,17},{8,30},{9,... | collective-permute-start | bytes 122888 | tf_op jit(solution)/shard_map/ppermute | solution.py:349
  34.2 1.3 %collective-permute-start.11 = (f32[80,128]{1,0:T(8,128)S(1)}, f32[80,128]{1,0:T(8,128)S(1)}, u32[]{:S(2)}, u32[]{:S(2)}) collective-permute-start(f32[80,128]{1,0:T(8,128)S(1)} %add_add_fusion.1), channel_id=1, source_target_pairs={{0,6},{1,7},{2,4},{3,5},{4,2},{5,3},{6,0},{7,1},{8,14},{9,15},{10,... | collective-permute-start | bytes 122888 | tf_op jit(solution)/shard_map/ppermute | solution.py:349
  35.5 0.3 collective-permute-start.10
  35.7 1.4 %collective-permute-done.12 = f32[80,128]{1,0:T(8,128)S(1)} collective-permute-done((f32[80,128]{1,0:T(8,128)S(1)}, f32[80,128]{1,0:T(8,128)S(1)}, u32[]{:S(2)}, u32[]{:S(2)}) %collective-permute-start.12) | collective-permute-done | bytes 40992 | tf_op jit(solution)/shard_map/ppermute | solution.py:349
  37.2 3.3 %collective-permute-done.11 = f32[80,128]{1,0:T(8,128)S(1)} collective-permute-done((f32[80,128]{1,0:T(8,128)S(1)}, f32[80,128]{1,0:T(8,128)S(1)}, u32[]{:S(2)}, u32[]{:S(2)}) %collective-permute-start.11) | collective-permute-done | bytes 40992 | tf_op jit(solution)/shard_map/ppermute | solution.py:349
  40.5 0.0 collective-permute-done.10
  40.5 9.3 %shard_map.44 = (f32[3,180,32,128]{3,2,1,0:T(8,128)}, f32[128,128]{1,0:T(8,128)}) custom-call(f32[80,128]{1,0:T(8,128)S(1)} %add_add_fusion.p_ref, bf16[3,360,128]{2,1,0:T(8,128)(2,1)S(1)} %get-tuple-element.26.an_ref, bf16[3,360,128]{2,1,0:T(8,128)(2,1)S(1)} %get-tuple-element.27.as_ref, bf16[3,4,32,128]{3,2,1,0:T(8,128)(2,1)S(1)} %get-tuple-element.28.ac_ref, ...), custom_call_target="tpu_custom_call" | custom-call | tf_op jit(solution)/shard_map/pallas_call | solution.py:414
  (6 shorter events, 0.1 us)
Async XLA Ops:
  0.6 14.0 %copy-start.2 = (bf16[3,32,180]{2,1,0:T(8,128)(2,1)S(1)}, bf16[3,32,180]{2,1,0:T(8,128)(2,1)}, u32[]{:S(2)}) copy-start(bf16[3,32,180]{2,1,0:T(8,128)(2,1)} %bg_ref.3) | copy-start | bytes 103684
  3.7 2.1 %copy-start = (bf16[3,180,32,128]{3,2,1,0:T(8,128)(2,1)}, bf16[3,180,32,128]{3,2,1,0:T(8,128)(2,1)S(1)}, u32[]{:S(2)}) copy-start(bf16[3,180,32,128]{3,2,1,0:T(8,128)(2,1)S(1)} %get-tuple-element.17.m_ref) | copy-start | bytes 13271044
  5.8 5.6 %collective-permute-start = (bf16[3,2,32,128]{3,2,1,0:T(8,128)(2,1)S(1)}, bf16[3,2,32,128]{3,2,1,0:T(8,128)(2,1)S(1)}, u32[]{:S(2)}, u32[]{:S(2)}) collective-permute-start(bf16[3,2,32,128]{3,2,1,0:T(8,128)(2,1)S(1)} %get-tuple-element.20), channel_id=1, source_target_pairs={{0,4},{4,0},{8,12},{12,8},{16,20},{20,16},{24,28},{28,24},{1,5},{5... | collective-permute-start | bytes 147464 | tf_op jit(solution)/shard_map/ppermute | solution.py:334
  6.2 5.3 %collective-permute-start.1 = (bf16[3,2,32,128]{3,2,1,0:T(8,128)(2,1)S(1)}, bf16[3,2,32,128]{3,2,1,0:T(8,128)(2,1)S(1)}, u32[]{:S(2)}, u32[]{:S(2)}) collective-permute-start(bf16[3,2,32,128]{3,2,1,0:T(8,128)(2,1)S(1)} %get-tuple-element.21), channel_id=1, source_target_pairs={{0,28},{4,8},{8,4},{12,16},{16,12},{20,24},{24,20},{28,0},{1,29},{... | collective-permute-start | bytes 147464 | tf_op jit(solution)/shard_map/ppermute | solution.py:333
  9.8 12.8 %collective-permute-start.2 = (bf16[3,360,128]{2,1,0:T(8,128)(2,1)S(1)}, bf16[3,360,128]{2,1,0:T(8,128)(2,1)S(1)}, u32[]{:S(2)}, u32[]{:S(2)}) collective-permute-start(bf16[3,360,128]{2,1,0:T(8,128)(2,1)S(1)} %get-tuple-element.22), channel_id=1, source_target_pairs={{0,1},{1,0},{2,3},{3,2},{4,5},{5,4},{6,7},{7,6},{8,9},{9,8},{10,11... | collective-permute-start | bytes 829448 | tf_op jit(solution)/shard_map/ppermute | solution.py:332
  11.4 11.2 %collective-permute-start.3 = (bf16[3,360,128]{2,1,0:T(8,128)(2,1)S(1)}, bf16[3,360,128]{2,1,0:T(8,128)(2,1)S(1)}, u32[]{:S(2)}, u32[]{:S(2)}) collective-permute-start(bf16[3,360,128]{2,1,0:T(8,128)(2,1)S(1)} %get-tuple-element.23), channel_id=1, source_target_pairs={{0,4},{1,2},{2,1},{3,7},{4,0},{5,6},{6,5},{7,3},{8,12},{9,10},{10,... | collective-permute-start | bytes 829448 | tf_op jit(solution)/shard_map/ppermute | solution.py:331
  11.6 10.9 %collective-permute-start.4 = (bf16[3,8,128]{2,1,0:T(8,128)(2,1)S(1)}, bf16[3,8,128]{2,1,0:T(8,128)(2,1)S(1)}, u32[]{:S(2)}, u32[]{:S(2)}) collective-permute-start(bf16[3,8,128]{2,1,0:T(8,128)(2,1)S(1)} %bitcast.8), channel_id=1, source_target_pairs={{0,1},{1,0},{2,3},{3,2},{4,5},{5,4},{6,7},{7,6},{8,9},{9,8},{10,11... | collective-permute-start | bytes 18440 | tf_op jit(solution)/shard_map/ppermute | solution.py:340
  14.7 7.9 %collective-permute-start.5 = (bf16[3,8,128]{2,1,0:T(8,128)(2,1)S(1)}, bf16[3,8,128]{2,1,0:T(8,128)(2,1)S(1)}, u32[]{:S(2)}, u32[]{:S(2)}) collective-permute-start(bf16[3,8,128]{2,1,0:T(8,128)(2,1)S(1)} %bitcast.7), channel_id=1, source_target_pairs={{0,4},{1,2},{2,1},{3,7},{4,0},{5,6},{6,5},{7,3},{8,12},{9,10},{10,... | collective-permute-start | bytes 18440 | tf_op jit(solution)/shard_map/ppermute | solution.py:339
  14.7 2.3 %copy-start.1 = (bf16[3,180,32,128]{3,2,1,0:T(8,128)(2,1)S(1)}, bf16[3,180,32,128]{3,2,1,0:T(8,128)(2,1)}, u32[]{:S(2)}) copy-start(bf16[3,180,32,128]{3,2,1,0:T(8,128)(2,1)} %copy-done) | copy-start | bytes 13271044
  24.6 1.5 %collective-permute-start.6 = (f32[80,128]{1,0:T(8,128)S(1)}, f32[80,128]{1,0:T(8,128)S(1)}, u32[]{:S(2)}, u32[]{:S(2)}) collective-permute-start(f32[80,128]{1,0:T(8,128)S(1)} %get-tuple-element.25), channel_id=1, source_target_pairs={{0,4},{1,5},{2,6},{3,7},{4,0},{5,1},{6,2},{7,3},{8,12},{9,13},{10,... | collective-permute-start | bytes 122888 | tf_op jit(solution)/shard_map/ppermute | solution.py:349
  26.1 4.3 %collective-permute-start.9 = (f32[80,128]{1,0:T(8,128)S(1)}, f32[80,128]{1,0:T(8,128)S(1)}, u32[]{:S(2)}, u32[]{:S(2)}) collective-permute-start(f32[80,128]{1,0:T(8,128)S(1)} %add.26), channel_id=1, source_target_pairs={{0,13},{1,12},{2,15},{3,14},{4,9},{5,8},{6,11},{7,10},{8,5},{9,4},... | collective-permute-start | bytes 122888 | tf_op jit(solution)/shard_map/ppermute | solution.py:349
  28.2 3.5 %collective-permute-start.8 = (f32[80,128]{1,0:T(8,128)S(1)}, f32[80,128]{1,0:T(8,128)S(1)}, u32[]{:S(2)}, u32[]{:S(2)}) collective-permute-start(f32[80,128]{1,0:T(8,128)S(1)} %add.26), channel_id=1, source_target_pairs={{0,5},{1,4},{2,7},{3,6},{4,1},{5,0},{6,3},{7,2},{8,13},{9,12},{10,... | collective-permute-start | bytes 122888 | tf_op jit(solution)/shard_map/ppermute | solution.py:349
  28.2 3.5 %collective-permute-start.7 = (f32[80,128]{1,0:T(8,128)S(1)}, f32[80,128]{1,0:T(8,128)S(1)}, u32[]{:S(2)}, u32[]{:S(2)}) collective-permute-start(f32[80,128]{1,0:T(8,128)S(1)} %add.26), channel_id=1, source_target_pairs={{0,12},{1,13},{2,14},{3,15},{4,8},{5,9},{6,10},{7,11},{8,4},{9,5},... | collective-permute-start | bytes 122888 | tf_op jit(solution)/shard_map/ppermute | solution.py:349
  31.8 5.4 %collective-permute-start.12 = (f32[80,128]{1,0:T(8,128)S(1)}, f32[80,128]{1,0:T(8,128)S(1)}, u32[]{:S(2)}, u32[]{:S(2)}) collective-permute-start(f32[80,128]{1,0:T(8,128)S(1)} %add_add_fusion.1), channel_id=1, source_target_pairs={{0,22},{1,23},{2,20},{3,21},{4,18},{5,19},{6,16},{7,17},{8,30},{9,... | collective-permute-start | bytes 122888 | tf_op jit(solution)/shard_map/ppermute | solution.py:349
  34.2 6.3 %collective-permute-start.11 = (f32[80,128]{1,0:T(8,128)S(1)}, f32[80,128]{1,0:T(8,128)S(1)}, u32[]{:S(2)}, u32[]{:S(2)}) collective-permute-start(f32[80,128]{1,0:T(8,128)S(1)} %add_add_fusion.1), channel_id=1, source_target_pairs={{0,6},{1,7},{2,4},{3,5},{4,2},{5,3},{6,0},{7,1},{8,14},{9,15},{10,... | collective-permute-start | bytes 122888 | tf_op jit(solution)/shard_map/ppermute | solution.py:349
  35.5 5.0 %collective-permute-start.10 = (f32[80,128]{1,0:T(8,128)S(1)}, f32[80,128]{1,0:T(8,128)S(1)}, u32[]{:S(2)}, u32[]{:S(2)}) collective-permute-start(f32[80,128]{1,0:T(8,128)S(1)} %add_add_fusion.1), channel_id=1, source_target_pairs={{0,20},{1,21},{2,22},{3,23},{4,16},{5,17},{6,18},{7,19},{8,28},{9,... | collective-permute-start | bytes 122888 | tf_op jit(solution)/shard_map/ppermute | solution.py:349

commit v4 on v3

--- a/solution.py
+++ b/solution.py
@@ -16,7 +16,10 @@
 
 def row_coefs(glob, nlat):
     phi = (0.125 * (glob.astype(F32) + 0.5) - 0.0625 * nlat) * (math.pi / 180.0)
-    cosine = jnp.cos(phi)
+    square = phi * phi
+    cosine = 0.0
+    for power in range(14, -2, -2):
+        cosine = cosine * square + (-1.0) ** (power // 2) / math.factorial(power)
     return 0.05 + 0.2 * (1.0 - cosine), jnp.sqrt(cosine)
 
 
@@ -49,7 +52,7 @@
     return lax.dot_general(a, a, (((0,), (0,)), ((), ())), preferred_element_type=F32)
 
 
-def fetch_kernel(place_ref, m_hbm, m_ref, lon_a_ref, lon_b_ref, lat_a_ref, lat_b_ref, low_ref, high_ref, sems):
+def edges_kernel(place_ref, m_hbm, near_ref, lon_a_ref, lon_b_ref, lat_a_ref, lat_b_ref, m_ref, low_ref, high_ref, sems):
     fields, cols, rows, width = m_ref.shape
     lon_even = lax.rem(place_ref[0], 2) == 0
     lat_even = lax.rem(place_ref[1], 2) == 0
@@ -59,6 +62,8 @@
     for f in range(fields):
         copies[f].wait()
         first, last = m_ref[f, 0:2], m_ref[f, cols - 2:cols]
+        near_ref[f, 0:4] = m_ref[f, 0:4]
+        near_ref[f, 4:8] = m_ref[f, cols - 4:cols]
         lon_a_ref[f] = jnp.where(lon_even, last, first)
         lon_b_ref[f] = jnp.where(lon_even, first, last)
         for l in range(cols):
@@ -69,10 +74,17 @@
         lat_b_ref[f] = jnp.where(lat_even, low, high).astype(BF16)
 
 
-def inner_kernel(place_ref, m_ref, bg_ref, a_ref, en_ref, es_ref, g_ref, mat_ref, coef_ref, entries_ref, *, nlat):
+def inner_kernel(place_ref, m_hbm, bg_ref, a_ref, en_ref, es_ref, g_ref, m_ref, mat_ref, coef_ref, entries_ref, sems, *,
+                 nlat):
     cols, rows = m_ref.shape[1], m_ref.shape[2]
     wide = 2
     nt = rows // 8
+
+    def fetch(f):
+        return pltpu.make_async_copy(m_hbm.at[f], m_ref.at[f], sems.at[f])
+
+    for f in range(m_ref.shape[0]):
+        fetch(f).start()
     first = place_ref[1] * rows
 
     sub = sublane()
@@ -104,7 +116,9 @@
                 entries_ref[pl.ds(128 + rows * i + 8 * t, 8), at[1]] = entry - high
     mat_ref[...] = entries_ref[...].astype(BF16)
 
-    def field(f, gram):
+    @pl.loop(0, m_ref.shape[0])
+    def _(f):
+        fetch(f).wait()
         ground = bg_ref[f].astype(F32)
         for l in (0, 1, cols - 2, cols - 1):
             a_ref[f, l] = jnp.zeros((rows, 128), BF16)
@@ -127,9 +141,8 @@
                 made = jnp.concatenate(made, axis=0).astype(BF16)
                 l = l0 + 4 * q
                 a_ref[f, l:l + 4] = made.reshape(4, rows, 128)
-        return gram + gram_of(a_ref[f].reshape(-1, 128))
-
-    g_ref[...] = lax.fori_loop(0, m_ref.shape[0], field, jnp.zeros((128, 128), F32))
+
+    g_ref[...] = gram_of(a_ref[...].reshape(-1, 128))
 
 
 def pack(g):
@@ -146,7 +159,7 @@
     return jnp.where(col >= row, upper, upper.T)
 
 
-def outer_kernel(place_ref, en_ref, es_ref, m_ref, lon_a_ref, lon_b_ref, lat_a_ref, lat_b_ref, corner_a_ref,
+def outer_kernel(place_ref, en_ref, es_ref, near_ref, lon_a_ref, lon_b_ref, lat_a_ref, lat_b_ref, corner_a_ref,
                  corner_b_ref, bg_ref, gin_ref, an_ref, as_ref, ac_ref, g_ref, pad_ref, x_ref, *, nlat):
     fields, pairs = lat_a_ref.shape[0], lat_a_ref.shape[1]
     rows, cols = bg_ref.shape[1], bg_ref.shape[2]
@@ -157,8 +170,6 @@
     nt = rows // 8
     sub = sublane()
     gram = gin_ref[...]
-    where = lax.broadcasted_iota(jnp.int32, (pairs, 128), 0)
-    inside = (where >= 4) & (where < pairs - 4)
 
     def splat(row):
         return jnp.full((8, 128), row, jnp.int32)
@@ -171,23 +182,25 @@
         c1, k1, _ = scaled_coefs(splat(first + halo), nlat)
         _, _, wa = scaled_coefs(splat(first + near) + (sub % 2 - par), nlat)
         many = pairs // 8
-        c = jnp.concatenate([c0 + c1] * many, axis=0)
-        k = jnp.concatenate([k0 + k1] * many, axis=0)
-        w = jnp.concatenate([0.04 * wa] * many, axis=0)
-        outermost = where % 2 == par
+        outermost = sub % 2 == par
+        c = jnp.concatenate([jnp.where(outermost, c0 + c1, 0.0)] * many, axis=0)
+        k = jnp.concatenate([jnp.where(outermost, k0 + k1, 0.0)] * many, axis=0)
+        w = jnp.concatenate([jnp.where(exists, 0.04 * wa, 0.0)] * many, axis=0)
         for f in range(fields):
-            h = jnp.where(use_b, b_h_ref[f].astype(F32), a_h_ref[f].astype(F32))
-            h = jnp.where(exists, h, 0.0)
-            pad_ref[8:8 + pairs] = h
-            nearer = pad_ref[8 + sign:8 + sign + pairs]
-            wide = pad_ref[8 + sign - 2:8 + sign - 2 + pairs] + pad_ref[8 + sign + 2:8 + sign + 2 + pairs]
-            more = h + jnp.where(outermost, c * nearer + k * wide, 0.0)
-            made = jnp.where(inside, e_ref[f] + w * more, 0.0).astype(BF16)
+            h = jnp.where(use_b, b_h_ref[f], a_h_ref[f]).astype(F32)
+            pad = pad_ref.at[fields * par + f]
+            pad[8:8 + pairs] = h
+            nearer = pad[8 + sign:8 + sign + pairs]
+            wide = pad[8 + sign - 2:8 + sign - 2 + pairs] + pad[8 + sign + 2:8 + sign + 2 + pairs]
+            made = e_ref[f] + w * (h + c * nearer + k * wide)
+            made = jnp.concatenate([jnp.where(sub >= 4, made[:8], 0.0), made[8:pairs - 8],
+                                    jnp.where(sub < 4, made[pairs - 8:], 0.0)], axis=0).astype(BF16)
+            edge = jnp.where(exists, jnp.concatenate([h[:8], h[pairs - 8:]], axis=0), 0.0)
             out_ref[f] = made
             gram = gram + gram_of(made)
             for l in range(4):
-                x_ref[f, 2 + l, at:at + 2] = h[2 * l:2 * l + 2]
-                x_ref[f, 6 + l, at:at + 2] = h[pairs - 8 + 2 * l:pairs - 6 + 2 * l]
+                x_ref[f, 2 + l, at:at + 2] = edge[2 * l:2 * l + 2]
+                x_ref[f, 6 + l, at:at + 2] = edge[8 + 2 * l:10 + 2 * l]
             corner = jnp.where(use_b, b_c_ref[f].astype(F32), a_c_ref[f].astype(F32))
             corner = jnp.where(exists, corner, 0.0)
             west = jnp.where(lon_even, corner[4:8], corner[0:4])
@@ -199,8 +212,8 @@
         for l in range(12):
             x_ref[f, l, rows + 2:rows + 6] = jnp.zeros((4, 128), F32)
         for l in range(4):
-            x_ref[f, 2 + l, 0:rows] = m_ref[f, l].astype(F32)
-            x_ref[f, 6 + l, 0:rows] = m_ref[f, cols - 4 + l].astype(F32)
+            x_ref[f, 2 + l, 0:rows] = near_ref[f, l].astype(F32)
+            x_ref[f, 6 + l, 0:rows] = near_ref[f, 4 + l].astype(F32)
         for l in range(2):
             a, b = lon_a_ref[f, l].astype(F32), lon_b_ref[f, l].astype(F32)
             x_ref[f, l, 0:rows] = jnp.where(lon_even, b, a)
@@ -236,34 +249,53 @@
 
 
 def factor(g):
-    n = 128
+    n, block, near = 128, 16, 4
     lane = lax.broadcasted_iota(jnp.int32, (8, n), 1)
-    sub = lax.broadcasted_iota(jnp.int32, (8, n), 0)
+    sub = sublane()
     w = list(g)
-    tiles = len(w)
-    for b0 in range(tiles):
-        cols = [[jnp.broadcast_to(w[b][:, 8 * b0 + j:8 * b0 + j + 1], (8, n)) for b in range(b0, tiles)]
-                for j in range(8)]
-        for s in range(8):
-            k = 8 * b0 + s
-            inverse = 1.0 / jnp.broadcast_to(cols[s][0][s:s + 1], (8, n))
-            pivot_row = jnp.where(lane == k, 1.0, jnp.broadcast_to(w[b0][s:s + 1], (8, n)))
-            rows = [jnp.broadcast_to(cols[j][0][s:s + 1], (8, n)) for j in range(s + 1, 8)]
-            for b in range(b0, tiles):
-                i = b - b0
-                f = cols[s][i] * inverse
-                if i == 0:
-                    if s == 7:
-                        continue
-                    f = jnp.where(sub > s, f, 0.0)
-                    kept = jnp.where((lane == k) & (sub > s), 0.0, w[b])
+    for t0 in range(0, len(w), 2):
+        k0 = 8 * t0
+        close = range(t0, min(len(w), t0 + near))
+        cols = {b: [jnp.broadcast_to(w[b][:, k0 + j:k0 + j + 1], (8, n)) for j in range(block)] for b in close}
+        below = {b: jnp.where((lane >= k0) & (lane < k0 + block), 0.0, w[b]) for b in range(t0 + 2, len(w))}
+        inverses = [None, None]
+        for s in range(block):
+            k, top, row = k0 + s, t0 + s // 8, s % 8
+            inverse = 1.0 / jnp.broadcast_to(cols[top][s][row:row + 1], (8, n))
+            old = inverses[s // 8]
+            inverses[s // 8] = inverse if old is None else jnp.where(sub >= row, inverse, old)
+            pivot_row = jnp.where(lane == k, 1.0, jnp.broadcast_to(w[top][row:row + 1], (8, n)))
+            outside = jnp.where((lane > k) & (lane < k0 + block), 0.0, pivot_row)
+            heads = [jnp.broadcast_to(cols[top][j][row:row + 1], (8, n)) for j in range(s + 1, block)]
+            for b in close:
+                if b < top or (b == top and row == 7):
+                    continue
+                f = cols[b][s] * inverse
+                if b == top:
+                    f = jnp.where(sub > row, f, 0.0)
+                if b < t0 + 2:
+                    at = (lane == k) & (sub > row) if b == top else lane == k
+                    w[b] = jnp.where(at, 0.0, w[b]) - f * pivot_row
                 else:
-                    kept = jnp.where(lane == k, 0.0, w[b])
-                w[b] = kept - f * pivot_row
-                for j in range(s + 1, 8):
-                    cols[j][i] = cols[j][i] - f * rows[j - s - 1]
+                    below[b] = below[b] - f * outside
+                for j in range(s + 1, block):
+                    cols[b][j] = cols[b][j] - f * heads[j - s - 1]
+        if t0 + near < len(w):
+            factors, rows = [], []
+            for h in range(2):
+                pivot = k0 + 8 * h + sub
+                factors.append(w[t0 + h] * inverses[h])
+                rows.append(jnp.where(lane == pivot, 1.0,
+                                      jnp.where((lane > pivot) & (lane < k0 + block), 0.0, w[t0 + h])))
+            update = lax.dot_general(jnp.concatenate(factors, axis=0), jnp.concatenate(rows, axis=0),
+                                     (((0,), (0,)), ((), ())), precision=lax.Precision.HIGHEST,
+                                     preferred_element_type=F32)
+            for b in range(t0 + near, len(w)):
+                below[b] = below[b] - update[8 * b:8 * b + 8]
+        for b in below:
+            w[b] = below[b]
     r, x = [], []
-    for b in range(tiles):
+    for b in range(len(w)):
         diag = lane == sub + 8 * b
         scale = lax.rsqrt(jnp.sum(jnp.where(diag, w[b], 0.0), axis=1, keepdims=True))
         r.append(jnp.where(lane >= sub + 8 * b, w[b] * scale, 0.0))
@@ -271,9 +303,12 @@
     return jnp.concatenate(r, axis=0), jnp.concatenate(x, axis=0)
 
 
-def modes_kernel(p_ref, an_ref, as_ref, ac_ref, a_ref, out_hbm, r_ref, x_ref, o_ref, sems, *, total, lons):
+def modes_kernel(p_ref, an_ref, as_ref, ac_ref, a_ref, out_hbm, r_ref, x_ref, o_ref, sems, *, total):
     fields, cols, rows, width = out_hbm.shape
-    per = cols // lons
+    quarter = cols // 4
+    bounds = [quarter * q for q in range(5)]
+    parts = [(f, lo, hi) for f in range(fields) for lo, hi in zip(bounds, bounds[1:])]
+    parts[:1] = [(0, 0, quarter // 3), (0, quarter // 3, quarter)]
     g = unpack(p_ref[...]) * (1.0 / total)
     r, x = factor(tiles_of(g))
     r_ref[...] = r
@@ -285,27 +320,23 @@
     def times(a):
         return jnp.dot(jnp.concatenate([a, a], axis=1), x_ref[...], preferred_element_type=F32)
 
-    def part_copy(f, q):
-        part = pl.ds(q * lons, lons)
-        return pltpu.make_async_copy(o_ref.at[f, part], out_hbm.at[f, part], sems.at[f * per + q])
-
-    for f in range(fields):
-        for q in range(per):
-            at = slice(q * lons, q * lons + lons)
-            o_ref[f, at] = times(a_ref[f, at].reshape(-1, width)).reshape(lons, rows, width)
-            north = times(an_ref[f, 2 * q * lons:2 * (q + 1) * lons])
-            south = times(as_ref[f, 2 * q * lons:2 * (q + 1) * lons])
-            for l in range(lons):
-                at = q * lons + l
-                if at < 2 or at >= cols - 2:
-                    o_ref[f, at] = times(ac_ref[f, at if at < 2 else at - cols + 4])
-                else:
-                    o_ref[f, at, 0:2] = north[2 * l:2 * l + 2]
-                    o_ref[f, at, rows - 2:rows] = south[2 * l:2 * l + 2]
-            part_copy(f, q).start()
-    for f in range(fields):
-        for q in range(per):
-            part_copy(f, q).wait()
+    def leave(i):
+        f, lo, hi = parts[i]
+        return pltpu.make_async_copy(o_ref.at[f, pl.ds(lo, hi - lo)], out_hbm.at[f, pl.ds(lo, hi - lo)], sems.at[i])
+
+    for i, (f, lo, hi) in enumerate(parts):
+        o_ref[f, lo:hi] = times(a_ref[f, lo:hi].reshape(-1, width)).reshape(hi - lo, rows, width)
+        if lo == 0:
+            north, south = times(an_ref[f]), times(as_ref[f])
+        for l in range(lo, hi):
+            if l < 2 or l >= cols - 2:
+                o_ref[f, l] = times(ac_ref[f, l if l < 2 else l - cols + 4])
+            else:
+                o_ref[f, l, 0:2] = north[2 * l:2 * l + 2]
+                o_ref[f, l, rows - 2:rows] = south[2 * l:2 * l + 2]
+        leave(i).start()
+    for i in range(len(parts)):
+        leave(i).wait()
 
 
 def exchanges(lon, lat):
@@ -367,7 +398,6 @@
     fields, rows, cols, width = members.shape
     lat, lon = lax.axis_size("lat"), lax.axis_size("lon")
     nlat = rows * lat
-    lons = cols // 4
     pairs = 2 * cols
     place = jnp.stack([lax.axis_index("lon"), lax.axis_index("lat")]).astype(jnp.int32)
     smem = pl.BlockSpec(memory_space=pltpu.SMEM)
@@ -378,47 +408,50 @@
     def kept(*xs):
         return [pltpu.with_memory_space_constraint(x, pltpu.VMEM) for x in xs]
 
-    m, *sent = pl.pallas_call(
-        fetch_kernel,
-        out_shape=(pltpu.VMEM((fields, cols, rows, width), BF16),) + (pltpu.VMEM((fields, 2, rows, width), BF16),) * 2
+    m = pltpu.with_memory_space_constraint(jnp.transpose(members, (0, 2, 1, 3)), pltpu.HBM)
+    near, *sent = pl.pallas_call(
+        edges_kernel,
+        out_shape=(pltpu.VMEM((fields, 8, rows, width), BF16),) + (pltpu.VMEM((fields, 2, rows, width), BF16),) * 2
         + (pltpu.VMEM((fields, pairs, width), BF16),) * 2,
         in_specs=[smem, hbm],
         out_specs=(vmem,) * 5,
-        scratch_shapes=[pltpu.VMEM((pairs, width), F32), pltpu.VMEM((pairs, width), F32),
-                        pltpu.SemaphoreType.DMA((fields,))],
+        scratch_shapes=[pltpu.VMEM((fields, cols, rows, width), BF16), pltpu.VMEM((pairs, width), F32),
+                        pltpu.VMEM((pairs, width), F32), pltpu.SemaphoreType.DMA((fields,))],
         compiler_params=params,
-    )(place, pltpu.with_memory_space_constraint(jnp.transpose(members, (0, 2, 1, 3)), pltpu.HBM))
+    )(place, m)
     beside = halos(*sent)
     a, en, es, gram = pl.pallas_call(
         functools.partial(inner_kernel, nlat=nlat),
         out_shape=(pltpu.VMEM((fields, cols, rows, width), BF16), pltpu.VMEM((fields, pairs, width), F32),
                    pltpu.VMEM((fields, pairs, width), F32), pltpu.VMEM((width, width), F32)),
-        in_specs=[smem, vmem, vmem],
+        in_specs=[smem, hbm, vmem],
         out_specs=(vmem,) * 4,
-        scratch_shapes=[pltpu.VMEM((256, 256), BF16), pltpu.VMEM((4, rows // 8, 8, 128), F32),
-                        pltpu.VMEM((256, 256), F32)],
+        scratch_shapes=[pltpu.VMEM((fields, cols, rows, width), BF16), pltpu.VMEM((256, 256), BF16),
+                        pltpu.VMEM((4, rows // 8, 8, 128), F32), pltpu.VMEM((256, 256), F32),
+                        pltpu.SemaphoreType.DMA((fields,))],
         compiler_params=params,
         cost_estimate=pl.CostEstimate(flops=16 * fields * cols * rows * width * width,
                                       bytes_accessed=8 * fields * cols * rows * width, transcendentals=0),
-    )(place, *kept(m), background)
+    )(place, m, background)
     an, as_, ac, packed = pl.pallas_call(
         functools.partial(outer_kernel, nlat=nlat),
         out_shape=(pltpu.VMEM((fields, pairs, width), BF16), pltpu.VMEM((fields, pairs, width), BF16),
                    pltpu.VMEM((fields, 4, rows, width), BF16), pltpu.VMEM((80, width), F32)),
         in_specs=[smem] + [vmem] * 11,
         out_specs=(vmem,) * 4,
-        scratch_shapes=[pltpu.VMEM((pairs + 16, width), F32), pltpu.VMEM((fields, 12, rows + 8, width), F32)],
+        scratch_shapes=[pltpu.VMEM((2 * fields, pairs + 16, width), F32),
+                        pltpu.VMEM((fields, 12, rows + 8, width), F32)],
         compiler_params=params,
-    )(place, *kept(en, es, m, *beside, background, gram))
+    )(place, *kept(en, es, near, *beside, background, gram))
     packed = total_gram(packed)
     modes, r_factor = pl.pallas_call(
-        functools.partial(modes_kernel, total=float(fields * nlat * cols * lon), lons=lons),
+        functools.partial(modes_kernel, total=float(fields * nlat * cols * lon)),
         out_shape=(jax.ShapeDtypeStruct((fields, cols, rows, width), F32),
                    jax.ShapeDtypeStruct((width, width), F32)),
         in_specs=[vmem] * 5,
         out_specs=(hbm, vmem),
         scratch_shapes=[pltpu.VMEM((2 * width, width), BF16), pltpu.VMEM((fields, cols, rows, width), F32),
-                        pltpu.SemaphoreType.DMA((fields * 4,))],
+                        pltpu.SemaphoreType.DMA((fields * 4 + 1,))],
         compiler_params=params,
     )(*kept(packed, an, as_, ac, a))
     return jnp.transpose(modes, (0, 2, 1, 3)), r_factor

time: 50 us -> 45.1 us (0.902)
  local copies, waits for them, and re-layouts: 4.36 us -> 0.02 us
  Pallas kernels: 20 us -> 19.4 us
    unnamed x7 -> x3, local copies, waits for them, and re-layouts: 4.35 us -> 0.01 us
    pallas_call x1, Pallas kernels: 9.33 us -> 8.53 us  [local(): pl.pallas_call(functools.partial(modes_kernel, total=float(fields * nlat...]
    pallas_call x1, Pallas kernels: 5.63 us -> 6.19 us  [local(): pl.pallas_call(functools.partial(inner_kernel, nlat=nlat), out_shape=(plt...]
  transfers between devices with their start and end apart: 13 -> 13, of which waited for: 6 -> 6; matrix products, arithmetic and copies ran while one was open for 0% -> 0% of each run, Pallas kernels for 11% -> 14%
where the time goes in v4:
time: 45.1 us; the launch traced here: 45 us
  Pallas kernels  19.4 us (43%)
  starting transfers between devices  16.4 us (36%)
  waiting for transfers between devices  8.33 us (18%)
  between operations  0.73 us (2%)
    pallas_call x1, Pallas kernels, local(): pl.pallas_call(functools.partial(modes_kernel, total=float(fields * nlat...  8.53 us
    ppermute x7, waiting for transfers between devices, partner(): return lax.ppermute(gram, ('lon', 'lat'), pairs)  8.13 us
    ppermute x7, starting transfers between devices, partner(): return lax.ppermute(gram, ('lon', 'lat'), pairs)  7.68 us
    pallas_call x1, Pallas kernels, local(): pl.pallas_call(functools.partial(inner_kernel, nlat=nlat), out_shape=(plt...  6.19 us
    ppermute x1, starting transfers between devices, halos(): lon_b = lax.ppermute(lon_b, 'lon', by_lon_b)  3.56 us
    ppermute x1, starting transfers between devices, halos(): corner_a = lax.ppermute(jnp.where(even, high, low), both, by_lat_a)  3.04 us
    pallas_call x1, Pallas kernels, local(): pl.pallas_call(edges_kernel, out_shape=(pltpu.VMEM((fields, 8, rows, widt...  2.98 us
    pallas_call x1, Pallas kernels, local(): pl.pallas_call(functools.partial(outer_kernel, nlat=nlat), out_shape=(plt...  1.71 us
  transfers between devices with their start and end apart: 13, of which 6 were waited for; matrix products, arithmetic and copies ran while one was open for 0% of the time, Pallas kernels for 14%

profile of v4, /device:TPU:0, one launch (start us, length us, event | category | flops | bytes accessed | tf_op | source)
XLA Modules:
  0.0 45.0 jit_solution(3551845966729881376)
XLA Ops:
  0.6 0.0 copy-start
  0.6 0.1 pad_add_fusion.place_ref
  0.7 3.0 %shard_map.42 = (bf16[3,8,32,128]{3,2,1,0:T(8,128)(2,1)S(1)}, bf16[3,2,32,128]{3,2,1,0:T(8,128)(2,1)S(1)}, bf16[3,2,32,128]{3,2,1,0:T(8,128)(2,1)S(1)}, bf16[3,3...) custom-call(s32[2]{0:T(128)S(1)} %pad_add_fusion.place_ref, bf16[3,180,32,128]{3,2,1,0:T(8,128)(2,1)} %bitcast.6), custom_call_target="tpu_custom_call" | custom-call | tf_op jit(solution)/shard_map/pallas_call | solution.py:412
  3.7 0.5 %collective-permute-start = (bf16[3,2,32,128]{3,2,1,0:T(8,128)(2,1)S(1)}, bf16[3,2,32,128]{3,2,1,0:T(8,128)(2,1)S(1)}, u32[]{:S(2)}, u32[]{:S(2)}) collective-permute-start(bf16[3,2,32,128]{3,2,1,0:T(8,128)(2,1)S(1)} %get-tuple-element.20), channel_id=1, source_target_pairs={{0,4},{4,0},{8,12},{12,8},{16,20},{20,16},{24,28},{28,24},{1,5},{5... | collective-permute-start | bytes 147464 | tf_op jit(solution)/shard_map/ppermute | solution.py:365
  4.2 3.6 %collective-permute-start.1 = (bf16[3,2,32,128]{3,2,1,0:T(8,128)(2,1)S(1)}, bf16[3,2,32,128]{3,2,1,0:T(8,128)(2,1)S(1)}, u32[]{:S(2)}, u32[]{:S(2)}) collective-permute-start(bf16[3,2,32,128]{3,2,1,0:T(8,128)(2,1)S(1)} %get-tuple-element.21), channel_id=1, source_target_pairs={{0,28},{4,8},{8,4},{12,16},{16,12},{20,24},{24,20},{28,0},{1,29},{... | collective-permute-start | bytes 147464 | tf_op jit(solution)/shard_map/ppermute | solution.py:364
  7.8 1.6 %collective-permute-start.2 = (bf16[3,360,128]{2,1,0:T(8,128)(2,1)S(1)}, bf16[3,360,128]{2,1,0:T(8,128)(2,1)S(1)}, u32[]{:S(2)}, u32[]{:S(2)}) collective-permute-start(bf16[3,360,128]{2,1,0:T(8,128)(2,1)S(1)} %get-tuple-element.22), channel_id=1, source_target_pairs={{0,1},{1,0},{2,3},{3,2},{4,5},{5,4},{6,7},{7,6},{8,9},{9,8},{10,11... | collective-permute-start | bytes 829448 | tf_op jit(solution)/shard_map/ppermute | solution.py:363
  9.4 0.0 collective-permute-start.3
  9.4 0.0 collective-permute-done.lon_a_ref
  9.4 0.2 collective-permute-done.1.lon_b_ref
  9.6 3.0 %collective-permute-start.4 = (bf16[3,8,128]{2,1,0:T(8,128)(2,1)S(1)}, bf16[3,8,128]{2,1,0:T(8,128)(2,1)S(1)}, u32[]{:S(2)}, u32[]{:S(2)}) collective-permute-start(bf16[3,8,128]{2,1,0:T(8,128)(2,1)S(1)} %bitcast.9), channel_id=1, source_target_pairs={{0,1},{1,0},{2,3},{3,2},{4,5},{5,4},{6,7},{7,6},{8,9},{9,8},{10,11... | collective-permute-start | bytes 18440 | tf_op jit(solution)/shard_map/ppermute | solution.py:371
  12.6 0.0 collective-permute-start.5
  12.6 0.0 copy-done
  12.6 6.2 %shard_map.41 = (bf16[3,180,32,128]{3,2,1,0:T(8,128)(2,1)S(1)}, f32[3,360,128]{2,1,0:T(8,128)S(1)}, f32[3,360,128]{2,1,0:T(8,128)S(1)}, f32[128,128]{1,0:T(8,128)S(1)}) custom-call(s32[2]{0:T(128)S(1)} %pad_add_fusion.place_ref, bf16[3,180,32,128]{3,2,1,0:T(8,128)(2,1)} %bitcast.7, bf16[3,32,180]{2,1,0:T(8,128)(2,1)S(1)} %copy-done), custom_call_target="tpu_custom_call" | custom-call | flops 4529848320 | bytes 17694720 | tf_op jit(solution)/shard_map/pallas_call | solution.py:423
  18.8 0.0 collective-permute-done.4.corner_a_ref
  18.9 0.0 collective-permute-done.5.corner_b_ref
  18.9 0.0 collective-permute-done.2.lat_a_ref
  18.9 0.0 collective-permute-done.3.lat_b_ref
  18.9 1.7 %shard_map.43 = (bf16[3,360,128]{2,1,0:T(8,128)(2,1)S(1)}, bf16[3,360,128]{2,1,0:T(8,128)(2,1)S(1)}, bf16[3,4,32,128]{3,2,1,0:T(8,128)(2,1)S(1)}, f32[80,128]{1,0:T(8,128)S(1)}) custom-call(s32[2]{0:T(128)S(1)} %pad_add_fusion.place_ref, f32[3,360,128]{2,1,0:T(8,128)S(1)} %get-tuple-element.17.en_ref, f32[3,360,128]{2,1,0:T(8,128)S(1)} %get-tuple-element.18.es_ref, ...), custom_call_target="tpu_custom_call" | custom-call | tf_op jit(solution)/shard_map/pallas_call | solution.py:436
  20.6 0.6 %collective-permute-start.6 = (f32[80,128]{1,0:T(8,128)S(1)}, f32[80,128]{1,0:T(8,128)S(1)}, u32[]{:S(2)}, u32[]{:S(2)}) collective-permute-start(f32[80,128]{1,0:T(8,128)S(1)} %get-tuple-element.25), channel_id=1, source_target_pairs={{0,4},{1,5},{2,6},{3,7},{4,0},{5,1},{6,2},{7,3},{8,12},{9,13},{10,... | collective-permute-start | bytes 122888 | tf_op jit(solution)/shard_map/ppermute | solution.py:380
  21.2 0.9 %collective-permute-done.6 = f32[80,128]{1,0:T(8,128)S(1)} collective-permute-done((f32[80,128]{1,0:T(8,128)S(1)}, f32[80,128]{1,0:T(8,128)S(1)}, u32[]{:S(2)}, u32[]{:S(2)}) %collective-permute-start.6) | collective-permute-done | bytes 40992 | tf_op jit(solution)/shard_map/ppermute | solution.py:380
  22.1 2.2 %collective-permute-start.9 = (f32[80,128]{1,0:T(8,128)S(1)}, f32[80,128]{1,0:T(8,128)S(1)}, u32[]{:S(2)}, u32[]{:S(2)}) collective-permute-start(f32[80,128]{1,0:T(8,128)S(1)} %add.26), channel_id=1, source_target_pairs={{0,13},{1,12},{2,15},{3,14},{4,9},{5,8},{6,11},{7,10},{8,5},{9,4},... | collective-permute-start | bytes 122888 | tf_op jit(solution)/shard_map/ppermute | solution.py:380
  24.2 0.0 collective-permute-start.8
  24.2 1.0 %collective-permute-start.7 = (f32[80,128]{1,0:T(8,128)S(1)}, f32[80,128]{1,0:T(8,128)S(1)}, u32[]{:S(2)}, u32[]{:S(2)}) collective-permute-start(f32[80,128]{1,0:T(8,128)S(1)} %add.26), channel_id=1, source_target_pairs={{0,12},{1,13},{2,14},{3,15},{4,8},{5,9},{6,10},{7,11},{8,4},{9,5},... | collective-permute-start | bytes 122888 | tf_op jit(solution)/shard_map/ppermute | solution.py:380
  25.2 1.2 %collective-permute-done.9 = f32[80,128]{1,0:T(8,128)S(1)} collective-permute-done((f32[80,128]{1,0:T(8,128)S(1)}, f32[80,128]{1,0:T(8,128)S(1)}, u32[]{:S(2)}, u32[]{:S(2)}) %collective-permute-start.9) | collective-permute-done | bytes 40992 | tf_op jit(solution)/shard_map/ppermute | solution.py:380
  26.4 1.3 %collective-permute-done.8 = f32[80,128]{1,0:T(8,128)S(1)} collective-permute-done((f32[80,128]{1,0:T(8,128)S(1)}, f32[80,128]{1,0:T(8,128)S(1)}, u32[]{:S(2)}, u32[]{:S(2)}) %collective-permute-start.8) | collective-permute-done | bytes 40992 | tf_op jit(solution)/shard_map/ppermute | solution.py:380
  27.7 0.0 collective-permute-done.7
  27.7 2.4 %collective-permute-start.12 = (f32[80,128]{1,0:T(8,128)S(1)}, f32[80,128]{1,0:T(8,128)S(1)}, u32[]{:S(2)}, u32[]{:S(2)}) collective-permute-start(f32[80,128]{1,0:T(8,128)S(1)} %add_add_fusion.1), channel_id=1, source_target_pairs={{0,22},{1,23},{2,20},{3,21},{4,18},{5,19},{6,16},{7,17},{8,30},{9,... | collective-permute-start | bytes 122888 | tf_op jit(solution)/shard_map/ppermute | solution.py:380
  30.1 1.3 %collective-permute-start.11 = (f32[80,128]{1,0:T(8,128)S(1)}, f32[80,128]{1,0:T(8,128)S(1)}, u32[]{:S(2)}, u32[]{:S(2)}) collective-permute-start(f32[80,128]{1,0:T(8,128)S(1)} %add_add_fusion.1), channel_id=1, source_target_pairs={{0,6},{1,7},{2,4},{3,5},{4,2},{5,3},{6,0},{7,1},{8,14},{9,15},{10,... | collective-permute-start | bytes 122888 | tf_op jit(solution)/shard_map/ppermute | solution.py:380
  31.4 0.3 collective-permute-start.10
  31.7 1.4 %collective-permute-done.12 = f32[80,128]{1,0:T(8,128)S(1)} collective-permute-done((f32[80,128]{1,0:T(8,128)S(1)}, f32[80,128]{1,0:T(8,128)S(1)}, u32[]{:S(2)}, u32[]{:S(2)}) %collective-permute-start.12) | collective-permute-done | bytes 40992 | tf_op jit(solution)/shard_map/ppermute | solution.py:380
  33.1 3.3 %collective-permute-done.11 = f32[80,128]{1,0:T(8,128)S(1)} collective-permute-done((f32[80,128]{1,0:T(8,128)S(1)}, f32[80,128]{1,0:T(8,128)S(1)}, u32[]{:S(2)}, u32[]{:S(2)}) %collective-permute-start.11) | collective-permute-done | bytes 40992 | tf_op jit(solution)/shard_map/ppermute | solution.py:380
  36.4 0.0 collective-permute-done.10
  36.5 8.5 %shard_map.44 = (f32[3,180,32,128]{3,2,1,0:T(8,128)}, f32[128,128]{1,0:T(8,128)}) custom-call(f32[80,128]{1,0:T(8,128)S(1)} %add_add_fusion.p_ref, bf16[3,360,128]{2,1,0:T(8,128)(2,1)S(1)} %get-tuple-element.26.an_ref, bf16[3,360,128]{2,1,0:T(8,128)(2,1)S(1)} %get-tuple-element.27.as_ref, bf16[3,4,32,128]{3,2,1,0:T(8,128)(2,1)S(1)} %get-tuple-element.28.ac_ref, ...), custom_call_target="tpu_custom_call" | custom-call | tf_op jit(solution)/shard_map/pallas_call | solution.py:447
  (6 shorter events, 0.1 us)
Async XLA Ops:
  0.6 12.0 %copy-start = (bf16[3,32,180]{2,1,0:T(8,128)(2,1)S(1)}, bf16[3,32,180]{2,1,0:T(8,128)(2,1)}, u32[]{:S(2)}) copy-start(bf16[3,32,180]{2,1,0:T(8,128)(2,1)} %bg_ref.3) | copy-start | bytes 103684
  3.7 5.7 %collective-permute-start = (bf16[3,2,32,128]{3,2,1,0:T(8,128)(2,1)S(1)}, bf16[3,2,32,128]{3,2,1,0:T(8,128)(2,1)S(1)}, u32[]{:S(2)}, u32[]{:S(2)}) collective-permute-start(bf16[3,2,32,128]{3,2,1,0:T(8,128)(2,1)S(1)} %get-tuple-element.20), channel_id=1, source_target_pairs={{0,4},{4,0},{8,12},{12,8},{16,20},{20,16},{24,28},{28,24},{1,5},{5... | collective-permute-start | bytes 147464 | tf_op jit(solution)/shard_map/ppermute | solution.py:365
  4.2 5.3 %collective-permute-start.1 = (bf16[3,2,32,128]{3,2,1,0:T(8,128)(2,1)S(1)}, bf16[3,2,32,128]{3,2,1,0:T(8,128)(2,1)S(1)}, u32[]{:S(2)}, u32[]{:S(2)}) collective-permute-start(bf16[3,2,32,128]{3,2,1,0:T(8,128)(2,1)S(1)} %get-tuple-element.21), channel_id=1, source_target_pairs={{0,28},{4,8},{8,4},{12,16},{16,12},{20,24},{24,20},{28,0},{1,29},{... | collective-permute-start | bytes 147464 | tf_op jit(solution)/shard_map/ppermute | solution.py:364
  7.8 11.1 %collective-permute-start.2 = (bf16[3,360,128]{2,1,0:T(8,128)(2,1)S(1)}, bf16[3,360,128]{2,1,0:T(8,128)(2,1)S(1)}, u32[]{:S(2)}, u32[]{:S(2)}) collective-permute-start(bf16[3,360,128]{2,1,0:T(8,128)(2,1)S(1)} %get-tuple-element.22), channel_id=1, source_target_pairs={{0,1},{1,0},{2,3},{3,2},{4,5},{5,4},{6,7},{7,6},{8,9},{9,8},{10,11... | collective-permute-start | bytes 829448 | tf_op jit(solution)/shard_map/ppermute | solution.py:363
  9.4 9.5 %collective-permute-start.3 = (bf16[3,360,128]{2,1,0:T(8,128)(2,1)S(1)}, bf16[3,360,128]{2,1,0:T(8,128)(2,1)S(1)}, u32[]{:S(2)}, u32[]{:S(2)}) collective-permute-start(bf16[3,360,128]{2,1,0:T(8,128)(2,1)S(1)} %get-tuple-element.23), channel_id=1, source_target_pairs={{0,4},{1,2},{2,1},{3,7},{4,0},{5,6},{6,5},{7,3},{8,12},{9,10},{10,... | collective-permute-start | bytes 829448 | tf_op jit(solution)/shard_map/ppermute | solution.py:362
  9.6 9.2 %collective-permute-start.4 = (bf16[3,8,128]{2,1,0:T(8,128)(2,1)S(1)}, bf16[3,8,128]{2,1,0:T(8,128)(2,1)S(1)}, u32[]{:S(2)}, u32[]{:S(2)}) collective-permute-start(bf16[3,8,128]{2,1,0:T(8,128)(2,1)S(1)} %bitcast.9), channel_id=1, source_target_pairs={{0,1},{1,0},{2,3},{3,2},{4,5},{5,4},{6,7},{7,6},{8,9},{9,8},{10,11... | collective-permute-start | bytes 18440 | tf_op jit(solution)/shard_map/ppermute | solution.py:371
  12.6 6.2 %collective-permute-start.5 = (bf16[3,8,128]{2,1,0:T(8,128)(2,1)S(1)}, bf16[3,8,128]{2,1,0:T(8,128)(2,1)S(1)}, u32[]{:S(2)}, u32[]{:S(2)}) collective-permute-start(bf16[3,8,128]{2,1,0:T(8,128)(2,1)S(1)} %bitcast.8), channel_id=1, source_target_pairs={{0,4},{1,2},{2,1},{3,7},{4,0},{5,6},{6,5},{7,3},{8,12},{9,10},{10,... | collective-permute-start | bytes 18440 | tf_op jit(solution)/shard_map/ppermute | solution.py:370
  20.6 1.4 %collective-permute-start.6 = (f32[80,128]{1,0:T(8,128)S(1)}, f32[80,128]{1,0:T(8,128)S(1)}, u32[]{:S(2)}, u32[]{:S(2)}) collective-permute-start(f32[80,128]{1,0:T(8,128)S(1)} %get-tuple-element.25), channel_id=1, source_target_pairs={{0,4},{1,5},{2,6},{3,7},{4,0},{5,1},{6,2},{7,3},{8,12},{9,13},{10,... | collective-permute-start | bytes 122888 | tf_op jit(solution)/shard_map/ppermute | solution.py:380
  22.1 4.3 %collective-permute-start.9 = (f32[80,128]{1,0:T(8,128)S(1)}, f32[80,128]{1,0:T(8,128)S(1)}, u32[]{:S(2)}, u32[]{:S(2)}) collective-permute-start(f32[80,128]{1,0:T(8,128)S(1)} %add.26), channel_id=1, source_target_pairs={{0,13},{1,12},{2,15},{3,14},{4,9},{5,8},{6,11},{7,10},{8,5},{9,4},... | collective-permute-start | bytes 122888 | tf_op jit(solution)/shard_map/ppermute | solution.py:380
  24.2 3.5 %collective-permute-start.8 = (f32[80,128]{1,0:T(8,128)S(1)}, f32[80,128]{1,0:T(8,128)S(1)}, u32[]{:S(2)}, u32[]{:S(2)}) collective-permute-start(f32[80,128]{1,0:T(8,128)S(1)} %add.26), channel_id=1, source_target_pairs={{0,5},{1,4},{2,7},{3,6},{4,1},{5,0},{6,3},{7,2},{8,13},{9,12},{10,... | collective-permute-start | bytes 122888 | tf_op jit(solution)/shard_map/ppermute | solution.py:380
  24.2 3.5 %collective-permute-start.7 = (f32[80,128]{1,0:T(8,128)S(1)}, f32[80,128]{1,0:T(8,128)S(1)}, u32[]{:S(2)}, u32[]{:S(2)}) collective-permute-start(f32[80,128]{1,0:T(8,128)S(1)} %add.26), channel_id=1, source_target_pairs={{0,12},{1,13},{2,14},{3,15},{4,8},{5,9},{6,10},{7,11},{8,4},{9,5},... | collective-permute-start | bytes 122888 | tf_op jit(solution)/shard_map/ppermute | solution.py:380
  27.7 5.4 %collective-permute-start.12 = (f32[80,128]{1,0:T(8,128)S(1)}, f32[80,128]{1,0:T(8,128)S(1)}, u32[]{:S(2)}, u32[]{:S(2)}) collective-permute-start(f32[80,128]{1,0:T(8,128)S(1)} %add_add_fusion.1), channel_id=1, source_target_pairs={{0,22},{1,23},{2,20},{3,21},{4,18},{5,19},{6,16},{7,17},{8,30},{9,... | collective-permute-start | bytes 122888 | tf_op jit(solution)/shard_map/ppermute | solution.py:380
  30.1 6.3 %collective-permute-start.11 = (f32[80,128]{1,0:T(8,128)S(1)}, f32[80,128]{1,0:T(8,128)S(1)}, u32[]{:S(2)}, u32[]{:S(2)}) collective-permute-start(f32[80,128]{1,0:T(8,128)S(1)} %add_add_fusion.1), channel_id=1, source_target_pairs={{0,6},{1,7},{2,4},{3,5},{4,2},{5,3},{6,0},{7,1},{8,14},{9,15},{10,... | collective-permute-start | bytes 122888 | tf_op jit(solution)/shard_map/ppermute | solution.py:380
  31.4 5.0 %collective-permute-start.10 = (f32[80,128]{1,0:T(8,128)S(1)}, f32[80,128]{1,0:T(8,128)S(1)}, u32[]{:S(2)}, u32[]{:S(2)}) collective-permute-start(f32[80,128]{1,0:T(8,128)S(1)} %add_add_fusion.1), channel_id=1, source_target_pairs={{0,20},{1,21},{2,22},{3,23},{4,16},{5,17},{6,18},{7,19},{8,28},{9,... | collective-permute-start | bytes 122888 | tf_op jit(solution)/shard_map/ppermute | solution.py:380

commit v5 on v4

--- a/solution.py
+++ b/solution.py
@@ -52,10 +52,12 @@
     return lax.dot_general(a, a, (((0,), (0,)), ((), ())), preferred_element_type=F32)
 
 
-def edges_kernel(place_ref, m_hbm, near_ref, lon_a_ref, lon_b_ref, lat_a_ref, lat_b_ref, m_ref, low_ref, high_ref, sems):
+def edges_kernel(place_ref, m_hbm, m_ref, near_ref, even_ref, lon_a_ref, lon_b_ref, lat_a_ref, lat_b_ref, low_ref, high_ref,
+                 sems):
     fields, cols, rows, width = m_ref.shape
     lon_even = lax.rem(place_ref[0], 2) == 0
     lat_even = lax.rem(place_ref[1], 2) == 0
+    even_ref[...] = jnp.where(jnp.full(even_ref.shape, lat_even, jnp.bool_), 1.0, 0.0)
     copies = [pltpu.make_async_copy(m_hbm.at[f], m_ref.at[f], sems.at[f]) for f in range(fields)]
     for copy in copies:
         copy.start()
@@ -74,19 +76,11 @@
         lat_b_ref[f] = jnp.where(lat_even, low, high).astype(BF16)
 
 
-def inner_kernel(place_ref, m_hbm, bg_ref, a_ref, en_ref, es_ref, g_ref, m_ref, mat_ref, coef_ref, entries_ref, sems, *,
-                 nlat):
+def inner_kernel(place_ref, m_ref, bg_ref, a_ref, en_ref, es_ref, g_ref, mat_ref, coef_ref, entries_ref, *, nlat):
     cols, rows = m_ref.shape[1], m_ref.shape[2]
     wide = 2
     nt = rows // 8
-
-    def fetch(f):
-        return pltpu.make_async_copy(m_hbm.at[f], m_ref.at[f], sems.at[f])
-
-    for f in range(m_ref.shape[0]):
-        fetch(f).start()
     first = place_ref[1] * rows
-
     sub = sublane()
     lane = lax.broadcasted_iota(jnp.int32, TILE, 1)
     for t in range(nt):
@@ -118,7 +112,6 @@
 
     @pl.loop(0, m_ref.shape[0])
     def _(f):
-        fetch(f).wait()
         ground = bg_ref[f].astype(F32)
         for l in (0, 1, cols - 2, cols - 1):
             a_ref[f, l] = jnp.zeros((rows, 128), BF16)
@@ -354,7 +347,7 @@
     return lon_a, lon_b, lat_a, lat_b
 
 
-def halos(lon_a, lon_b, lat_a, lat_b):
+def halos(even, lon_a, lon_b, lat_a, lat_b):
     lon, lat = lax.axis_size("lon"), lax.axis_size("lat")
     by_lon_a, by_lon_b, by_lat_a, by_lat_b = exchanges(lon, lat)
     both = ("lon", "lat")
@@ -366,7 +359,7 @@
     sides = jnp.concatenate([lon_a, lon_b], axis=1)
     low = sides[:, :, :2].reshape(fields, 8, width)
     high = sides[:, :, rows - 2:].reshape(fields, 8, width)
-    even = lax.axis_index("lat") % 2 == 0
+    even = jnp.broadcast_to(even[None] > 0.5, low.shape)
     corner_b = lax.ppermute(jnp.where(even, low, high), both, by_lat_b)
     corner_a = lax.ppermute(jnp.where(even, high, low), both, by_lat_a)
     return lon_a, lon_b, lat_a, lat_b, corner_a, corner_b
@@ -409,30 +402,30 @@
         return [pltpu.with_memory_space_constraint(x, pltpu.VMEM) for x in xs]
 
     m = pltpu.with_memory_space_constraint(jnp.transpose(members, (0, 2, 1, 3)), pltpu.HBM)
-    near, *sent = pl.pallas_call(
+    m, near, even, *sent = pl.pallas_call(
         edges_kernel,
-        out_shape=(pltpu.VMEM((fields, 8, rows, width), BF16),) + (pltpu.VMEM((fields, 2, rows, width), BF16),) * 2
+        out_shape=(pltpu.VMEM((fields, cols, rows, width), BF16), pltpu.VMEM((fields, 8, rows, width), BF16),
+                   pltpu.VMEM(TILE, F32)) + (pltpu.VMEM((fields, 2, rows, width), BF16),) * 2
         + (pltpu.VMEM((fields, pairs, width), BF16),) * 2,
         in_specs=[smem, hbm],
-        out_specs=(vmem,) * 5,
-        scratch_shapes=[pltpu.VMEM((fields, cols, rows, width), BF16), pltpu.VMEM((pairs, width), F32),
-                        pltpu.VMEM((pairs, width), F32), pltpu.SemaphoreType.DMA((fields,))],
+        out_specs=(vmem,) * 7,
+        scratch_shapes=[pltpu.VMEM((pairs, width), F32), pltpu.VMEM((pairs, width), F32),
+                        pltpu.SemaphoreType.DMA((fields,))],
         compiler_params=params,
     )(place, m)
-    beside = halos(*sent)
+    beside = halos(even, *sent)
     a, en, es, gram = pl.pallas_call(
         functools.partial(inner_kernel, nlat=nlat),
         out_shape=(pltpu.VMEM((fields, cols, rows, width), BF16), pltpu.VMEM((fields, pairs, width), F32),
                    pltpu.VMEM((fields, pairs, width), F32), pltpu.VMEM((width, width), F32)),
-        in_specs=[smem, hbm, vmem],
+        in_specs=[smem, vmem, vmem],
         out_specs=(vmem,) * 4,
-        scratch_shapes=[pltpu.VMEM((fields, cols, rows, width), BF16), pltpu.VMEM((256, 256), BF16),
-                        pltpu.VMEM((4, rows // 8, 8, 128), F32), pltpu.VMEM((256, 256), F32),
-                        pltpu.SemaphoreType.DMA((fields,))],
+        scratch_shapes=[pltpu.VMEM((256, 256), BF16), pltpu.VMEM((4, rows // 8, 8, 128), F32),
+                        pltpu.VMEM((256, 256), F32)],
         compiler_params=params,
         cost_estimate=pl.CostEstimate(flops=16 * fields * cols * rows * width * width,
                                       bytes_accessed=8 * fields * cols * rows * width, transcendentals=0),
-    )(place, m, background)
+    )(place, *kept(m), background)
     an, as_, ac, packed = pl.pallas_call(
         functools.partial(outer_kernel, nlat=nlat),
         out_shape=(pltpu.VMEM((fields, pairs, width), BF16), pltpu.VMEM((fields, pairs, width), BF16),

time: 45.1 us -> 43.5 us (0.965)
  Pallas kernels: 19.4 us -> 18.2 us
    pallas_call x1, Pallas kernels: 6.19 us -> 4.93 us  [local(): pl.pallas_call(functools.partial(inner_kernel, nlat=nlat), out_shape=(plt...]
    ppermute x7, starting transfers between devices: 7.68 us -> 7.17 us  [partner(): return lax.ppermute(gram, ('lon', 'lat'), pairs)]
  transfers between devices with their start and end apart: 13 -> 13, of which waited for: 6 -> 7; matrix products, arithmetic and copies ran while one was open for 0% -> 0% of each run, Pallas kernels for 14% -> 11%
where the time goes in v5:
time: 43.5 us; the launch traced here: 43.3 us
  Pallas kernels  18.2 us (42%)
  starting transfers between devices  16.2 us (37%)
  waiting for transfers between devices  8.07 us (19%)
  between operations  0.75 us (2%)
    pallas_call x1, Pallas kernels, local(): pl.pallas_call(functools.partial(modes_kernel, total=float(fields * nlat...  8.53 us
    ppermute x7, waiting for transfers between devices, partner(): return lax.ppermute(gram, ('lon', 'lat'), pairs)  7.89 us
    ppermute x7, starting transfers between devices, partner(): return lax.ppermute(gram, ('lon', 'lat'), pairs)  7.17 us
    pallas_call x1, Pallas kernels, local(): pl.pallas_call(functools.partial(inner_kernel, nlat=nlat), out_shape=(plt...  4.93 us
    ppermute x1, starting transfers between devices, halos(): lon_b = lax.ppermute(lon_b, 'lon', by_lon_b)  3.56 us
    pallas_call x1, Pallas kernels, local(): pl.pallas_call(edges_kernel, out_shape=(pltpu.VMEM((fields, cols, rows, w...  2.98 us
    ppermute x1, starting transfers between devices, halos(): corner_a = lax.ppermute(jnp.where(even, high, low), both, by_lat_a)  2.96 us
    pallas_call x1, Pallas kernels, local(): pl.pallas_call(functools.partial(outer_kernel, nlat=nlat), out_shape=(plt...  1.73 us
  transfers between devices with their start and end apart: 13, of which 7 were waited for; matrix products, arithmetic and copies ran while one was open for 0% of the time, Pallas kernels for 11%

profile of v5, /device:TPU:0, one launch (start us, length us, event | category | flops | bytes accessed | tf_op | source)
XLA Modules:
  0.0 43.3 jit_solution(2035882511566231439)
XLA Ops:
  0.6 0.0 copy-start
  0.6 0.1 pad_add_fusion.place_ref
  0.7 3.0 %shard_map.41 = (bf16[3,180,32,128]{3,2,1,0:T(8,128)(2,1)S(1)}, bf16[3,8,32,128]{3,2,1,0:T(8,128)(2,1)S(1)}, f32[8,128]{1,0:T(8,128)S(1)}, bf16[3,2,32,128]{3,2,...) custom-call(s32[2]{0:T(128)S(1)} %pad_add_fusion.place_ref, ...), custom_call_target="tpu_custom_call" | custom-call | tf_op jit(solution)/shard_map/pallas_call | solution.py:405
  3.7 0.5 %collective-permute-start = (bf16[3,2,32,128]{3,2,1,0:T(8,128)(2,1)S(1)}, bf16[3,2,32,128]{3,2,1,0:T(8,128)(2,1)S(1)}, u32[]{:S(2)}, u32[]{:S(2)}) collective-permute-start(bf16[3,2,32,128]{3,2,1,0:T(8,128)(2,1)S(1)} %get-tuple-element.23), channel_id=1, source_target_pairs={{0,4},{4,0},{8,12},{12,8},{16,20},{20,16},{24,28},{28,24},{1,5},{5... | collective-permute-start | bytes 147464 | tf_op jit(solution)/shard_map/ppermute | solution.py:358
  4.2 3.6 %collective-permute-start.1 = (bf16[3,2,32,128]{3,2,1,0:T(8,128)(2,1)S(1)}, bf16[3,2,32,128]{3,2,1,0:T(8,128)(2,1)S(1)}, u32[]{:S(2)}, u32[]{:S(2)}) collective-permute-start(bf16[3,2,32,128]{3,2,1,0:T(8,128)(2,1)S(1)} %get-tuple-element.24), channel_id=1, source_target_pairs={{0,28},{4,8},{8,4},{12,16},{16,12},{20,24},{24,20},{28,0},{1,29},{... | collective-permute-start | bytes 147464 | tf_op jit(solution)/shard_map/ppermute | solution.py:357
  7.8 1.6 %collective-permute-start.2 = (bf16[3,360,128]{2,1,0:T(8,128)(2,1)S(1)}, bf16[3,360,128]{2,1,0:T(8,128)(2,1)S(1)}, u32[]{:S(2)}, u32[]{:S(2)}) collective-permute-start(bf16[3,360,128]{2,1,0:T(8,128)(2,1)S(1)} %get-tuple-element.25), channel_id=1, source_target_pairs={{0,1},{1,0},{2,3},{3,2},{4,5},{5,4},{6,7},{7,6},{8,9},{9,8},{10,11... | collective-permute-start | bytes 829448 | tf_op jit(solution)/shard_map/ppermute | solution.py:356
  9.4 0.0 collective-permute-start.3
  9.4 0.0 collective-permute-done.lon_a_ref
  9.4 0.2 collective-permute-done.1.lon_b_ref
  9.6 0.4 collective-permute-start.5
  10.0 3.0 %collective-permute-start.4 = (bf16[3,8,128]{2,1,0:T(8,128)(2,1)S(1)}, bf16[3,8,128]{2,1,0:T(8,128)(2,1)S(1)}, u32[]{:S(2)}, u32[]{:S(2)}) collective-permute-start(bf16[3,8,128]{2,1,0:T(8,128)(2,1)S(1)} %get-tuple-element.39), channel_id=1, source_target_pairs={{0,1},{1,0},{2,3},{3,2},{4,5},{5,4},{6,7},{7,6},{8,9},{9,8},{10,11... | collective-permute-start | bytes 18440 | tf_op jit(solution)/shard_map/ppermute | solution.py:364
  13.0 0.0 copy-done
  13.0 4.9 %shard_map.42 = (bf16[3,180,32,128]{3,2,1,0:T(8,128)(2,1)S(1)}, f32[3,360,128]{2,1,0:T(8,128)S(1)}, f32[3,360,128]{2,1,0:T(8,128)S(1)}, f32[128,128]{1,0:T(8,128)S(1)}) custom-call(s32[2]{0:T(128)S(1)} %pad_add_fusion.place_ref, bf16[3,180,32,128]{3,2,1,0:T(8,128)(2,1)S(1)} %get-tuple-element.19.m_ref, bf16[3,32,180]{2,1,0:T(8,128)(2,1)S(1)} %copy-done), custom_call_target="tpu_custom_call" | custom-call | flops 4529848320 | bytes 17694720 | tf_op jit(solution)/shard_map/pallas_call | solution.py:417
  17.9 0.0 collective-permute-done.5.corner_b_ref
  17.9 0.0 collective-permute-done.4.corner_a_ref
  17.9 0.0 collective-permute-done.2.lat_a_ref
  17.9 0.0 collective-permute-done.3.lat_b_ref
  18.0 1.7 %shard_map.43 = (bf16[3,360,128]{2,1,0:T(8,128)(2,1)S(1)}, bf16[3,360,128]{2,1,0:T(8,128)(2,1)S(1)}, bf16[3,4,32,128]{3,2,1,0:T(8,128)(2,1)S(1)}, f32[80,128]{1,0:T(8,128)S(1)}) custom-call(s32[2]{0:T(128)S(1)} %pad_add_fusion.place_ref, f32[3,360,128]{2,1,0:T(8,128)S(1)} %get-tuple-element.20.en_ref, f32[3,360,128]{2,1,0:T(8,128)S(1)} %get-tuple-element.21.es_ref, ...), custom_call_target="tpu_custom_call" | custom-call | tf_op jit(solution)/shard_map/pallas_call | solution.py:429
  19.7 0.1 collective-permute-start.6
  19.8 1.2 %collective-permute-done.6 = f32[80,128]{1,0:T(8,128)S(1)} collective-permute-done((f32[80,128]{1,0:T(8,128)S(1)}, f32[80,128]{1,0:T(8,128)S(1)}, u32[]{:S(2)}, u32[]{:S(2)}) %collective-permute-start.6) | collective-permute-done | bytes 40992 | tf_op jit(solution)/shard_map/ppermute | solution.py:373
  21.0 0.9 %collective-permute-start.9 = (f32[80,128]{1,0:T(8,128)S(1)}, f32[80,128]{1,0:T(8,128)S(1)}, u32[]{:S(2)}, u32[]{:S(2)}) collective-permute-start(f32[80,128]{1,0:T(8,128)S(1)} %add.21), channel_id=1, source_target_pairs={{0,13},{1,12},{2,15},{3,14},{4,9},{5,8},{6,11},{7,10},{8,5},{9,4},... | collective-permute-start | bytes 122888 | tf_op jit(solution)/shard_map/ppermute | solution.py:373
  21.9 1.3 %collective-permute-start.8 = (f32[80,128]{1,0:T(8,128)S(1)}, f32[80,128]{1,0:T(8,128)S(1)}, u32[]{:S(2)}, u32[]{:S(2)}) collective-permute-start(f32[80,128]{1,0:T(8,128)S(1)} %add.21), channel_id=1, source_target_pairs={{0,5},{1,4},{2,7},{3,6},{4,1},{5,0},{6,3},{7,2},{8,13},{9,12},{10,... | collective-permute-start | bytes 122888 | tf_op jit(solution)/shard_map/ppermute | solution.py:373
  23.2 0.8 %collective-permute-start.7 = (f32[80,128]{1,0:T(8,128)S(1)}, f32[80,128]{1,0:T(8,128)S(1)}, u32[]{:S(2)}, u32[]{:S(2)}) collective-permute-start(f32[80,128]{1,0:T(8,128)S(1)} %add.21), channel_id=1, source_target_pairs={{0,12},{1,13},{2,14},{3,15},{4,8},{5,9},{6,10},{7,11},{8,4},{9,5},... | collective-permute-start | bytes 122888 | tf_op jit(solution)/shard_map/ppermute | solution.py:373
  24.0 1.4 %collective-permute-done.9 = f32[80,128]{1,0:T(8,128)S(1)} collective-permute-done((f32[80,128]{1,0:T(8,128)S(1)}, f32[80,128]{1,0:T(8,128)S(1)}, u32[]{:S(2)}, u32[]{:S(2)}) %collective-permute-start.9) | collective-permute-done | bytes 40992 | tf_op jit(solution)/shard_map/ppermute | solution.py:373
  25.4 0.3 collective-permute-done.8
  25.7 0.9 %collective-permute-done.7 = f32[80,128]{1,0:T(8,128)S(1)} collective-permute-done((f32[80,128]{1,0:T(8,128)S(1)}, f32[80,128]{1,0:T(8,128)S(1)}, u32[]{:S(2)}, u32[]{:S(2)}) %collective-permute-start.7) | collective-permute-done | bytes 40992 | tf_op jit(solution)/shard_map/ppermute | solution.py:373
  26.6 2.8 %collective-permute-start.12 = (f32[80,128]{1,0:T(8,128)S(1)}, f32[80,128]{1,0:T(8,128)S(1)}, u32[]{:S(2)}, u32[]{:S(2)}) collective-permute-start(f32[80,128]{1,0:T(8,128)S(1)} %add_add_fusion.1), channel_id=1, source_target_pairs={{0,22},{1,23},{2,20},{3,21},{4,18},{5,19},{6,16},{7,17},{8,30},{9,... | collective-permute-start | bytes 122888 | tf_op jit(solution)/shard_map/ppermute | solution.py:373
  29.4 0.9 %collective-permute-start.11 = (f32[80,128]{1,0:T(8,128)S(1)}, f32[80,128]{1,0:T(8,128)S(1)}, u32[]{:S(2)}, u32[]{:S(2)}) collective-permute-start(f32[80,128]{1,0:T(8,128)S(1)} %add_add_fusion.1), channel_id=1, source_target_pairs={{0,6},{1,7},{2,4},{3,5},{4,2},{5,3},{6,0},{7,1},{8,14},{9,15},{10,... | collective-permute-start | bytes 122888 | tf_op jit(solution)/shard_map/ppermute | solution.py:373
  30.4 0.4 collective-permute-start.10
  30.8 2.2 %collective-permute-done.12 = f32[80,128]{1,0:T(8,128)S(1)} collective-permute-done((f32[80,128]{1,0:T(8,128)S(1)}, f32[80,128]{1,0:T(8,128)S(1)}, u32[]{:S(2)}, u32[]{:S(2)}) %collective-permute-start.12) | collective-permute-done | bytes 40992 | tf_op jit(solution)/shard_map/ppermute | solution.py:373
  33.0 1.8 %collective-permute-done.11 = f32[80,128]{1,0:T(8,128)S(1)} collective-permute-done((f32[80,128]{1,0:T(8,128)S(1)}, f32[80,128]{1,0:T(8,128)S(1)}, u32[]{:S(2)}, u32[]{:S(2)}) %collective-permute-start.11) | collective-permute-done | bytes 40992 | tf_op jit(solution)/shard_map/ppermute | solution.py:373
  34.8 0.0 collective-permute-done.10
  34.8 8.5 %shard_map.44 = (f32[3,180,32,128]{3,2,1,0:T(8,128)}, f32[128,128]{1,0:T(8,128)}) custom-call(f32[80,128]{1,0:T(8,128)S(1)} %add_add_fusion.p_ref, bf16[3,360,128]{2,1,0:T(8,128)(2,1)S(1)} %get-tuple-element.30.an_ref, bf16[3,360,128]{2,1,0:T(8,128)(2,1)S(1)} %get-tuple-element.31.as_ref, bf16[3,4,32,128]{3,2,1,0:T(8,128)(2,1)S(1)} %get-tuple-element.32.ac_ref, ...), custom_call_target="tpu_custom_call" | custom-call | tf_op jit(solution)/shard_map/pallas_call | solution.py:440
  (8 shorter events, 0.1 us)
Async XLA Ops:
  0.6 12.4 %copy-start = (bf16[3,32,180]{2,1,0:T(8,128)(2,1)S(1)}, bf16[3,32,180]{2,1,0:T(8,128)(2,1)}, u32[]{:S(2)}) copy-start(bf16[3,32,180]{2,1,0:T(8,128)(2,1)} %bg_ref.3) | copy-start | bytes 103684
  3.7 5.7 %collective-permute-start = (bf16[3,2,32,128]{3,2,1,0:T(8,128)(2,1)S(1)}, bf16[3,2,32,128]{3,2,1,0:T(8,128)(2,1)S(1)}, u32[]{:S(2)}, u32[]{:S(2)}) collective-permute-start(bf16[3,2,32,128]{3,2,1,0:T(8,128)(2,1)S(1)} %get-tuple-element.23), channel_id=1, source_target_pairs={{0,4},{4,0},{8,12},{12,8},{16,20},{20,16},{24,28},{28,24},{1,5},{5... | collective-permute-start | bytes 147464 | tf_op jit(solution)/shard_map/ppermute | solution.py:358
  4.2 5.3 %collective-permute-start.1 = (bf16[3,2,32,128]{3,2,1,0:T(8,128)(2,1)S(1)}, bf16[3,2,32,128]{3,2,1,0:T(8,128)(2,1)S(1)}, u32[]{:S(2)}, u32[]{:S(2)}) collective-permute-start(bf16[3,2,32,128]{3,2,1,0:T(8,128)(2,1)S(1)} %get-tuple-element.24), channel_id=1, source_target_pairs={{0,28},{4,8},{8,4},{12,16},{16,12},{20,24},{24,20},{28,0},{1,29},{... | collective-permute-start | bytes 147464 | tf_op jit(solution)/shard_map/ppermute | solution.py:357
  7.8 10.2 %collective-permute-start.2 = (bf16[3,360,128]{2,1,0:T(8,128)(2,1)S(1)}, bf16[3,360,128]{2,1,0:T(8,128)(2,1)S(1)}, u32[]{:S(2)}, u32[]{:S(2)}) collective-permute-start(bf16[3,360,128]{2,1,0:T(8,128)(2,1)S(1)} %get-tuple-element.25), channel_id=1, source_target_pairs={{0,1},{1,0},{2,3},{3,2},{4,5},{5,4},{6,7},{7,6},{8,9},{9,8},{10,11... | collective-permute-start | bytes 829448 | tf_op jit(solution)/shard_map/ppermute | solution.py:356
  9.4 8.6 %collective-permute-start.3 = (bf16[3,360,128]{2,1,0:T(8,128)(2,1)S(1)}, bf16[3,360,128]{2,1,0:T(8,128)(2,1)S(1)}, u32[]{:S(2)}, u32[]{:S(2)}) collective-permute-start(bf16[3,360,128]{2,1,0:T(8,128)(2,1)S(1)} %get-tuple-element.26), channel_id=1, source_target_pairs={{0,4},{1,2},{2,1},{3,7},{4,0},{5,6},{6,5},{7,3},{8,12},{9,10},{10,... | collective-permute-start | bytes 829448 | tf_op jit(solution)/shard_map/ppermute | solution.py:355
  9.6 8.3 %collective-permute-start.5 = (bf16[3,8,128]{2,1,0:T(8,128)(2,1)S(1)}, bf16[3,8,128]{2,1,0:T(8,128)(2,1)S(1)}, u32[]{:S(2)}, u32[]{:S(2)}) collective-permute-start(bf16[3,8,128]{2,1,0:T(8,128)(2,1)S(1)} %get-tuple-element.38), channel_id=1, source_target_pairs={{0,4},{1,2},{2,1},{3,7},{4,0},{5,6},{6,5},{7,3},{8,12},{9,10},{10,... | collective-permute-start | bytes 18440 | tf_op jit(solution)/shard_map/ppermute | solution.py:363
  10.0 7.9 %collective-permute-start.4 = (bf16[3,8,128]{2,1,0:T(8,128)(2,1)S(1)}, bf16[3,8,128]{2,1,0:T(8,128)(2,1)S(1)}, u32[]{:S(2)}, u32[]{:S(2)}) collective-permute-start(bf16[3,8,128]{2,1,0:T(8,128)(2,1)S(1)} %get-tuple-element.39), channel_id=1, source_target_pairs={{0,1},{1,0},{2,3},{3,2},{4,5},{5,4},{6,7},{7,6},{8,9},{9,8},{10,11... | collective-permute-start | bytes 18440 | tf_op jit(solution)/shard_map/ppermute | solution.py:364
  19.7 1.3 %collective-permute-start.6 = (f32[80,128]{1,0:T(8,128)S(1)}, f32[80,128]{1,0:T(8,128)S(1)}, u32[]{:S(2)}, u32[]{:S(2)}) collective-permute-start(f32[80,128]{1,0:T(8,128)S(1)} %get-tuple-element.29), channel_id=1, source_target_pairs={{0,4},{1,5},{2,6},{3,7},{4,0},{5,1},{6,2},{7,3},{8,12},{9,13},{10,... | collective-permute-start | bytes 122888 | tf_op jit(solution)/shard_map/ppermute | solution.py:373
  21.0 4.4 %collective-permute-start.9 = (f32[80,128]{1,0:T(8,128)S(1)}, f32[80,128]{1,0:T(8,128)S(1)}, u32[]{:S(2)}, u32[]{:S(2)}) collective-permute-start(f32[80,128]{1,0:T(8,128)S(1)} %add.21), channel_id=1, source_target_pairs={{0,13},{1,12},{2,15},{3,14},{4,9},{5,8},{6,11},{7,10},{8,5},{9,4},... | collective-permute-start | bytes 122888 | tf_op jit(solution)/shard_map/ppermute | solution.py:373
  21.9 3.9 %collective-permute-start.8 = (f32[80,128]{1,0:T(8,128)S(1)}, f32[80,128]{1,0:T(8,128)S(1)}, u32[]{:S(2)}, u32[]{:S(2)}) collective-permute-start(f32[80,128]{1,0:T(8,128)S(1)} %add.21), channel_id=1, source_target_pairs={{0,5},{1,4},{2,7},{3,6},{4,1},{5,0},{6,3},{7,2},{8,13},{9,12},{10,... | collective-permute-start | bytes 122888 | tf_op jit(solution)/shard_map/ppermute | solution.py:373
  23.2 3.4 %collective-permute-start.7 = (f32[80,128]{1,0:T(8,128)S(1)}, f32[80,128]{1,0:T(8,128)S(1)}, u32[]{:S(2)}, u32[]{:S(2)}) collective-permute-start(f32[80,128]{1,0:T(8,128)S(1)} %add.21), channel_id=1, source_target_pairs={{0,12},{1,13},{2,14},{3,15},{4,8},{5,9},{6,10},{7,11},{8,4},{9,5},... | collective-permute-start | bytes 122888 | tf_op jit(solution)/shard_map/ppermute | solution.py:373
  26.6 6.3 %collective-permute-start.12 = (f32[80,128]{1,0:T(8,128)S(1)}, f32[80,128]{1,0:T(8,128)S(1)}, u32[]{:S(2)}, u32[]{:S(2)}) collective-permute-start(f32[80,128]{1,0:T(8,128)S(1)} %add_add_fusion.1), channel_id=1, source_target_pairs={{0,22},{1,23},{2,20},{3,21},{4,18},{5,19},{6,16},{7,17},{8,30},{9,... | collective-permute-start | bytes 122888 | tf_op jit(solution)/shard_map/ppermute | solution.py:373
  29.4 5.3 %collective-permute-start.11 = (f32[80,128]{1,0:T(8,128)S(1)}, f32[80,128]{1,0:T(8,128)S(1)}, u32[]{:S(2)}, u32[]{:S(2)}) collective-permute-start(f32[80,128]{1,0:T(8,128)S(1)} %add_add_fusion.1), channel_id=1, source_target_pairs={{0,6},{1,7},{2,4},{3,5},{4,2},{5,3},{6,0},{7,1},{8,14},{9,15},{10,... | collective-permute-start | bytes 122888 | tf_op jit(solution)/shard_map/ppermute | solution.py:373
  30.4 4.4 %collective-permute-start.10 = (f32[80,128]{1,0:T(8,128)S(1)}, f32[80,128]{1,0:T(8,128)S(1)}, u32[]{:S(2)}, u32[]{:S(2)}) collective-permute-start(f32[80,128]{1,0:T(8,128)S(1)} %add_add_fusion.1), channel_id=1, source_target_pairs={{0,20},{1,21},{2,22},{3,23},{4,16},{5,17},{6,18},{7,19},{8,28},{9,... | collective-permute-start | bytes 122888 | tf_op jit(solution)/shard_map/ppermute | solution.py:373

commit v6 on v5

--- a/solution.py
+++ b/solution.py
@@ -52,33 +52,7 @@
     return lax.dot_general(a, a, (((0,), (0,)), ((), ())), preferred_element_type=F32)
 
 
-def edges_kernel(place_ref, m_hbm, m_ref, near_ref, even_ref, lon_a_ref, lon_b_ref, lat_a_ref, lat_b_ref, low_ref, high_ref,
-                 sems):
-    fields, cols, rows, width = m_ref.shape
-    lon_even = lax.rem(place_ref[0], 2) == 0
-    lat_even = lax.rem(place_ref[1], 2) == 0
-    even_ref[...] = jnp.where(jnp.full(even_ref.shape, lat_even, jnp.bool_), 1.0, 0.0)
-    copies = [pltpu.make_async_copy(m_hbm.at[f], m_ref.at[f], sems.at[f]) for f in range(fields)]
-    for copy in copies:
-        copy.start()
-    for f in range(fields):
-        copies[f].wait()
-        first, last = m_ref[f, 0:2], m_ref[f, cols - 2:cols]
-        near_ref[f, 0:4] = m_ref[f, 0:4]
-        near_ref[f, 4:8] = m_ref[f, cols - 4:cols]
-        lon_a_ref[f] = jnp.where(lon_even, last, first)
-        lon_b_ref[f] = jnp.where(lon_even, first, last)
-        for l in range(cols):
-            low_ref[2 * l:2 * l + 2] = m_ref[f, l, 0:16].astype(F32)[0:2]
-            high_ref[2 * l:2 * l + 2] = m_ref[f, l, rows - 16:rows].astype(F32)[14:16]
-        low, high = low_ref[...], high_ref[...]
-        lat_a_ref[f] = jnp.where(lat_even, high, low).astype(BF16)
-        lat_b_ref[f] = jnp.where(lat_even, low, high).astype(BF16)
-
-
-def inner_kernel(place_ref, m_ref, bg_ref, a_ref, en_ref, es_ref, g_ref, mat_ref, coef_ref, entries_ref, *, nlat):
-    cols, rows = m_ref.shape[1], m_ref.shape[2]
-    wide = 2
+def tables(place_ref, mat_ref, coef_ref, edge_ref, entries_ref, rows, nlat):
     nt = rows // 8
     first = place_ref[1] * rows
     sub = sublane()
@@ -110,6 +84,58 @@
                 entries_ref[pl.ds(128 + rows * i + 8 * t, 8), at[1]] = entry - high
     mat_ref[...] = entries_ref[...].astype(BF16)
 
+    def splat(row):
+        return jnp.full(TILE, row, jnp.int32)
+
+    for side, (near, halo, par, exists) in enumerate(((0, -1, 0, first > 0), (rows - 1, rows, 1, first + rows < nlat))):
+        c0, k0, _ = scaled_coefs(splat(first + near), nlat)
+        c1, k1, _ = scaled_coefs(splat(first + halo), nlat)
+        _, _, w = scaled_coefs(splat(first + near) + (sub % 2 - par), nlat)
+        outermost = sub % 2 == par
+        edge_ref[side, 0] = jnp.where(outermost, c0 + c1, 0.0)
+        edge_ref[side, 1] = jnp.where(outermost, k0 + k1, 0.0)
+        edge_ref[side, 2] = jnp.where(exists, 0.04 * w, 0.0)
+    for t in range(nt):
+        edge_ref[2, t], edge_ref[3, t], edge_ref[4, t] = scaled_coefs(first + 8 * t + sub, nlat)
+    beyond = first + rows + jnp.where(sub < 4, sub, sub - 8 - rows)
+    real = (beyond >= 0) & (beyond < nlat)
+    c, k, _ = scaled_coefs(beyond, nlat)
+    edge_ref[2, nt], edge_ref[3, nt] = jnp.where(real, c, 0.0), jnp.where(real, k, 0.0)
+    edge_ref[4, nt] = jnp.where(real, 1.0, 0.0)
+
+
+def edges_kernel(place_ref, m_hbm, m_ref, near_ref, even_ref, mat_ref, coef_ref, edge_ref, lon_a_ref, lon_b_ref,
+                 lat_a_ref, lat_b_ref, entries_ref, low_ref, high_ref, sems, *, nlat):
+    fields, cols, rows, width = m_ref.shape
+    lon_even = lax.rem(place_ref[0], 2) == 0
+    lat_even = lax.rem(place_ref[1], 2) == 0
+    even_ref[...] = jnp.where(jnp.full(even_ref.shape, lat_even, jnp.bool_), 1.0, 0.0)
+    pieces = [(f, lo, hi) for f in range(fields) for lo, hi in ((0, cols // 16 * 8), (cols // 16 * 8, cols))]
+    copies = [pltpu.make_async_copy(m_hbm.at[f, pl.ds(lo, hi - lo)], m_ref.at[f, pl.ds(lo, hi - lo)], sems.at[i])
+              for i, (f, lo, hi) in enumerate(pieces)]
+    for copy in copies:
+        copy.start()
+    tables(place_ref, mat_ref, coef_ref, edge_ref, entries_ref, rows, nlat)
+    for copy, (f, lo, hi) in zip(copies, pieces):
+        copy.wait()
+        for l in range(lo, hi):
+            low_ref[f, 2 * l:2 * l + 2] = m_ref[f, l, 0:16].astype(F32)[0:2]
+            high_ref[f, 2 * l:2 * l + 2] = m_ref[f, l, rows - 16:rows].astype(F32)[14:16]
+        low, high = low_ref[f, 2 * lo:2 * hi], high_ref[f, 2 * lo:2 * hi]
+        lat_a_ref[f, 2 * lo:2 * hi] = jnp.where(lat_even, high, low).astype(BF16)
+        lat_b_ref[f, 2 * lo:2 * hi] = jnp.where(lat_even, low, high).astype(BF16)
+        if hi == cols:
+            first, last = m_ref[f, 0:2], m_ref[f, cols - 2:cols]
+            near_ref[f, 0:4] = m_ref[f, 0:4]
+            near_ref[f, 4:8] = m_ref[f, cols - 4:cols]
+            lon_a_ref[f] = jnp.where(lon_even, last, first)
+            lon_b_ref[f] = jnp.where(lon_even, first, last)
+
+
+def inner_kernel(m_ref, bg_ref, mat_ref, coef_ref, a_ref, en_ref, es_ref, g_ref):
+    cols, rows = m_ref.shape[1], m_ref.shape[2]
+    wide = 2
+    nt = rows // 8
     @pl.loop(0, m_ref.shape[0])
     def _(f):
         ground = bg_ref[f].astype(F32)
@@ -153,7 +179,7 @@
 
 
 def outer_kernel(place_ref, en_ref, es_ref, near_ref, lon_a_ref, lon_b_ref, lat_a_ref, lat_b_ref, corner_a_ref,
-                 corner_b_ref, bg_ref, gin_ref, an_ref, as_ref, ac_ref, g_ref, pad_ref, x_ref, *, nlat):
+                 corner_b_ref, bg_ref, gin_ref, table_ref, an_ref, as_ref, ac_ref, g_ref, pad_ref, x_ref, *, nlat):
     fields, pairs = lat_a_ref.shape[0], lat_a_ref.shape[1]
     rows, cols = bg_ref.shape[1], bg_ref.shape[2]
     first = place_ref[1] * rows
@@ -164,21 +190,10 @@
     sub = sublane()
     gram = gin_ref[...]
 
-    def splat(row):
-        return jnp.full((8, 128), row, jnp.int32)
-
-    for e_ref, a_h_ref, b_h_ref, a_c_ref, b_c_ref, use_b, exists, out_ref, near, halo, par, sign, at in (
-            (en_ref, lat_a_ref, lat_b_ref, corner_a_ref, corner_b_ref, lat_even, has_north, an_ref, 0, -1, 0, 1, rows + 6),
-            (es_ref, lat_b_ref, lat_a_ref, corner_b_ref, corner_a_ref, lat_even, has_south, as_ref, rows - 1, rows, 1, -1,
-             rows)):
-        c0, k0, _ = scaled_coefs(splat(first + near), nlat)
-        c1, k1, _ = scaled_coefs(splat(first + halo), nlat)
-        _, _, wa = scaled_coefs(splat(first + near) + (sub % 2 - par), nlat)
-        many = pairs // 8
-        outermost = sub % 2 == par
-        c = jnp.concatenate([jnp.where(outermost, c0 + c1, 0.0)] * many, axis=0)
-        k = jnp.concatenate([jnp.where(outermost, k0 + k1, 0.0)] * many, axis=0)
-        w = jnp.concatenate([jnp.where(exists, 0.04 * wa, 0.0)] * many, axis=0)
+    for e_ref, a_h_ref, b_h_ref, a_c_ref, b_c_ref, use_b, exists, out_ref, par, sign, at in (
+            (en_ref, lat_a_ref, lat_b_ref, corner_a_ref, corner_b_ref, lat_even, has_north, an_ref, 0, 1, rows + 6),
+            (es_ref, lat_b_ref, lat_a_ref, corner_b_ref, corner_a_ref, lat_even, has_south, as_ref, 1, -1, rows)):
+        c, k, w = (jnp.concatenate([table_ref[par, i]] * (pairs // 8), axis=0) for i in range(3))
         for f in range(fields):
             h = jnp.where(use_b, b_h_ref[f], a_h_ref[f]).astype(F32)
             pad = pad_ref.at[fields * par + f]
@@ -212,13 +227,8 @@
             x_ref[f, l, 0:rows] = jnp.where(lon_even, b, a)
             x_ref[f, 10 + l, 0:rows] = jnp.where(lon_even, a, b)
 
-    coefs = [scaled_coefs(first + 8 * t + sub, nlat) for t in range(nt)]
-    beyond = first + rows + jnp.where(sub < 4, sub, sub - 8 - rows)
-    c, k, _ = scaled_coefs(beyond, nlat)
-    real = (beyond >= 0) & (beyond < nlat)
-    vc = [x[0] for x in coefs] + [jnp.where(real, c, 0.0)]
-    vk = [x[1] for x in coefs] + [jnp.where(real, k, 0.0)]
-    one = jnp.where(real, 1.0, 0.0)
+    vc, vk = ([table_ref[2 + i, t] for t in range(nt + 1)] for i in range(2))
+    one = table_ref[4, nt]
     for f in range(fields):
         bg = bg_ref[f].astype(F32)
         for side in range(2):
@@ -235,7 +245,7 @@
                 for t in range(nt):
                     y = ns[t] + vc[t] * v[l + 1][t] + vk[t] * (v[l][t] + v[l + 2][t])
                     b = jnp.broadcast_to(bg[8 * t:8 * t + 8, at:at + 1], TILE)
-                    parts.append((0.04 * y - b) * coefs[t][2])
+                    parts.append((0.04 * y - b) * table_ref[4, t])
                 ac_ref[f, 2 * side + l] = jnp.concatenate(parts, axis=0).astype(BF16)
     gram = gram + gram_of(ac_ref[...].reshape(-1, 128))
     g_ref[...] = pack(gram)
@@ -402,40 +412,39 @@
         return [pltpu.with_memory_space_constraint(x, pltpu.VMEM) for x in xs]
 
     m = pltpu.with_memory_space_constraint(jnp.transpose(members, (0, 2, 1, 3)), pltpu.HBM)
-    m, near, even, *sent = pl.pallas_call(
-        edges_kernel,
+    m, near, even, mat, coef, table, *sent = pl.pallas_call(
+        functools.partial(edges_kernel, nlat=nlat),
         out_shape=(pltpu.VMEM((fields, cols, rows, width), BF16), pltpu.VMEM((fields, 8, rows, width), BF16),
-                   pltpu.VMEM(TILE, F32)) + (pltpu.VMEM((fields, 2, rows, width), BF16),) * 2
+                   pltpu.VMEM(TILE, F32), pltpu.VMEM((256, 256), BF16), pltpu.VMEM((4, rows // 8, 8, 128), F32),
+                   pltpu.VMEM((5, rows // 8 + 1, 8, 128), F32)) + (pltpu.VMEM((fields, 2, rows, width), BF16),) * 2
         + (pltpu.VMEM((fields, pairs, width), BF16),) * 2,
         in_specs=[smem, hbm],
-        out_specs=(vmem,) * 7,
-        scratch_shapes=[pltpu.VMEM((pairs, width), F32), pltpu.VMEM((pairs, width), F32),
-                        pltpu.SemaphoreType.DMA((fields,))],
+        out_specs=(vmem,) * 10,
+        scratch_shapes=[pltpu.VMEM((256, 256), F32), pltpu.VMEM((fields, pairs, width), F32),
+                        pltpu.VMEM((fields, pairs, width), F32), pltpu.SemaphoreType.DMA((2 * fields,))],
         compiler_params=params,
     )(place, m)
     beside = halos(even, *sent)
     a, en, es, gram = pl.pallas_call(
-        functools.partial(inner_kernel, nlat=nlat),
+        inner_kernel,
         out_shape=(pltpu.VMEM((fields, cols, rows, width), BF16), pltpu.VMEM((fields, pairs, width), F32),
                    pltpu.VMEM((fields, pairs, width), F32), pltpu.VMEM((width, width), F32)),
-        in_specs=[smem, vmem, vmem],
+        in_specs=[vmem] * 4,
         out_specs=(vmem,) * 4,
-        scratch_shapes=[pltpu.VMEM((256, 256), BF16), pltpu.VMEM((4, rows // 8, 8, 128), F32),
-                        pltpu.VMEM((256, 256), F32)],
         compiler_params=params,
         cost_estimate=pl.CostEstimate(flops=16 * fields * cols * rows * width * width,
                                       bytes_accessed=8 * fields * cols * rows * width, transcendentals=0),
-    )(place, *kept(m), background)
+    )(*kept(m), background, *kept(mat, coef))
     an, as_, ac, packed = pl.pallas_call(
         functools.partial(outer_kernel, nlat=nlat),
         out_shape=(pltpu.VMEM((fields, pairs, width), BF16), pltpu.VMEM((fields, pairs, width), BF16),
                    pltpu.VMEM((fields, 4, rows, width), BF16), pltpu.VMEM((80, width), F32)),
-        in_specs=[smem] + [vmem] * 11,
+        in_specs=[smem] + [vmem] * 12,
         out_specs=(vmem,) * 4,
         scratch_shapes=[pltpu.VMEM((2 * fields, pairs + 16, width), F32),
                         pltpu.VMEM((fields, 12, rows + 8, width), F32)],
         compiler_params=params,
-    )(place, *kept(en, es, near, *beside, background, gram))
+    )(place, *kept(en, es, near, *beside, background, gram, table))
     packed = total_gram(packed)
     modes, r_factor = pl.pallas_call(
         functools.partial(modes_kernel, total=float(fields * nlat * cols * lon)),

time: 43.5 us -> 42.6 us (0.979)
  Pallas kernels: 18.2 us -> 17.3 us
    pallas_call x2, Pallas kernels: 7.9 us -> 7.13 us  [the longest x1 4.23 us: local(): pl.pallas_call(inner_kernel, out_shape=(pltpu.VMEM((fields, cols, rows, w...]
  transfers between devices with their start and end apart: 13 -> 13, of which waited for: 7 -> 7; matrix products, arithmetic and copies ran while one was open for 0% -> 0% of each run, Pallas kernels for 11% -> 10%
where the time goes in v6:
time: 42.6 us; the launch traced here: 42.5 us
  Pallas kernels  17.3 us (41%)
  starting transfers between devices  16.2 us (38%)
  waiting for transfers between devices  8.04 us (19%)
  between operations  0.75 us (2%)
    pallas_call x1, Pallas kernels, local(): pl.pallas_call(functools.partial(modes_kernel, total=float(fields * nlat...  8.53 us
    ppermute x7, waiting for transfers between devices, partner(): return lax.ppermute(gram, ('lon', 'lat'), pairs)  7.86 us
    ppermute x7, starting transfers between devices, partner(): return lax.ppermute(gram, ('lon', 'lat'), pairs)  7.17 us
    pallas_call x1, Pallas kernels, local(): pl.pallas_call(inner_kernel, out_shape=(pltpu.VMEM((fields, cols, rows, w...  4.23 us
    ppermute x1, starting transfers between devices, halos(): lon_b = lax.ppermute(lon_b, 'lon', by_lon_b)  3.56 us
    ppermute x1, starting transfers between devices, halos(): corner_a = lax.ppermute(jnp.where(even, high, low), both, by_lat_a)  2.96 us
    pallas_call x1, Pallas kernels, local(): pl.pallas_call(functools.partial(edges_kernel, nlat=nlat), out_shape=(plt...  2.9 us
    pallas_call x1, Pallas kernels, local(): pl.pallas_call(functools.partial(outer_kernel, nlat=nlat), out_shape=(plt...  1.68 us
  transfers between devices with their start and end apart: 13, of which 7 were waited for; matrix products, arithmetic and copies ran while one was open for 0% of the time, Pallas kernels for 10%

profile of v6, /device:TPU:0, one launch (start us, length us, event | category | flops | bytes accessed | tf_op | source)
XLA Modules:
  0.0 42.5 jit_solution(827751627317295140)
XLA Ops:
  0.6 0.0 copy-start
  0.6 0.1 pad_add_fusion.place_ref
  0.7 2.9 %shard_map.41 = (bf16[3,180,32,128]{3,2,1,0:T(8,128)(2,1)S(1)}, bf16[3,8,32,128]{3,2,1,0:T(8,128)(2,1)S(1)}, f32[8,128]{1,0:T(8,128)S(1)}, bf16[256,256]{1,0:T(8...) custom-call(s32[2]{0:T(128)S(1)} %pad_add_fusion.place_ref, ...), custom_call_target="tpu_custom_call" | custom-call | tf_op jit(solution)/shard_map/pallas_call | solution.py:415
  3.6 0.5 %collective-permute-start = (bf16[3,2,32,128]{3,2,1,0:T(8,128)(2,1)S(1)}, bf16[3,2,32,128]{3,2,1,0:T(8,128)(2,1)S(1)}, u32[]{:S(2)}, u32[]{:S(2)}) collective-permute-start(bf16[3,2,32,128]{3,2,1,0:T(8,128)(2,1)S(1)} %get-tuple-element.28), channel_id=1, source_target_pairs={{0,4},{4,0},{8,12},{12,8},{16,20},{20,16},{24,28},{28,24},{1,5},{5... | collective-permute-start | bytes 147464 | tf_op jit(solution)/shard_map/ppermute | solution.py:368
  4.1 3.6 %collective-permute-start.1 = (bf16[3,2,32,128]{3,2,1,0:T(8,128)(2,1)S(1)}, bf16[3,2,32,128]{3,2,1,0:T(8,128)(2,1)S(1)}, u32[]{:S(2)}, u32[]{:S(2)}) collective-permute-start(bf16[3,2,32,128]{3,2,1,0:T(8,128)(2,1)S(1)} %get-tuple-element.29), channel_id=1, source_target_pairs={{0,28},{4,8},{8,4},{12,16},{16,12},{20,24},{24,20},{28,0},{1,29},{... | collective-permute-start | bytes 147464 | tf_op jit(solution)/shard_map/ppermute | solution.py:367
  7.7 1.6 %collective-permute-start.2 = (bf16[3,360,128]{2,1,0:T(8,128)(2,1)S(1)}, bf16[3,360,128]{2,1,0:T(8,128)(2,1)S(1)}, u32[]{:S(2)}, u32[]{:S(2)}) collective-permute-start(bf16[3,360,128]{2,1,0:T(8,128)(2,1)S(1)} %get-tuple-element.30), channel_id=1, source_target_pairs={{0,1},{1,0},{2,3},{3,2},{4,5},{5,4},{6,7},{7,6},{8,9},{9,8},{10,11... | collective-permute-start | bytes 829448 | tf_op jit(solution)/shard_map/ppermute | solution.py:366
  9.3 0.0 collective-permute-start.3
  9.3 0.0 collective-permute-done.lon_a_ref
  9.3 0.2 collective-permute-done.1.lon_b_ref
  9.5 0.4 collective-permute-start.5
  9.9 3.0 %collective-permute-start.4 = (bf16[3,8,128]{2,1,0:T(8,128)(2,1)S(1)}, bf16[3,8,128]{2,1,0:T(8,128)(2,1)S(1)}, u32[]{:S(2)}, u32[]{:S(2)}) collective-permute-start(bf16[3,8,128]{2,1,0:T(8,128)(2,1)S(1)} %get-tuple-element.45), channel_id=1, source_target_pairs={{0,1},{1,0},{2,3},{3,2},{4,5},{5,4},{6,7},{7,6},{8,9},{9,8},{10,11... | collective-permute-start | bytes 18440 | tf_op jit(solution)/shard_map/ppermute | solution.py:374
  12.9 0.0 copy-done
  12.9 4.2 %shard_map.42 = (bf16[3,180,32,128]{3,2,1,0:T(8,128)(2,1)S(1)}, f32[3,360,128]{2,1,0:T(8,128)S(1)}, f32[3,360,128]{2,1,0:T(8,128)S(1)}, f32[128,128]{1,0:T(8,128)S(1)}) custom-call(bf16[3,180,32,128]{3,2,1,0:T(8,128)(2,1)S(1)} %get-tuple-element.22.m_ref, bf16[3,32,180]{2,1,0:T(8,128)(2,1)S(1)} %copy-done, bf16[256,256]{1,0:T(8,128)(2,1)S(1)} %get-tuple-element.23.mat_ref, ...), custom_call_target="tpu_custom_call" | custom-call | flops 4529848320 | bytes 17694720 | tf_op jit(solution)/shard_map/pallas_call | solution.py:428
  17.1 0.0 collective-permute-done.5.corner_b_ref
  17.2 0.0 collective-permute-done.4.corner_a_ref
  17.2 0.0 collective-permute-done.2.lat_a_ref
  17.2 0.0 collective-permute-done.3.lat_b_ref
  17.2 1.7 %shard_map.43 = (bf16[3,360,128]{2,1,0:T(8,128)(2,1)S(1)}, bf16[3,360,128]{2,1,0:T(8,128)(2,1)S(1)}, bf16[3,4,32,128]{3,2,1,0:T(8,128)(2,1)S(1)}, f32[80,128]{1,0:T(8,128)S(1)}) custom-call(s32[2]{0:T(128)S(1)} %pad_add_fusion.place_ref, f32[3,360,128]{2,1,0:T(8,128)S(1)} %get-tuple-element.25.en_ref, f32[3,360,128]{2,1,0:T(8,128)S(1)} %get-tuple-element.26.es_ref, ...), custom_call_target="tpu_custom_call" | custom-call | tf_op jit(solution)/shard_map/pallas_call | solution.py:438
  18.9 0.1 collective-permute-start.6
  19.0 1.2 %collective-permute-done.6 = f32[80,128]{1,0:T(8,128)S(1)} collective-permute-done((f32[80,128]{1,0:T(8,128)S(1)}, f32[80,128]{1,0:T(8,128)S(1)}, u32[]{:S(2)}, u32[]{:S(2)}) %collective-permute-start.6) | collective-permute-done | bytes 40992 | tf_op jit(solution)/shard_map/ppermute | solution.py:383
  20.2 1.6 %collective-permute-start.9 = (f32[80,128]{1,0:T(8,128)S(1)}, f32[80,128]{1,0:T(8,128)S(1)}, u32[]{:S(2)}, u32[]{:S(2)}) collective-permute-start(f32[80,128]{1,0:T(8,128)S(1)} %add.21), channel_id=1, source_target_pairs={{0,13},{1,12},{2,15},{3,14},{4,9},{5,8},{6,11},{7,10},{8,5},{9,4},... | collective-permute-start | bytes 122888 | tf_op jit(solution)/shard_map/ppermute | solution.py:383
  21.7 0.6 %collective-permute-start.8 = (f32[80,128]{1,0:T(8,128)S(1)}, f32[80,128]{1,0:T(8,128)S(1)}, u32[]{:S(2)}, u32[]{:S(2)}) collective-permute-start(f32[80,128]{1,0:T(8,128)S(1)} %add.21), channel_id=1, source_target_pairs={{0,5},{1,4},{2,7},{3,6},{4,1},{5,0},{6,3},{7,2},{8,13},{9,12},{10,... | collective-permute-start | bytes 122888 | tf_op jit(solution)/shard_map/ppermute | solution.py:383
  22.4 0.8 %collective-permute-start.7 = (f32[80,128]{1,0:T(8,128)S(1)}, f32[80,128]{1,0:T(8,128)S(1)}, u32[]{:S(2)}, u32[]{:S(2)}) collective-permute-start(f32[80,128]{1,0:T(8,128)S(1)} %add.21), channel_id=1, source_target_pairs={{0,12},{1,13},{2,14},{3,15},{4,8},{5,9},{6,10},{7,11},{8,4},{9,5},... | collective-permute-start | bytes 122888 | tf_op jit(solution)/shard_map/ppermute | solution.py:383
  23.1 1.4 %collective-permute-done.9 = f32[80,128]{1,0:T(8,128)S(1)} collective-permute-done((f32[80,128]{1,0:T(8,128)S(1)}, f32[80,128]{1,0:T(8,128)S(1)}, u32[]{:S(2)}, u32[]{:S(2)}) %collective-permute-start.9) | collective-permute-done | bytes 40992 | tf_op jit(solution)/shard_map/ppermute | solution.py:383
  24.6 0.6 %collective-permute-done.8 = f32[80,128]{1,0:T(8,128)S(1)} collective-permute-done((f32[80,128]{1,0:T(8,128)S(1)}, f32[80,128]{1,0:T(8,128)S(1)}, u32[]{:S(2)}, u32[]{:S(2)}) %collective-permute-start.8) | collective-permute-done | bytes 40992 | tf_op jit(solution)/shard_map/ppermute | solution.py:383
  25.2 0.6 %collective-permute-done.7 = f32[80,128]{1,0:T(8,128)S(1)} collective-permute-done((f32[80,128]{1,0:T(8,128)S(1)}, f32[80,128]{1,0:T(8,128)S(1)}, u32[]{:S(2)}, u32[]{:S(2)}) %collective-permute-start.7) | collective-permute-done | bytes 40992 | tf_op jit(solution)/shard_map/ppermute | solution.py:383
  25.8 2.9 %collective-permute-start.12 = (f32[80,128]{1,0:T(8,128)S(1)}, f32[80,128]{1,0:T(8,128)S(1)}, u32[]{:S(2)}, u32[]{:S(2)}) collective-permute-start(f32[80,128]{1,0:T(8,128)S(1)} %add_add_fusion.1), channel_id=1, source_target_pairs={{0,22},{1,23},{2,20},{3,21},{4,18},{5,19},{6,16},{7,17},{8,30},{9,... | collective-permute-start | bytes 122888 | tf_op jit(solution)/shard_map/ppermute | solution.py:383
  28.8 0.7 %collective-permute-start.11 = (f32[80,128]{1,0:T(8,128)S(1)}, f32[80,128]{1,0:T(8,128)S(1)}, u32[]{:S(2)}, u32[]{:S(2)}) collective-permute-start(f32[80,128]{1,0:T(8,128)S(1)} %add_add_fusion.1), channel_id=1, source_target_pairs={{0,6},{1,7},{2,4},{3,5},{4,2},{5,3},{6,0},{7,1},{8,14},{9,15},{10,... | collective-permute-start | bytes 122888 | tf_op jit(solution)/shard_map/ppermute | solution.py:383
  29.5 0.4 %collective-permute-start.10 = (f32[80,128]{1,0:T(8,128)S(1)}, f32[80,128]{1,0:T(8,128)S(1)}, u32[]{:S(2)}, u32[]{:S(2)}) collective-permute-start(f32[80,128]{1,0:T(8,128)S(1)} %add_add_fusion.1), channel_id=1, source_target_pairs={{0,20},{1,21},{2,22},{3,23},{4,16},{5,17},{6,18},{7,19},{8,28},{9,... | collective-permute-start | bytes 122888 | tf_op jit(solution)/shard_map/ppermute | solution.py:383
  29.9 1.2 %collective-permute-done.12 = f32[80,128]{1,0:T(8,128)S(1)} collective-permute-done((f32[80,128]{1,0:T(8,128)S(1)}, f32[80,128]{1,0:T(8,128)S(1)}, u32[]{:S(2)}, u32[]{:S(2)}) %collective-permute-start.12) | collective-permute-done | bytes 40992 | tf_op jit(solution)/shard_map/ppermute | solution.py:383
  31.1 2.8 %collective-permute-done.11 = f32[80,128]{1,0:T(8,128)S(1)} collective-permute-done((f32[80,128]{1,0:T(8,128)S(1)}, f32[80,128]{1,0:T(8,128)S(1)}, u32[]{:S(2)}, u32[]{:S(2)}) %collective-permute-start.11) | collective-permute-done | bytes 40992 | tf_op jit(solution)/shard_map/ppermute | solution.py:383
  33.9 0.0 collective-permute-done.10
  34.0 8.5 %shard_map.44 = (f32[3,180,32,128]{3,2,1,0:T(8,128)}, f32[128,128]{1,0:T(8,128)}) custom-call(f32[80,128]{1,0:T(8,128)S(1)} %add_add_fusion.p_ref, bf16[3,360,128]{2,1,0:T(8,128)(2,1)S(1)} %get-tuple-element.36.an_ref, bf16[3,360,128]{2,1,0:T(8,128)(2,1)S(1)} %get-tuple-element.37.as_ref, bf16[3,4,32,128]{3,2,1,0:T(8,128)(2,1)S(1)} %get-tuple-element.38.ac_ref, ...), custom_call_target="tpu_custom_call" | custom-call | tf_op jit(solution)/shard_map/pallas_call | solution.py:449
  (8 shorter events, 0.1 us)
Async XLA Ops:
  0.6 12.3 %copy-start = (bf16[3,32,180]{2,1,0:T(8,128)(2,1)S(1)}, bf16[3,32,180]{2,1,0:T(8,128)(2,1)}, u32[]{:S(2)}) copy-start(bf16[3,32,180]{2,1,0:T(8,128)(2,1)} %bg_ref.3) | copy-start | bytes 103684
  3.6 5.7 %collective-permute-start = (bf16[3,2,32,128]{3,2,1,0:T(8,128)(2,1)S(1)}, bf16[3,2,32,128]{3,2,1,0:T(8,128)(2,1)S(1)}, u32[]{:S(2)}, u32[]{:S(2)}) collective-permute-start(bf16[3,2,32,128]{3,2,1,0:T(8,128)(2,1)S(1)} %get-tuple-element.28), channel_id=1, source_target_pairs={{0,4},{4,0},{8,12},{12,8},{16,20},{20,16},{24,28},{28,24},{1,5},{5... | collective-permute-start | bytes 147464 | tf_op jit(solution)/shard_map/ppermute | solution.py:368
  4.1 5.3 %collective-permute-start.1 = (bf16[3,2,32,128]{3,2,1,0:T(8,128)(2,1)S(1)}, bf16[3,2,32,128]{3,2,1,0:T(8,128)(2,1)S(1)}, u32[]{:S(2)}, u32[]{:S(2)}) collective-permute-start(bf16[3,2,32,128]{3,2,1,0:T(8,128)(2,1)S(1)} %get-tuple-element.29), channel_id=1, source_target_pairs={{0,28},{4,8},{8,4},{12,16},{16,12},{20,24},{24,20},{28,0},{1,29},{... | collective-permute-start | bytes 147464 | tf_op jit(solution)/shard_map/ppermute | solution.py:367
  7.7 9.5 %collective-permute-start.2 = (bf16[3,360,128]{2,1,0:T(8,128)(2,1)S(1)}, bf16[3,360,128]{2,1,0:T(8,128)(2,1)S(1)}, u32[]{:S(2)}, u32[]{:S(2)}) collective-permute-start(bf16[3,360,128]{2,1,0:T(8,128)(2,1)S(1)} %get-tuple-element.30), channel_id=1, source_target_pairs={{0,1},{1,0},{2,3},{3,2},{4,5},{5,4},{6,7},{7,6},{8,9},{9,8},{10,11... | collective-permute-start | bytes 829448 | tf_op jit(solution)/shard_map/ppermute | solution.py:366
  9.3 7.9 %collective-permute-start.3 = (bf16[3,360,128]{2,1,0:T(8,128)(2,1)S(1)}, bf16[3,360,128]{2,1,0:T(8,128)(2,1)S(1)}, u32[]{:S(2)}, u32[]{:S(2)}) collective-permute-start(bf16[3,360,128]{2,1,0:T(8,128)(2,1)S(1)} %get-tuple-element.31), channel_id=1, source_target_pairs={{0,4},{1,2},{2,1},{3,7},{4,0},{5,6},{6,5},{7,3},{8,12},{9,10},{10,... | collective-permute-start | bytes 829448 | tf_op jit(solution)/shard_map/ppermute | solution.py:365
  9.5 7.6 %collective-permute-start.5 = (bf16[3,8,128]{2,1,0:T(8,128)(2,1)S(1)}, bf16[3,8,128]{2,1,0:T(8,128)(2,1)S(1)}, u32[]{:S(2)}, u32[]{:S(2)}) collective-permute-start(bf16[3,8,128]{2,1,0:T(8,128)(2,1)S(1)} %get-tuple-element.44), channel_id=1, source_target_pairs={{0,4},{1,2},{2,1},{3,7},{4,0},{5,6},{6,5},{7,3},{8,12},{9,10},{10,... | collective-permute-start | bytes 18440 | tf_op jit(solution)/shard_map/ppermute | solution.py:373
  9.9 7.2 %collective-permute-start.4 = (bf16[3,8,128]{2,1,0:T(8,128)(2,1)S(1)}, bf16[3,8,128]{2,1,0:T(8,128)(2,1)S(1)}, u32[]{:S(2)}, u32[]{:S(2)}) collective-permute-start(bf16[3,8,128]{2,1,0:T(8,128)(2,1)S(1)} %get-tuple-element.45), channel_id=1, source_target_pairs={{0,1},{1,0},{2,3},{3,2},{4,5},{5,4},{6,7},{7,6},{8,9},{9,8},{10,11... | collective-permute-start | bytes 18440 | tf_op jit(solution)/shard_map/ppermute | solution.py:374
  18.9 1.3 %collective-permute-start.6 = (f32[80,128]{1,0:T(8,128)S(1)}, f32[80,128]{1,0:T(8,128)S(1)}, u32[]{:S(2)}, u32[]{:S(2)}) collective-permute-start(f32[80,128]{1,0:T(8,128)S(1)} %get-tuple-element.35), channel_id=1, source_target_pairs={{0,4},{1,5},{2,6},{3,7},{4,0},{5,1},{6,2},{7,3},{8,12},{9,13},{10,... | collective-permute-start | bytes 122888 | tf_op jit(solution)/shard_map/ppermute | solution.py:383
  20.2 4.4 %collective-permute-start.9 = (f32[80,128]{1,0:T(8,128)S(1)}, f32[80,128]{1,0:T(8,128)S(1)}, u32[]{:S(2)}, u32[]{:S(2)}) collective-permute-start(f32[80,128]{1,0:T(8,128)S(1)} %add.21), channel_id=1, source_target_pairs={{0,13},{1,12},{2,15},{3,14},{4,9},{5,8},{6,11},{7,10},{8,5},{9,4},... | collective-permute-start | bytes 122888 | tf_op jit(solution)/shard_map/ppermute | solution.py:383
  21.7 3.4 %collective-permute-start.8 = (f32[80,128]{1,0:T(8,128)S(1)}, f32[80,128]{1,0:T(8,128)S(1)}, u32[]{:S(2)}, u32[]{:S(2)}) collective-permute-start(f32[80,128]{1,0:T(8,128)S(1)} %add.21), channel_id=1, source_target_pairs={{0,5},{1,4},{2,7},{3,6},{4,1},{5,0},{6,3},{7,2},{8,13},{9,12},{10,... | collective-permute-start | bytes 122888 | tf_op jit(solution)/shard_map/ppermute | solution.py:383
  22.4 3.4 %collective-permute-start.7 = (f32[80,128]{1,0:T(8,128)S(1)}, f32[80,128]{1,0:T(8,128)S(1)}, u32[]{:S(2)}, u32[]{:S(2)}) collective-permute-start(f32[80,128]{1,0:T(8,128)S(1)} %add.21), channel_id=1, source_target_pairs={{0,12},{1,13},{2,14},{3,15},{4,8},{5,9},{6,10},{7,11},{8,4},{9,5},... | collective-permute-start | bytes 122888 | tf_op jit(solution)/shard_map/ppermute | solution.py:383
  25.8 5.3 %collective-permute-start.12 = (f32[80,128]{1,0:T(8,128)S(1)}, f32[80,128]{1,0:T(8,128)S(1)}, u32[]{:S(2)}, u32[]{:S(2)}) collective-permute-start(f32[80,128]{1,0:T(8,128)S(1)} %add_add_fusion.1), channel_id=1, source_target_pairs={{0,22},{1,23},{2,20},{3,21},{4,18},{5,19},{6,16},{7,17},{8,30},{9,... | collective-permute-start | bytes 122888 | tf_op jit(solution)/shard_map/ppermute | solution.py:383
  28.8 5.2 %collective-permute-start.11 = (f32[80,128]{1,0:T(8,128)S(1)}, f32[80,128]{1,0:T(8,128)S(1)}, u32[]{:S(2)}, u32[]{:S(2)}) collective-permute-start(f32[80,128]{1,0:T(8,128)S(1)} %add_add_fusion.1), channel_id=1, source_target_pairs={{0,6},{1,7},{2,4},{3,5},{4,2},{5,3},{6,0},{7,1},{8,14},{9,15},{10,... | collective-permute-start | bytes 122888 | tf_op jit(solution)/shard_map/ppermute | solution.py:383
  29.5 4.4 %collective-permute-start.10 = (f32[80,128]{1,0:T(8,128)S(1)}, f32[80,128]{1,0:T(8,128)S(1)}, u32[]{:S(2)}, u32[]{:S(2)}) collective-permute-start(f32[80,128]{1,0:T(8,128)S(1)} %add_add_fusion.1), channel_id=1, source_target_pairs={{0,20},{1,21},{2,22},{3,23},{4,16},{5,17},{6,18},{7,19},{8,28},{9,... | collective-permute-start | bytes 122888 | tf_op jit(solution)/shard_map/ppermute | solution.py:383

commit v7 on v6

--- a/solution.py
+++ b/solution.py
@@ -262,27 +262,39 @@
         cols = {b: [jnp.broadcast_to(w[b][:, k0 + j:k0 + j + 1], (8, n)) for j in range(block)] for b in close}
         below = {b: jnp.where((lane >= k0) & (lane < k0 + block), 0.0, w[b]) for b in range(t0 + 2, len(w))}
         inverses = [None, None]
-        for s in range(block):
+        for s in range(0, block, 2):
             k, top, row = k0 + s, t0 + s // 8, s % 8
-            inverse = 1.0 / jnp.broadcast_to(cols[top][s][row:row + 1], (8, n))
+            p, q = (jnp.broadcast_to(cols[top][s + i][row:row + 1], (8, n)) for i in range(2))
+            second = jnp.broadcast_to(cols[top][s + 1][row + 1:row + 2], (8, n))
+            inverse, inverse2 = 1.0 / p, p / (p * second - q * q)
+            ratio = q * inverse
             old = inverses[s // 8]
-            inverses[s // 8] = inverse if old is None else jnp.where(sub >= row, inverse, old)
+            both = jnp.where(sub > row, inverse2, inverse)
+            inverses[s // 8] = both if old is None else jnp.where(sub >= row, both, old)
             pivot_row = jnp.where(lane == k, 1.0, jnp.broadcast_to(w[top][row:row + 1], (8, n)))
+            next_row = jnp.where(lane == k, 0.0, jnp.broadcast_to(w[top][row + 1:row + 2], (8, n))) - ratio * pivot_row
+            next_row = jnp.where(lane == k + 1, 1.0, next_row)
             outside = jnp.where((lane > k) & (lane < k0 + block), 0.0, pivot_row)
-            heads = [jnp.broadcast_to(cols[top][j][row:row + 1], (8, n)) for j in range(s + 1, block)]
+            outside2 = jnp.where((lane > k + 1) & (lane < k0 + block), 0.0, next_row)
+            heads = [jnp.broadcast_to(cols[top][j][row:row + 1], (8, n)) for j in range(s + 2, block)]
+            heads2 = [jnp.broadcast_to(cols[top][j][row + 1:row + 2], (8, n)) - ratio * heads[j - s - 2]
+                      for j in range(s + 2, block)]
             for b in close:
-                if b < top or (b == top and row == 7):
+                if b < top:
                     continue
                 f = cols[b][s] * inverse
+                f2 = (cols[b][s + 1] - f * q) * inverse2
                 if b == top:
-                    f = jnp.where(sub > row, f, 0.0)
+                    f, f2 = jnp.where(sub > row, f, 0.0), jnp.where(sub > row + 1, f2, 0.0)
                 if b < t0 + 2:
-                    at = (lane == k) & (sub > row) if b == top else lane == k
-                    w[b] = jnp.where(at, 0.0, w[b]) - f * pivot_row
+                    here, here2 = lane == k, lane == k + 1
+                    if b == top:
+                        here, here2 = here & (sub > row), here2 & (sub > row + 1)
+                    w[b] = jnp.where(here2, 0.0, jnp.where(here, 0.0, w[b]) - f * pivot_row) - f2 * next_row
                 else:
-                    below[b] = below[b] - f * outside
-                for j in range(s + 1, block):
-                    cols[b][j] = cols[b][j] - f * heads[j - s - 1]
+                    below[b] = below[b] - (f * outside + f2 * outside2)
+                for j in range(s + 2, block):
+                    cols[b][j] = cols[b][j] - (f * heads[j - s - 2] + f2 * heads2[j - s - 2])
         if t0 + near < len(w):
             factors, rows = [], []
             for h in range(2):
@@ -329,7 +341,10 @@
 
     for i, (f, lo, hi) in enumerate(parts):
         o_ref[f, lo:hi] = times(a_ref[f, lo:hi].reshape(-1, width)).reshape(hi - lo, rows, width)
-        if lo == 0:
+        if i == 0:
+            few = -(-2 * hi // 16) * 16
+            north, south = times(an_ref[f, :few]), times(as_ref[f, :few])
+        elif i == 1 or lo == 0:
             north, south = times(an_ref[f]), times(as_ref[f])
         for l in range(lo, hi):
             if l < 2 or l >= cols - 2:
@@ -383,17 +398,17 @@
         return lax.ppermute(gram, ("lon", "lat"), pairs)
 
     gram = gram + partner(1, 0)
-    by_lon = [1 << i for i in range(1, lon.bit_length() - 1)]
-    by_lat = [1 << i for i in range(lat.bit_length() - 1)]
-    while by_lon or by_lat:
-        if by_lon and by_lat:
-            dk, dz = by_lon.pop(0), by_lat.pop(0)
-            x, z, xz = partner(dk ^ 1, 0), partner(1, dz), partner(dk ^ 1, dz)
-            gram = (gram + x) + (z + xz)
-        elif by_lon:
-            gram = gram + partner(by_lon.pop(0) ^ 1, 0)
-        else:
-            gram = gram + partner(1, by_lat.pop(0))
+    by_lon = [(1 << i, 0) for i in range(1, lon.bit_length() - 1)]
+    by_lat = [(0, 1 << i) for i in range(lat.bit_length() - 1)]
+    for steps in (by_lon, by_lat):
+        while steps:
+            dk, dz = steps.pop(0)
+            if steps:
+                ek, ez = steps.pop(0)
+                e, d, de = partner(ek ^ 1, ez), partner(dk ^ 1, dz), partner(dk ^ ek ^ 1, dz ^ ez)
+                gram = (gram + d) + (e + de)
+            else:
+                gram = gram + partner(dk ^ 1, dz)
     return gram
 
 

time: 42.6 us -> 41.5 us (0.974)
  waiting for transfers between devices: 8.04 us -> 6.83 us
    ppermute x7, waiting for transfers between devices: 7.86 us -> 6.65 us  [partner(): return lax.ppermute(gram, ('lon', 'lat'), pairs)]
  transfers between devices with their start and end apart: 13 -> 13, of which waited for: 7 -> 8; matrix products, arithmetic and copies ran while one was open for 0% -> 0% of each run, Pallas kernels for 10% -> 10%
where the time goes in v7:
time: 41.5 us; the launch traced here: 41.1 us
  Pallas kernels  17.2 us (41%)
  starting transfers between devices  16.2 us (39%)
  waiting for transfers between devices  6.83 us (16%)
  between operations  0.75 us (2%)
    pallas_call x1, Pallas kernels, local(): pl.pallas_call(functools.partial(modes_kernel, total=float(fields * nlat...  8.38 us
    ppermute x7, starting transfers between devices, partner(): return lax.ppermute(gram, ('lon', 'lat'), pairs)  7.17 us
    ppermute x7, waiting for transfers between devices, partner(): return lax.ppermute(gram, ('lon', 'lat'), pairs)  6.65 us
    pallas_call x1, Pallas kernels, local(): pl.pallas_call(inner_kernel, out_shape=(pltpu.VMEM((fields, cols, rows, w...  4.23 us
    ppermute x1, starting transfers between devices, halos(): lon_b = lax.ppermute(lon_b, 'lon', by_lon_b)  3.56 us
    ppermute x1, starting transfers between devices, halos(): corner_a = lax.ppermute(jnp.where(even, high, low), both, by_lat_a)  2.96 us
    pallas_call x1, Pallas kernels, local(): pl.pallas_call(functools.partial(edges_kernel, nlat=nlat), out_shape=(plt...  2.9 us
    pallas_call x1, Pallas kernels, local(): pl.pallas_call(functools.partial(outer_kernel, nlat=nlat), out_shape=(plt...  1.68 us
  transfers between devices with their start and end apart: 13, of which 8 were waited for; matrix products, arithmetic and copies ran while one was open for 0% of the time, Pallas kernels for 10%

profile of v7, /device:TPU:0, one launch (start us, length us, event | category | flops | bytes accessed | tf_op | source)
XLA Modules:
  0.0 41.1 jit_solution(7063150495813195418)
XLA Ops:
  0.6 0.0 copy-start
  0.6 0.1 pad_add_fusion.place_ref
  0.7 2.9 %shard_map.41 = (bf16[3,180,32,128]{3,2,1,0:T(8,128)(2,1)S(1)}, bf16[3,8,32,128]{3,2,1,0:T(8,128)(2,1)S(1)}, f32[8,128]{1,0:T(8,128)S(1)}, bf16[256,256]{1,0:T(8...) custom-call(s32[2]{0:T(128)S(1)} %pad_add_fusion.place_ref, ...), custom_call_target="tpu_custom_call" | custom-call | tf_op jit(solution)/shard_map/pallas_call | solution.py:430
  3.6 0.5 %collective-permute-start = (bf16[3,2,32,128]{3,2,1,0:T(8,128)(2,1)S(1)}, bf16[3,2,32,128]{3,2,1,0:T(8,128)(2,1)S(1)}, u32[]{:S(2)}, u32[]{:S(2)}) collective-permute-start(bf16[3,2,32,128]{3,2,1,0:T(8,128)(2,1)S(1)} %get-tuple-element.28), channel_id=1, source_target_pairs={{0,4},{4,0},{8,12},{12,8},{16,20},{20,16},{24,28},{28,24},{1,5},{5... | collective-permute-start | bytes 147464 | tf_op jit(solution)/shard_map/ppermute | solution.py:383
  4.1 3.6 %collective-permute-start.1 = (bf16[3,2,32,128]{3,2,1,0:T(8,128)(2,1)S(1)}, bf16[3,2,32,128]{3,2,1,0:T(8,128)(2,1)S(1)}, u32[]{:S(2)}, u32[]{:S(2)}) collective-permute-start(bf16[3,2,32,128]{3,2,1,0:T(8,128)(2,1)S(1)} %get-tuple-element.29), channel_id=1, source_target_pairs={{0,28},{4,8},{8,4},{12,16},{16,12},{20,24},{24,20},{28,0},{1,29},{... | collective-permute-start | bytes 147464 | tf_op jit(solution)/shard_map/ppermute | solution.py:382
  7.7 1.6 %collective-permute-start.2 = (bf16[3,360,128]{2,1,0:T(8,128)(2,1)S(1)}, bf16[3,360,128]{2,1,0:T(8,128)(2,1)S(1)}, u32[]{:S(2)}, u32[]{:S(2)}) collective-permute-start(bf16[3,360,128]{2,1,0:T(8,128)(2,1)S(1)} %get-tuple-element.30), channel_id=1, source_target_pairs={{0,1},{1,0},{2,3},{3,2},{4,5},{5,4},{6,7},{7,6},{8,9},{9,8},{10,11... | collective-permute-start | bytes 829448 | tf_op jit(solution)/shard_map/ppermute | solution.py:381
  9.3 0.0 collective-permute-start.3
  9.3 0.0 collective-permute-done.lon_a_ref
  9.3 0.2 collective-permute-done.1.lon_b_ref
  9.5 0.4 %collective-permute-start.5 = (bf16[3,8,128]{2,1,0:T(8,128)(2,1)S(1)}, bf16[3,8,128]{2,1,0:T(8,128)(2,1)S(1)}, u32[]{:S(2)}, u32[]{:S(2)}) collective-permute-start(bf16[3,8,128]{2,1,0:T(8,128)(2,1)S(1)} %get-tuple-element.44), channel_id=1, source_target_pairs={{0,4},{1,2},{2,1},{3,7},{4,0},{5,6},{6,5},{7,3},{8,12},{9,10},{10,... | collective-permute-start | bytes 18440 | tf_op jit(solution)/shard_map/ppermute | solution.py:388
  9.9 3.0 %collective-permute-start.4 = (bf16[3,8,128]{2,1,0:T(8,128)(2,1)S(1)}, bf16[3,8,128]{2,1,0:T(8,128)(2,1)S(1)}, u32[]{:S(2)}, u32[]{:S(2)}) collective-permute-start(bf16[3,8,128]{2,1,0:T(8,128)(2,1)S(1)} %get-tuple-element.45), channel_id=1, source_target_pairs={{0,1},{1,0},{2,3},{3,2},{4,5},{5,4},{6,7},{7,6},{8,9},{9,8},{10,11... | collective-permute-start | bytes 18440 | tf_op jit(solution)/shard_map/ppermute | solution.py:389
  12.9 0.0 copy-done
  12.9 4.2 %shard_map.42 = (bf16[3,180,32,128]{3,2,1,0:T(8,128)(2,1)S(1)}, f32[3,360,128]{2,1,0:T(8,128)S(1)}, f32[3,360,128]{2,1,0:T(8,128)S(1)}, f32[128,128]{1,0:T(8,128)S(1)}) custom-call(bf16[3,180,32,128]{3,2,1,0:T(8,128)(2,1)S(1)} %get-tuple-element.22.m_ref, bf16[3,32,180]{2,1,0:T(8,128)(2,1)S(1)} %copy-done, bf16[256,256]{1,0:T(8,128)(2,1)S(1)} %get-tuple-element.23.mat_ref, ...), custom_call_target="tpu_custom_call" | custom-call | flops 4529848320 | bytes 17694720 | tf_op jit(solution)/shard_map/pallas_call | solution.py:443
  17.1 0.0 collective-permute-done.5.corner_b_ref
  17.2 0.0 collective-permute-done.4.corner_a_ref
  17.2 0.0 collective-permute-done.2.lat_a_ref
  17.2 0.0 collective-permute-done.3.lat_b_ref
  17.2 1.7 %shard_map.43 = (bf16[3,360,128]{2,1,0:T(8,128)(2,1)S(1)}, bf16[3,360,128]{2,1,0:T(8,128)(2,1)S(1)}, bf16[3,4,32,128]{3,2,1,0:T(8,128)(2,1)S(1)}, f32[80,128]{1,0:T(8,128)S(1)}) custom-call(s32[2]{0:T(128)S(1)} %pad_add_fusion.place_ref, f32[3,360,128]{2,1,0:T(8,128)S(1)} %get-tuple-element.25.en_ref, f32[3,360,128]{2,1,0:T(8,128)S(1)} %get-tuple-element.26.es_ref, ...), custom_call_target="tpu_custom_call" | custom-call | tf_op jit(solution)/shard_map/pallas_call | solution.py:453
  18.9 0.1 collective-permute-start.6
  19.0 1.2 %collective-permute-done.6 = f32[80,128]{1,0:T(8,128)S(1)} collective-permute-done((f32[80,128]{1,0:T(8,128)S(1)}, f32[80,128]{1,0:T(8,128)S(1)}, u32[]{:S(2)}, u32[]{:S(2)}) %collective-permute-start.6) | collective-permute-done | bytes 40992 | tf_op jit(solution)/shard_map/ppermute | solution.py:398
  20.2 1.9 %collective-permute-start.9 = (f32[80,128]{1,0:T(8,128)S(1)}, f32[80,128]{1,0:T(8,128)S(1)}, u32[]{:S(2)}, u32[]{:S(2)}) collective-permute-start(f32[80,128]{1,0:T(8,128)S(1)} %add.21), channel_id=1, source_target_pairs={{0,28},{1,29},{2,30},{3,31},{4,24},{5,25},{6,26},{7,27},{8,20},{9,... | collective-permute-start | bytes 122888 | tf_op jit(solution)/shard_map/ppermute | solution.py:398
  22.1 0.3 collective-permute-start.8
  22.4 0.8 %collective-permute-start.7 = (f32[80,128]{1,0:T(8,128)S(1)}, f32[80,128]{1,0:T(8,128)S(1)}, u32[]{:S(2)}, u32[]{:S(2)}) collective-permute-start(f32[80,128]{1,0:T(8,128)S(1)} %add.21), channel_id=1, source_target_pairs={{0,12},{1,13},{2,14},{3,15},{4,8},{5,9},{6,10},{7,11},{8,4},{9,5},... | collective-permute-start | bytes 122888 | tf_op jit(solution)/shard_map/ppermute | solution.py:398
  23.1 1.4 %collective-permute-done.9 = f32[80,128]{1,0:T(8,128)S(1)} collective-permute-done((f32[80,128]{1,0:T(8,128)S(1)}, f32[80,128]{1,0:T(8,128)S(1)}, u32[]{:S(2)}, u32[]{:S(2)}) %collective-permute-start.9) | collective-permute-done | bytes 40992 | tf_op jit(solution)/shard_map/ppermute | solution.py:398
  24.6 1.0 %collective-permute-done.8 = f32[80,128]{1,0:T(8,128)S(1)} collective-permute-done((f32[80,128]{1,0:T(8,128)S(1)}, f32[80,128]{1,0:T(8,128)S(1)}, u32[]{:S(2)}, u32[]{:S(2)}) %collective-permute-start.8) | collective-permute-done | bytes 40992 | tf_op jit(solution)/shard_map/ppermute | solution.py:398
  25.6 0.2 collective-permute-done.7
  25.8 2.2 %collective-permute-start.12 = (f32[80,128]{1,0:T(8,128)S(1)}, f32[80,128]{1,0:T(8,128)S(1)}, u32[]{:S(2)}, u32[]{:S(2)}) collective-permute-start(f32[80,128]{1,0:T(8,128)S(1)} %add_add_fusion.1), channel_id=1, source_target_pairs={{0,7},{1,6},{2,5},{3,4},{4,3},{5,2},{6,1},{7,0},{8,15},{9,14},{10,... | collective-permute-start | bytes 122888 | tf_op jit(solution)/shard_map/ppermute | solution.py:398
  28.0 0.5 %collective-permute-start.11 = (f32[80,128]{1,0:T(8,128)S(1)}, f32[80,128]{1,0:T(8,128)S(1)}, u32[]{:S(2)}, u32[]{:S(2)}) collective-permute-start(f32[80,128]{1,0:T(8,128)S(1)} %add_add_fusion.1), channel_id=1, source_target_pairs={{0,6},{1,7},{2,4},{3,5},{4,2},{5,3},{6,0},{7,1},{8,14},{9,15},{10,... | collective-permute-start | bytes 122888 | tf_op jit(solution)/shard_map/ppermute | solution.py:398
  28.5 1.4 %collective-permute-start.10 = (f32[80,128]{1,0:T(8,128)S(1)}, f32[80,128]{1,0:T(8,128)S(1)}, u32[]{:S(2)}, u32[]{:S(2)}) collective-permute-start(f32[80,128]{1,0:T(8,128)S(1)} %add_add_fusion.1), channel_id=1, source_target_pairs={{0,5},{1,4},{2,7},{3,6},{4,1},{5,0},{6,3},{7,2},{8,13},{9,12},{10,... | collective-permute-start | bytes 122888 | tf_op jit(solution)/shard_map/ppermute | solution.py:398
  29.9 1.2 %collective-permute-done.12 = f32[80,128]{1,0:T(8,128)S(1)} collective-permute-done((f32[80,128]{1,0:T(8,128)S(1)}, f32[80,128]{1,0:T(8,128)S(1)}, u32[]{:S(2)}, u32[]{:S(2)}) %collective-permute-start.12) | collective-permute-done | bytes 40992 | tf_op jit(solution)/shard_map/ppermute | solution.py:398
  31.1 1.2 %collective-permute-done.11 = f32[80,128]{1,0:T(8,128)S(1)} collective-permute-done((f32[80,128]{1,0:T(8,128)S(1)}, f32[80,128]{1,0:T(8,128)S(1)}, u32[]{:S(2)}, u32[]{:S(2)}) %collective-permute-start.11) | collective-permute-done | bytes 40992 | tf_op jit(solution)/shard_map/ppermute | solution.py:398
  32.3 0.4 collective-permute-done.10
  32.7 8.4 %shard_map.44 = (f32[3,180,32,128]{3,2,1,0:T(8,128)}, f32[128,128]{1,0:T(8,128)}) custom-call(f32[80,128]{1,0:T(8,128)S(1)} %add_add_fusion.p_ref, bf16[3,360,128]{2,1,0:T(8,128)(2,1)S(1)} %get-tuple-element.36.an_ref, bf16[3,360,128]{2,1,0:T(8,128)(2,1)S(1)} %get-tuple-element.37.as_ref, bf16[3,4,32,128]{3,2,1,0:T(8,128)(2,1)S(1)} %get-tuple-element.38.ac_ref, ...), custom_call_target="tpu_custom_call" | custom-call | tf_op jit(solution)/shard_map/pallas_call | solution.py:464
  (8 shorter events, 0.1 us)
Async XLA Ops:
  0.6 12.3 %copy-start = (bf16[3,32,180]{2,1,0:T(8,128)(2,1)S(1)}, bf16[3,32,180]{2,1,0:T(8,128)(2,1)}, u32[]{:S(2)}) copy-start(bf16[3,32,180]{2,1,0:T(8,128)(2,1)} %bg_ref.3) | copy-start | bytes 103684
  3.6 5.7 %collective-permute-start = (bf16[3,2,32,128]{3,2,1,0:T(8,128)(2,1)S(1)}, bf16[3,2,32,128]{3,2,1,0:T(8,128)(2,1)S(1)}, u32[]{:S(2)}, u32[]{:S(2)}) collective-permute-start(bf16[3,2,32,128]{3,2,1,0:T(8,128)(2,1)S(1)} %get-tuple-element.28), channel_id=1, source_target_pairs={{0,4},{4,0},{8,12},{12,8},{16,20},{20,16},{24,28},{28,24},{1,5},{5... | collective-permute-start | bytes 147464 | tf_op jit(solution)/shard_map/ppermute | solution.py:383
  4.1 5.3 %collective-permute-start.1 = (bf16[3,2,32,128]{3,2,1,0:T(8,128)(2,1)S(1)}, bf16[3,2,32,128]{3,2,1,0:T(8,128)(2,1)S(1)}, u32[]{:S(2)}, u32[]{:S(2)}) collective-permute-start(bf16[3,2,32,128]{3,2,1,0:T(8,128)(2,1)S(1)} %get-tuple-element.29), channel_id=1, source_target_pairs={{0,28},{4,8},{8,4},{12,16},{16,12},{20,24},{24,20},{28,0},{1,29},{... | collective-permute-start | bytes 147464 | tf_op jit(solution)/shard_map/ppermute | solution.py:382
  7.7 9.5 %collective-permute-start.2 = (bf16[3,360,128]{2,1,0:T(8,128)(2,1)S(1)}, bf16[3,360,128]{2,1,0:T(8,128)(2,1)S(1)}, u32[]{:S(2)}, u32[]{:S(2)}) collective-permute-start(bf16[3,360,128]{2,1,0:T(8,128)(2,1)S(1)} %get-tuple-element.30), channel_id=1, source_target_pairs={{0,1},{1,0},{2,3},{3,2},{4,5},{5,4},{6,7},{7,6},{8,9},{9,8},{10,11... | collective-permute-start | bytes 829448 | tf_op jit(solution)/shard_map/ppermute | solution.py:381
  9.3 7.9 %collective-permute-start.3 = (bf16[3,360,128]{2,1,0:T(8,128)(2,1)S(1)}, bf16[3,360,128]{2,1,0:T(8,128)(2,1)S(1)}, u32[]{:S(2)}, u32[]{:S(2)}) collective-permute-start(bf16[3,360,128]{2,1,0:T(8,128)(2,1)S(1)} %get-tuple-element.31), channel_id=1, source_target_pairs={{0,4},{1,2},{2,1},{3,7},{4,0},{5,6},{6,5},{7,3},{8,12},{9,10},{10,... | collective-permute-start | bytes 829448 | tf_op jit(solution)/shard_map/ppermute | solution.py:380
  9.5 7.6 %collective-permute-start.5 = (bf16[3,8,128]{2,1,0:T(8,128)(2,1)S(1)}, bf16[3,8,128]{2,1,0:T(8,128)(2,1)S(1)}, u32[]{:S(2)}, u32[]{:S(2)}) collective-permute-start(bf16[3,8,128]{2,1,0:T(8,128)(2,1)S(1)} %get-tuple-element.44), channel_id=1, source_target_pairs={{0,4},{1,2},{2,1},{3,7},{4,0},{5,6},{6,5},{7,3},{8,12},{9,10},{10,... | collective-permute-start | bytes 18440 | tf_op jit(solution)/shard_map/ppermute | solution.py:388
  9.9 7.2 %collective-permute-start.4 = (bf16[3,8,128]{2,1,0:T(8,128)(2,1)S(1)}, bf16[3,8,128]{2,1,0:T(8,128)(2,1)S(1)}, u32[]{:S(2)}, u32[]{:S(2)}) collective-permute-start(bf16[3,8,128]{2,1,0:T(8,128)(2,1)S(1)} %get-tuple-element.45), channel_id=1, source_target_pairs={{0,1},{1,0},{2,3},{3,2},{4,5},{5,4},{6,7},{7,6},{8,9},{9,8},{10,11... | collective-permute-start | bytes 18440 | tf_op jit(solution)/shard_map/ppermute | solution.py:389
  18.9 1.3 %collective-permute-start.6 = (f32[80,128]{1,0:T(8,128)S(1)}, f32[80,128]{1,0:T(8,128)S(1)}, u32[]{:S(2)}, u32[]{:S(2)}) collective-permute-start(f32[80,128]{1,0:T(8,128)S(1)} %get-tuple-element.35), channel_id=1, source_target_pairs={{0,4},{1,5},{2,6},{3,7},{4,0},{5,1},{6,2},{7,3},{8,12},{9,13},{10,... | collective-permute-start | bytes 122888 | tf_op jit(solution)/shard_map/ppermute | solution.py:398
  20.2 4.4 %collective-permute-start.9 = (f32[80,128]{1,0:T(8,128)S(1)}, f32[80,128]{1,0:T(8,128)S(1)}, u32[]{:S(2)}, u32[]{:S(2)}) collective-permute-start(f32[80,128]{1,0:T(8,128)S(1)} %add.21), channel_id=1, source_target_pairs={{0,28},{1,29},{2,30},{3,31},{4,24},{5,25},{6,26},{7,27},{8,20},{9,... | collective-permute-start | bytes 122888 | tf_op jit(solution)/shard_map/ppermute | solution.py:398
  22.1 3.5 %collective-permute-start.8 = (f32[80,128]{1,0:T(8,128)S(1)}, f32[80,128]{1,0:T(8,128)S(1)}, u32[]{:S(2)}, u32[]{:S(2)}) collective-permute-start(f32[80,128]{1,0:T(8,128)S(1)} %add.21), channel_id=1, source_target_pairs={{0,20},{1,21},{2,22},{3,23},{4,16},{5,17},{6,18},{7,19},{8,28},{9,... | collective-permute-start | bytes 122888 | tf_op jit(solution)/shard_map/ppermute | solution.py:398
  22.4 3.4 %collective-permute-start.7 = (f32[80,128]{1,0:T(8,128)S(1)}, f32[80,128]{1,0:T(8,128)S(1)}, u32[]{:S(2)}, u32[]{:S(2)}) collective-permute-start(f32[80,128]{1,0:T(8,128)S(1)} %add.21), channel_id=1, source_target_pairs={{0,12},{1,13},{2,14},{3,15},{4,8},{5,9},{6,10},{7,11},{8,4},{9,5},... | collective-permute-start | bytes 122888 | tf_op jit(solution)/shard_map/ppermute | solution.py:398
  25.8 5.3 %collective-permute-start.12 = (f32[80,128]{1,0:T(8,128)S(1)}, f32[80,128]{1,0:T(8,128)S(1)}, u32[]{:S(2)}, u32[]{:S(2)}) collective-permute-start(f32[80,128]{1,0:T(8,128)S(1)} %add_add_fusion.1), channel_id=1, source_target_pairs={{0,7},{1,6},{2,5},{3,4},{4,3},{5,2},{6,1},{7,0},{8,15},{9,14},{10,... | collective-permute-start | bytes 122888 | tf_op jit(solution)/shard_map/ppermute | solution.py:398
  28.0 4.4 %collective-permute-start.11 = (f32[80,128]{1,0:T(8,128)S(1)}, f32[80,128]{1,0:T(8,128)S(1)}, u32[]{:S(2)}, u32[]{:S(2)}) collective-permute-start(f32[80,128]{1,0:T(8,128)S(1)} %add_add_fusion.1), channel_id=1, source_target_pairs={{0,6},{1,7},{2,4},{3,5},{4,2},{5,3},{6,0},{7,1},{8,14},{9,15},{10,... | collective-permute-start | bytes 122888 | tf_op jit(solution)/shard_map/ppermute | solution.py:398
  28.5 4.2 %collective-permute-start.10 = (f32[80,128]{1,0:T(8,128)S(1)}, f32[80,128]{1,0:T(8,128)S(1)}, u32[]{:S(2)}, u32[]{:S(2)}) collective-permute-start(f32[80,128]{1,0:T(8,128)S(1)} %add_add_fusion.1), channel_id=1, source_target_pairs={{0,5},{1,4},{2,7},{3,6},{4,1},{5,0},{6,3},{7,2},{8,13},{9,12},{10,... | collective-permute-start | bytes 122888 | tf_op jit(solution)/shard_map/ppermute | solution.py:398

commit v8 on v6

--- a/solution.py
+++ b/solution.py
@@ -329,7 +329,10 @@
 
     for i, (f, lo, hi) in enumerate(parts):
         o_ref[f, lo:hi] = times(a_ref[f, lo:hi].reshape(-1, width)).reshape(hi - lo, rows, width)
-        if lo == 0:
+        if i == 0:
+            few = -(-2 * hi // 16) * 16
+            north, south = times(an_ref[f, :few]), times(as_ref[f, :few])
+        elif i == 1 or lo == 0:
             north, south = times(an_ref[f]), times(as_ref[f])
         for l in range(lo, hi):
             if l < 2 or l >= cols - 2:
@@ -383,17 +386,17 @@
         return lax.ppermute(gram, ("lon", "lat"), pairs)
 
     gram = gram + partner(1, 0)
-    by_lon = [1 << i for i in range(1, lon.bit_length() - 1)]
-    by_lat = [1 << i for i in range(lat.bit_length() - 1)]
-    while by_lon or by_lat:
-        if by_lon and by_lat:
-            dk, dz = by_lon.pop(0), by_lat.pop(0)
-            x, z, xz = partner(dk ^ 1, 0), partner(1, dz), partner(dk ^ 1, dz)
-            gram = (gram + x) + (z + xz)
-        elif by_lon:
-            gram = gram + partner(by_lon.pop(0) ^ 1, 0)
-        else:
-            gram = gram + partner(1, by_lat.pop(0))
+    by_lon = [(1 << i, 0) for i in range(1, lon.bit_length() - 1)]
+    by_lat = [(0, 1 << i) for i in range(lat.bit_length() - 1)]
+    for steps in (by_lon, by_lat):
+        while steps:
+            dk, dz = steps.pop(0)
+            if steps:
+                ek, ez = steps.pop(0)
+                e, d, de = partner(ek ^ 1, ez), partner(dk ^ 1, dz), partner(dk ^ ek ^ 1, dz ^ ez)
+                gram = (gram + d) + (e + de)
+            else:
+                gram = gram + partner(dk ^ 1, dz)
     return gram
 
 

time: 42.6 us -> 41.7 us (0.979)
  waiting for transfers between devices: 8.04 us -> 6.83 us
    ppermute x7, waiting for transfers between devices: 7.86 us -> 6.65 us  [partner(): return lax.ppermute(gram, ('lon', 'lat'), pairs)]
  transfers between devices with their start and end apart: 13 -> 13, of which waited for: 7 -> 8; matrix products, arithmetic and copies ran while one was open for 0% -> 0% of each run, Pallas kernels for 10% -> 10%
where the time goes in v8:
time: 41.7 us; the launch traced here: 41.2 us
  Pallas kernels  17.3 us (41%)
  starting transfers between devices  16.2 us (39%)
  waiting for transfers between devices  6.83 us (16%)
  between operations  0.75 us (2%)
    pallas_call x1, Pallas kernels, local(): pl.pallas_call(functools.partial(modes_kernel, total=float(fields * nlat...  8.5 us
    ppermute x7, starting transfers between devices, partner(): return lax.ppermute(gram, ('lon', 'lat'), pairs)  7.17 us
    ppermute x7, waiting for transfers between devices, partner(): return lax.ppermute(gram, ('lon', 'lat'), pairs)  6.65 us
    pallas_call x1, Pallas kernels, local(): pl.pallas_call(inner_kernel, out_shape=(pltpu.VMEM((fields, cols, rows, w...  4.23 us
    ppermute x1, starting transfers between devices, halos(): lon_b = lax.ppermute(lon_b, 'lon', by_lon_b)  3.56 us
    ppermute x1, starting transfers between devices, halos(): corner_a = lax.ppermute(jnp.where(even, high, low), both, by_lat_a)  2.96 us
    pallas_call x1, Pallas kernels, local(): pl.pallas_call(functools.partial(edges_kernel, nlat=nlat), out_shape=(plt...  2.9 us
    pallas_call x1, Pallas kernels, local(): pl.pallas_call(functools.partial(outer_kernel, nlat=nlat), out_shape=(plt...  1.68 us
  transfers between devices with their start and end apart: 13, of which 8 were waited for; matrix products, arithmetic and copies ran while one was open for 0% of the time, Pallas kernels for 10%

profile of v8, /device:TPU:0, one launch (start us, length us, event | category | flops | bytes accessed | tf_op | source)
XLA Modules:
  0.0 41.2 jit_solution(9906516260597828974)
XLA Ops:
  0.6 0.0 copy-start
  0.6 0.1 pad_add_fusion.place_ref
  0.7 2.9 %shard_map.41 = (bf16[3,180,32,128]{3,2,1,0:T(8,128)(2,1)S(1)}, bf16[3,8,32,128]{3,2,1,0:T(8,128)(2,1)S(1)}, f32[8,128]{1,0:T(8,128)S(1)}, bf16[256,256]{1,0:T(8...) custom-call(s32[2]{0:T(128)S(1)} %pad_add_fusion.place_ref, ...), custom_call_target="tpu_custom_call" | custom-call | tf_op jit(solution)/shard_map/pallas_call | solution.py:418
  3.6 0.5 %collective-permute-start = (bf16[3,2,32,128]{3,2,1,0:T(8,128)(2,1)S(1)}, bf16[3,2,32,128]{3,2,1,0:T(8,128)(2,1)S(1)}, u32[]{:S(2)}, u32[]{:S(2)}) collective-permute-start(bf16[3,2,32,128]{3,2,1,0:T(8,128)(2,1)S(1)} %get-tuple-element.28), channel_id=1, source_target_pairs={{0,4},{4,0},{8,12},{12,8},{16,20},{20,16},{24,28},{28,24},{1,5},{5... | collective-permute-start | bytes 147464 | tf_op jit(solution)/shard_map/ppermute | solution.py:371
  4.1 3.6 %collective-permute-start.1 = (bf16[3,2,32,128]{3,2,1,0:T(8,128)(2,1)S(1)}, bf16[3,2,32,128]{3,2,1,0:T(8,128)(2,1)S(1)}, u32[]{:S(2)}, u32[]{:S(2)}) collective-permute-start(bf16[3,2,32,128]{3,2,1,0:T(8,128)(2,1)S(1)} %get-tuple-element.29), channel_id=1, source_target_pairs={{0,28},{4,8},{8,4},{12,16},{16,12},{20,24},{24,20},{28,0},{1,29},{... | collective-permute-start | bytes 147464 | tf_op jit(solution)/shard_map/ppermute | solution.py:370
  7.7 1.6 %collective-permute-start.2 = (bf16[3,360,128]{2,1,0:T(8,128)(2,1)S(1)}, bf16[3,360,128]{2,1,0:T(8,128)(2,1)S(1)}, u32[]{:S(2)}, u32[]{:S(2)}) collective-permute-start(bf16[3,360,128]{2,1,0:T(8,128)(2,1)S(1)} %get-tuple-element.30), channel_id=1, source_target_pairs={{0,1},{1,0},{2,3},{3,2},{4,5},{5,4},{6,7},{7,6},{8,9},{9,8},{10,11... | collective-permute-start | bytes 829448 | tf_op jit(solution)/shard_map/ppermute | solution.py:369
  9.3 0.0 collective-permute-start.3
  9.3 0.0 collective-permute-done.lon_a_ref
  9.3 0.2 collective-permute-done.1.lon_b_ref
  9.5 0.4 %collective-permute-start.5 = (bf16[3,8,128]{2,1,0:T(8,128)(2,1)S(1)}, bf16[3,8,128]{2,1,0:T(8,128)(2,1)S(1)}, u32[]{:S(2)}, u32[]{:S(2)}) collective-permute-start(bf16[3,8,128]{2,1,0:T(8,128)(2,1)S(1)} %get-tuple-element.44), channel_id=1, source_target_pairs={{0,4},{1,2},{2,1},{3,7},{4,0},{5,6},{6,5},{7,3},{8,12},{9,10},{10,... | collective-permute-start | bytes 18440 | tf_op jit(solution)/shard_map/ppermute | solution.py:376
  9.9 3.0 %collective-permute-start.4 = (bf16[3,8,128]{2,1,0:T(8,128)(2,1)S(1)}, bf16[3,8,128]{2,1,0:T(8,128)(2,1)S(1)}, u32[]{:S(2)}, u32[]{:S(2)}) collective-permute-start(bf16[3,8,128]{2,1,0:T(8,128)(2,1)S(1)} %get-tuple-element.45), channel_id=1, source_target_pairs={{0,1},{1,0},{2,3},{3,2},{4,5},{5,4},{6,7},{7,6},{8,9},{9,8},{10,11... | collective-permute-start | bytes 18440 | tf_op jit(solution)/shard_map/ppermute | solution.py:377
  12.9 0.0 copy-done
  12.9 4.2 %shard_map.42 = (bf16[3,180,32,128]{3,2,1,0:T(8,128)(2,1)S(1)}, f32[3,360,128]{2,1,0:T(8,128)S(1)}, f32[3,360,128]{2,1,0:T(8,128)S(1)}, f32[128,128]{1,0:T(8,128)S(1)}) custom-call(bf16[3,180,32,128]{3,2,1,0:T(8,128)(2,1)S(1)} %get-tuple-element.22.m_ref, bf16[3,32,180]{2,1,0:T(8,128)(2,1)S(1)} %copy-done, bf16[256,256]{1,0:T(8,128)(2,1)S(1)} %get-tuple-element.23.mat_ref, ...), custom_call_target="tpu_custom_call" | custom-call | flops 4529848320 | bytes 17694720 | tf_op jit(solution)/shard_map/pallas_call | solution.py:431
  17.1 0.0 collective-permute-done.5.corner_b_ref
  17.2 0.0 collective-permute-done.4.corner_a_ref
  17.2 0.0 collective-permute-done.2.lat_a_ref
  17.2 0.0 collective-permute-done.3.lat_b_ref
  17.2 1.7 %shard_map.43 = (bf16[3,360,128]{2,1,0:T(8,128)(2,1)S(1)}, bf16[3,360,128]{2,1,0:T(8,128)(2,1)S(1)}, bf16[3,4,32,128]{3,2,1,0:T(8,128)(2,1)S(1)}, f32[80,128]{1,0:T(8,128)S(1)}) custom-call(s32[2]{0:T(128)S(1)} %pad_add_fusion.place_ref, f32[3,360,128]{2,1,0:T(8,128)S(1)} %get-tuple-element.25.en_ref, f32[3,360,128]{2,1,0:T(8,128)S(1)} %get-tuple-element.26.es_ref, ...), custom_call_target="tpu_custom_call" | custom-call | tf_op jit(solution)/shard_map/pallas_call | solution.py:441
  18.9 0.1 collective-permute-start.6
  19.0 1.2 %collective-permute-done.6 = f32[80,128]{1,0:T(8,128)S(1)} collective-permute-done((f32[80,128]{1,0:T(8,128)S(1)}, f32[80,128]{1,0:T(8,128)S(1)}, u32[]{:S(2)}, u32[]{:S(2)}) %collective-permute-start.6) | collective-permute-done | bytes 40992 | tf_op jit(solution)/shard_map/ppermute | solution.py:386
  20.2 1.9 %collective-permute-start.9 = (f32[80,128]{1,0:T(8,128)S(1)}, f32[80,128]{1,0:T(8,128)S(1)}, u32[]{:S(2)}, u32[]{:S(2)}) collective-permute-start(f32[80,128]{1,0:T(8,128)S(1)} %add.21), channel_id=1, source_target_pairs={{0,28},{1,29},{2,30},{3,31},{4,24},{5,25},{6,26},{7,27},{8,20},{9,... | collective-permute-start | bytes 122888 | tf_op jit(solution)/shard_map/ppermute | solution.py:386
  22.1 0.3 collective-permute-start.8
  22.4 0.8 %collective-permute-start.7 = (f32[80,128]{1,0:T(8,128)S(1)}, f32[80,128]{1,0:T(8,128)S(1)}, u32[]{:S(2)}, u32[]{:S(2)}) collective-permute-start(f32[80,128]{1,0:T(8,128)S(1)} %add.21), channel_id=1, source_target_pairs={{0,12},{1,13},{2,14},{3,15},{4,8},{5,9},{6,10},{7,11},{8,4},{9,5},... | collective-permute-start | bytes 122888 | tf_op jit(solution)/shard_map/ppermute | solution.py:386
  23.1 1.4 %collective-permute-done.9 = f32[80,128]{1,0:T(8,128)S(1)} collective-permute-done((f32[80,128]{1,0:T(8,128)S(1)}, f32[80,128]{1,0:T(8,128)S(1)}, u32[]{:S(2)}, u32[]{:S(2)}) %collective-permute-start.9) | collective-permute-done | bytes 40992 | tf_op jit(solution)/shard_map/ppermute | solution.py:386
  24.6 1.0 %collective-permute-done.8 = f32[80,128]{1,0:T(8,128)S(1)} collective-permute-done((f32[80,128]{1,0:T(8,128)S(1)}, f32[80,128]{1,0:T(8,128)S(1)}, u32[]{:S(2)}, u32[]{:S(2)}) %collective-permute-start.8) | collective-permute-done | bytes 40992 | tf_op jit(solution)/shard_map/ppermute | solution.py:386
  25.6 0.2 collective-permute-done.7
  25.8 2.2 %collective-permute-start.12 = (f32[80,128]{1,0:T(8,128)S(1)}, f32[80,128]{1,0:T(8,128)S(1)}, u32[]{:S(2)}, u32[]{:S(2)}) collective-permute-start(f32[80,128]{1,0:T(8,128)S(1)} %add_add_fusion.1), channel_id=1, source_target_pairs={{0,7},{1,6},{2,5},{3,4},{4,3},{5,2},{6,1},{7,0},{8,15},{9,14},{10,... | collective-permute-start | bytes 122888 | tf_op jit(solution)/shard_map/ppermute | solution.py:386
  28.0 0.5 %collective-permute-start.11 = (f32[80,128]{1,0:T(8,128)S(1)}, f32[80,128]{1,0:T(8,128)S(1)}, u32[]{:S(2)}, u32[]{:S(2)}) collective-permute-start(f32[80,128]{1,0:T(8,128)S(1)} %add_add_fusion.1), channel_id=1, source_target_pairs={{0,6},{1,7},{2,4},{3,5},{4,2},{5,3},{6,0},{7,1},{8,14},{9,15},{10,... | collective-permute-start | bytes 122888 | tf_op jit(solution)/shard_map/ppermute | solution.py:386
  28.5 1.4 %collective-permute-start.10 = (f32[80,128]{1,0:T(8,128)S(1)}, f32[80,128]{1,0:T(8,128)S(1)}, u32[]{:S(2)}, u32[]{:S(2)}) collective-permute-start(f32[80,128]{1,0:T(8,128)S(1)} %add_add_fusion.1), channel_id=1, source_target_pairs={{0,5},{1,4},{2,7},{3,6},{4,1},{5,0},{6,3},{7,2},{8,13},{9,12},{10,... | collective-permute-start | bytes 122888 | tf_op jit(solution)/shard_map/ppermute | solution.py:386
  29.9 1.2 %collective-permute-done.12 = f32[80,128]{1,0:T(8,128)S(1)} collective-permute-done((f32[80,128]{1,0:T(8,128)S(1)}, f32[80,128]{1,0:T(8,128)S(1)}, u32[]{:S(2)}, u32[]{:S(2)}) %collective-permute-start.12) | collective-permute-done | bytes 40992 | tf_op jit(solution)/shard_map/ppermute | solution.py:386
  31.1 1.2 %collective-permute-done.11 = f32[80,128]{1,0:T(8,128)S(1)} collective-permute-done((f32[80,128]{1,0:T(8,128)S(1)}, f32[80,128]{1,0:T(8,128)S(1)}, u32[]{:S(2)}, u32[]{:S(2)}) %collective-permute-start.11) | collective-permute-done | bytes 40992 | tf_op jit(solution)/shard_map/ppermute | solution.py:386
  32.3 0.4 collective-permute-done.10
  32.7 8.5 %shard_map.44 = (f32[3,180,32,128]{3,2,1,0:T(8,128)}, f32[128,128]{1,0:T(8,128)}) custom-call(f32[80,128]{1,0:T(8,128)S(1)} %add_add_fusion.p_ref, bf16[3,360,128]{2,1,0:T(8,128)(2,1)S(1)} %get-tuple-element.36.an_ref, bf16[3,360,128]{2,1,0:T(8,128)(2,1)S(1)} %get-tuple-element.37.as_ref, bf16[3,4,32,128]{3,2,1,0:T(8,128)(2,1)S(1)} %get-tuple-element.38.ac_ref, ...), custom_call_target="tpu_custom_call" | custom-call | tf_op jit(solution)/shard_map/pallas_call | solution.py:452
  (8 shorter events, 0.1 us)
Async XLA Ops:
  0.6 12.3 %copy-start = (bf16[3,32,180]{2,1,0:T(8,128)(2,1)S(1)}, bf16[3,32,180]{2,1,0:T(8,128)(2,1)}, u32[]{:S(2)}) copy-start(bf16[3,32,180]{2,1,0:T(8,128)(2,1)} %bg_ref.3) | copy-start | bytes 103684
  3.6 5.7 %collective-permute-start = (bf16[3,2,32,128]{3,2,1,0:T(8,128)(2,1)S(1)}, bf16[3,2,32,128]{3,2,1,0:T(8,128)(2,1)S(1)}, u32[]{:S(2)}, u32[]{:S(2)}) collective-permute-start(bf16[3,2,32,128]{3,2,1,0:T(8,128)(2,1)S(1)} %get-tuple-element.28), channel_id=1, source_target_pairs={{0,4},{4,0},{8,12},{12,8},{16,20},{20,16},{24,28},{28,24},{1,5},{5... | collective-permute-start | bytes 147464 | tf_op jit(solution)/shard_map/ppermute | solution.py:371
  4.1 5.3 %collective-permute-start.1 = (bf16[3,2,32,128]{3,2,1,0:T(8,128)(2,1)S(1)}, bf16[3,2,32,128]{3,2,1,0:T(8,128)(2,1)S(1)}, u32[]{:S(2)}, u32[]{:S(2)}) collective-permute-start(bf16[3,2,32,128]{3,2,1,0:T(8,128)(2,1)S(1)} %get-tuple-element.29), channel_id=1, source_target_pairs={{0,28},{4,8},{8,4},{12,16},{16,12},{20,24},{24,20},{28,0},{1,29},{... | collective-permute-start | bytes 147464 | tf_op jit(solution)/shard_map/ppermute | solution.py:370
  7.7 9.5 %collective-permute-start.2 = (bf16[3,360,128]{2,1,0:T(8,128)(2,1)S(1)}, bf16[3,360,128]{2,1,0:T(8,128)(2,1)S(1)}, u32[]{:S(2)}, u32[]{:S(2)}) collective-permute-start(bf16[3,360,128]{2,1,0:T(8,128)(2,1)S(1)} %get-tuple-element.30), channel_id=1, source_target_pairs={{0,1},{1,0},{2,3},{3,2},{4,5},{5,4},{6,7},{7,6},{8,9},{9,8},{10,11... | collective-permute-start | bytes 829448 | tf_op jit(solution)/shard_map/ppermute | solution.py:369
  9.3 7.9 %collective-permute-start.3 = (bf16[3,360,128]{2,1,0:T(8,128)(2,1)S(1)}, bf16[3,360,128]{2,1,0:T(8,128)(2,1)S(1)}, u32[]{:S(2)}, u32[]{:S(2)}) collective-permute-start(bf16[3,360,128]{2,1,0:T(8,128)(2,1)S(1)} %get-tuple-element.31), channel_id=1, source_target_pairs={{0,4},{1,2},{2,1},{3,7},{4,0},{5,6},{6,5},{7,3},{8,12},{9,10},{10,... | collective-permute-start | bytes 829448 | tf_op jit(solution)/shard_map/ppermute | solution.py:368
  9.5 7.6 %collective-permute-start.5 = (bf16[3,8,128]{2,1,0:T(8,128)(2,1)S(1)}, bf16[3,8,128]{2,1,0:T(8,128)(2,1)S(1)}, u32[]{:S(2)}, u32[]{:S(2)}) collective-permute-start(bf16[3,8,128]{2,1,0:T(8,128)(2,1)S(1)} %get-tuple-element.44), channel_id=1, source_target_pairs={{0,4},{1,2},{2,1},{3,7},{4,0},{5,6},{6,5},{7,3},{8,12},{9,10},{10,... | collective-permute-start | bytes 18440 | tf_op jit(solution)/shard_map/ppermute | solution.py:376
  9.9 7.2 %collective-permute-start.4 = (bf16[3,8,128]{2,1,0:T(8,128)(2,1)S(1)}, bf16[3,8,128]{2,1,0:T(8,128)(2,1)S(1)}, u32[]{:S(2)}, u32[]{:S(2)}) collective-permute-start(bf16[3,8,128]{2,1,0:T(8,128)(2,1)S(1)} %get-tuple-element.45), channel_id=1, source_target_pairs={{0,1},{1,0},{2,3},{3,2},{4,5},{5,4},{6,7},{7,6},{8,9},{9,8},{10,11... | collective-permute-start | bytes 18440 | tf_op jit(solution)/shard_map/ppermute | solution.py:377
  18.9 1.3 %collective-permute-start.6 = (f32[80,128]{1,0:T(8,128)S(1)}, f32[80,128]{1,0:T(8,128)S(1)}, u32[]{:S(2)}, u32[]{:S(2)}) collective-permute-start(f32[80,128]{1,0:T(8,128)S(1)} %get-tuple-element.35), channel_id=1, source_target_pairs={{0,4},{1,5},{2,6},{3,7},{4,0},{5,1},{6,2},{7,3},{8,12},{9,13},{10,... | collective-permute-start | bytes 122888 | tf_op jit(solution)/shard_map/ppermute | solution.py:386
  20.2 4.4 %collective-permute-start.9 = (f32[80,128]{1,0:T(8,128)S(1)}, f32[80,128]{1,0:T(8,128)S(1)}, u32[]{:S(2)}, u32[]{:S(2)}) collective-permute-start(f32[80,128]{1,0:T(8,128)S(1)} %add.21), channel_id=1, source_target_pairs={{0,28},{1,29},{2,30},{3,31},{4,24},{5,25},{6,26},{7,27},{8,20},{9,... | collective-permute-start | bytes 122888 | tf_op jit(solution)/shard_map/ppermute | solution.py:386
  22.1 3.5 %collective-permute-start.8 = (f32[80,128]{1,0:T(8,128)S(1)}, f32[80,128]{1,0:T(8,128)S(1)}, u32[]{:S(2)}, u32[]{:S(2)}) collective-permute-start(f32[80,128]{1,0:T(8,128)S(1)} %add.21), channel_id=1, source_target_pairs={{0,20},{1,21},{2,22},{3,23},{4,16},{5,17},{6,18},{7,19},{8,28},{9,... | collective-permute-start | bytes 122888 | tf_op jit(solution)/shard_map/ppermute | solution.py:386
  22.4 3.4 %collective-permute-start.7 = (f32[80,128]{1,0:T(8,128)S(1)}, f32[80,128]{1,0:T(8,128)S(1)}, u32[]{:S(2)}, u32[]{:S(2)}) collective-permute-start(f32[80,128]{1,0:T(8,128)S(1)} %add.21), channel_id=1, source_target_pairs={{0,12},{1,13},{2,14},{3,15},{4,8},{5,9},{6,10},{7,11},{8,4},{9,5},... | collective-permute-start | bytes 122888 | tf_op jit(solution)/shard_map/ppermute | solution.py:386
  25.8 5.3 %collective-permute-start.12 = (f32[80,128]{1,0:T(8,128)S(1)}, f32[80,128]{1,0:T(8,128)S(1)}, u32[]{:S(2)}, u32[]{:S(2)}) collective-permute-start(f32[80,128]{1,0:T(8,128)S(1)} %add_add_fusion.1), channel_id=1, source_target_pairs={{0,7},{1,6},{2,5},{3,4},{4,3},{5,2},{6,1},{7,0},{8,15},{9,14},{10,... | collective-permute-start | bytes 122888 | tf_op jit(solution)/shard_map/ppermute | solution.py:386
  28.0 4.4 %collective-permute-start.11 = (f32[80,128]{1,0:T(8,128)S(1)}, f32[80,128]{1,0:T(8,128)S(1)}, u32[]{:S(2)}, u32[]{:S(2)}) collective-permute-start(f32[80,128]{1,0:T(8,128)S(1)} %add_add_fusion.1), channel_id=1, source_target_pairs={{0,6},{1,7},{2,4},{3,5},{4,2},{5,3},{6,0},{7,1},{8,14},{9,15},{10,... | collective-permute-start | bytes 122888 | tf_op jit(solution)/shard_map/ppermute | solution.py:386
  28.5 4.2 %collective-permute-start.10 = (f32[80,128]{1,0:T(8,128)S(1)}, f32[80,128]{1,0:T(8,128)S(1)}, u32[]{:S(2)}, u32[]{:S(2)}) collective-permute-start(f32[80,128]{1,0:T(8,128)S(1)} %add_add_fusion.1), channel_id=1, source_target_pairs={{0,5},{1,4},{2,7},{3,6},{4,1},{5,0},{6,3},{7,2},{8,13},{9,12},{10,... | collective-permute-start | bytes 122888 | tf_op jit(solution)/shard_map/ppermute | solution.py:386
